TPU v7x, 32 devices: a whole 2x2x4 slice. The times are simulated.
32 devices in a mesh: src: 4 (over z), tgt: 8 (over y, x, core).
Axes of the slice: x: 2, y: 2, z: 4, core: 2. Of those that a mesh axis runs over, the one named last changes fastest.
Arguments:
- coupling: bfloat16 [2048, 4096], P('src', 'tgt'), may hold values from 0.25 to 4
- src_pcs: bfloat16 [50, 2048], P(None, 'src'), may hold values from -24 to 24
- tgt_pcs: bfloat16 [50, 4096], P(None, 'tgt'), may hold values from -24 to 24
- src_mass: float32 [2048], P('src'), may hold values from 0.25 to 4
- tgt_mass: float32 [4096], P('tgt'), may hold values from 0.25 to 4
Outputs:
- log_coupling: float32 [2048, 4096], P('src', 'tgt')
- row_potential: float32 [2048], P('src')
- col_potential: float32 [4096], P('tgt')
All inputs are finite; a program needn't handle non-finite values.
Results may differ from a plain program's by a relative error of at most 0.0019.
Values sent between devices are 32-bit elements; how exact they have to be, the bound alone decides.
No kernel may reach another device: no remote copies, remote signals or barrier semaphores. Data moves between devices by JAX's collectives and lax.ppermute only.
A program may use at most 64 MiB of HBM per device.

v0:
```python
import functools
import math

import jax
import jax.numpy as jnp
from jax import lax
from jax.experimental import pallas as pl
from jax.experimental.pallas import tpu as pltpu
from jax.sharding import PartitionSpec as P

ITERS = 4

eps_reg = 0.5
marg_power = 1.0 / (1.0 + eps_reg)
tiny_eps = 1e-06

LANES = 128
DEPTH = 64
LN2 = math.log(2.0)
SCORES_BYTES = 1 << 24
LIFT = 54.0
SPAN = 145.0
VMEM = pl.BlockSpec(memory_space=pltpu.VMEM)


def params(mib):
    return pltpu.CompilerParams(vmem_limit_bytes=mib << 20)


def tree(values, combine):
    values = list(values)
    while len(values) > 1:
        paired = [combine(values[i], values[i + 1]) for i in range(0, len(values) - 1, 2)]
        values = paired + ([values[-1]] if len(values) % 2 else [])
    return values[0]


def pieces(value):
    high = value.astype(jnp.bfloat16)
    rest = value - high.astype(jnp.float32)
    middle = rest.astype(jnp.bfloat16)
    low = (rest - middle.astype(jnp.float32)).astype(jnp.bfloat16)
    return high, middle, low


def padded(value):
    return jnp.concatenate(
        [value, jnp.zeros((DEPTH - value.shape[0], value.shape[1]), value.dtype)], axis=0
    )


def front_kernel(*refs):
    sources, (half_ref, whole_ref, moment_ref), local, sems = refs[:5], refs[5:8], refs[8:13], refs[13]
    copies = [pltpu.make_async_copy(a, b, sems.at[i]) for i, (a, b) in enumerate(zip(sources, local))]
    for copy in copies:
        copy.start()
    coupling_ref, src_ref, tgt_ref, src_mass_ref, tgt_mass_ref = local
    pcs = src_ref.shape[0]
    half = half_ref.shape[1]
    odd = lax.rem(lax.axis_index("tgt"), 2)
    for copy in copies[1:]:
        copy.wait()
    src = src_ref[...].astype(jnp.float32)
    tgt = tgt_ref[...].astype(jnp.float32)
    below = jnp.zeros((half_ref.shape[0] - pcs - 1, 2 * half), jnp.float32)
    joined = jnp.concatenate([src, jnp.log2(src_mass_ref[...]), below], axis=0)
    half_ref[...] = jnp.where(odd == 0, joined[:, :half], joined[:, half:])
    below = jnp.zeros((half_ref.shape[0] - pcs - 1, tgt.shape[1]), jnp.float32)
    whole_ref[...] = jnp.concatenate([tgt, jnp.log2(tgt_mass_ref[...]), below], axis=0)
    src = padded(src).astype(jnp.bfloat16)
    tgt = padded(tgt).astype(jnp.bfloat16)
    twice = jnp.concatenate([src, src], axis=0)
    copies[0].wait()
    panel = jnp.dot(twice, coupling_ref[...], preferred_element_type=jnp.float32)
    moment = sum(
        lax.dot_general(tgt, part, (((1,), (1,)), ((), ())), preferred_element_type=jnp.float32)
        for part in pieces(panel)
    )
    lane = lax.broadcasted_iota(jnp.int32, (DEPTH // 2, LANES), 1)
    moment = jnp.where(lane < DEPTH, moment[: DEPTH // 2], moment[DEPTH // 2 :])
    for i in range(4):
        moment_ref[:, i * LANES : (i + 1) * LANES] = moment[i * 8 : i * 8 + 8]


def prepare_kernel(pcs, blocks, merged, near_ref, far_ref, *refs):
    tgt_refs, (src_ref, turned_ref, log_src_ref, log_tgt_ref, line_ref) = refs[:merged], refs[merged:]
    packed_rows = near_ref.shape[0] // blocks
    half = near_ref.shape[1]
    width = tgt_refs[0].shape[1]
    z = lax.axis_index("src")
    t = lax.axis_index("tgt")
    odd = lax.rem(t, 2)
    total_rows = 2 * half * blocks
    total_cols = width * lax.axis_size("tgt")
    for b in range(blocks):
        place = jnp.bitwise_xor(z, b)
        for ref, side in ((near_ref, odd), (far_ref, 1 - odd)):
            block = ref[pl.ds(b * packed_rows, packed_rows), :]
            lanes = pl.ds(pl.multiple_of((place * 2 + side) * half, half), half)
            log_src_ref[:, lanes] = marg_power * (block[pcs : pcs + 1] + math.log2(total_cols))
            block = padded(block).astype(jnp.bfloat16)
            for copy in range(4):
                src_ref[pl.ds(copy * DEPTH, DEPTH), lanes] = block
    mine = lax.rem(lax.div(t, 2), merged)
    for b in range(merged):
        base = pl.multiple_of(jnp.bitwise_xor(mine, b) * width, width)
        block = padded(tgt_refs[b][:packed_rows, :])
        line_ref[:, pl.ds(base, width)] = marg_power * (block[pcs : pcs + 1] + math.log2(total_rows))
        turned = jnp.concatenate([block, block], axis=0).T
        log_tgt_ref[pl.ds(base, width), :] = jnp.broadcast_to(
            marg_power * (turned[:, pcs : pcs + 1] + math.log2(total_rows)), (width, LANES)
        )
        turned_ref[pl.ds(base, width), :] = turned.astype(jnp.bfloat16)


def start_kernel(pcs, entries, src_all, turned_ref, *refs):
    moment_refs, (scores_ref, sums_ref, weights) = refs[:-3], refs[-3:]
    total_rows = src_all.shape[1]
    packed = tree([ref[...] for ref in moment_refs], jnp.add) * entries ** (-0.5)
    spread = jnp.sqrt(jnp.sum(packed * packed) * (1.0 / (pcs * pcs)) + tiny_eps)
    packed = packed / spread * (2.0 / (eps_reg * pcs) / LN2)
    packed = jnp.concatenate([packed[:, i * LANES : (i + 1) * LANES] for i in range(4)], axis=0)
    turned = pltpu.roll(packed, DEPTH, axis=1)
    left = lax.broadcasted_iota(jnp.int32, packed.shape, 1) < DEPTH
    normed = jnp.concatenate(
        [jnp.where(left, packed, turned), jnp.where(left, turned, packed)], axis=0
    )
    high, middle, low = pieces(normed)
    upper = jnp.concatenate([high, middle], axis=0)
    lower = jnp.concatenate([low, jnp.zeros_like(low)], axis=0)

    width = min(512, turned_ref.shape[0])
    first = lax.broadcasted_iota(jnp.int32, (width, LANES), 1) < DEPTH
    for base in range(0, turned_ref.shape[0], width):
        at = pl.ds(base, width)
        weighted = sum(
            jnp.dot(turned_ref[at, :], part, preferred_element_type=jnp.float32)
            for part in (upper, lower)
        )
        high, middle, low = pieces(weighted)
        weights[at, :LANES] = jnp.where(first, high, middle)
        weights[at, LANES:] = jnp.where(first, low, jnp.zeros_like(low))

    chunk, rows = 1024, min(256, scores_ref.shape[0])
    across = total_rows // chunk

    def step(i, carry):
        lanes = pl.ds(pl.multiple_of(lax.rem(i, across) * chunk, chunk), chunk)
        at = pl.ds(pl.multiple_of(lax.div(i, across) * rows, rows), rows)
        scores_ref[at, lanes] = jnp.dot(
            weights[at, :], src_all[:, lanes], preferred_element_type=jnp.float32
        )
        return carry

    lax.fori_loop(0, across * (scores_ref.shape[0] // rows), step, 0)
    rows_running(scores_ref, sums_ref)


def down(highest, summed):
    top = jnp.max(highest, axis=0, keepdims=True)
    return top + jnp.log2(jnp.sum(summed * jnp.exp2(highest - top), axis=0, keepdims=True))


def logsum(one, other):
    top = jnp.maximum(one, other)
    return top + jnp.log2(jnp.exp2(one - top) + jnp.exp2(other - top))


def row_values(log_src_ref, sums_ref, more_ref):
    return log_src_ref[...] - marg_power * logsum(sums_ref[...], more_ref[...])


def lane_tiles(ref):
    return [pl.ds(j, LANES) for j in range(0, ref.shape[1], LANES)]


def halves(low):
    low = pl.multiple_of(low, 16)
    return pl.ds(low, 16), [pl.ds(low, 8), pl.ds(pl.multiple_of(low + 8, 8), 8)]


def running(highest, summed, terms):
    fresh = jnp.maximum(highest, tree(terms, jnp.maximum))
    total = tree([jnp.exp2(term - fresh) for term in terms], jnp.add)
    return fresh, summed * jnp.exp2(highest - fresh) + total


def columns_running(scores_ref, rows_ref, top_ref, sum_ref, base, count):
    tiles = lane_tiles(scores_ref)
    span = min(16, len(tiles))

    def scan(i, carry):
        for u in range(4):
            low = pl.multiple_of((i * 4 + u) * 8, 8)
            at = pl.ds(pl.multiple_of(base + low, 8), 8)
            state = None
            for start in range(0, len(tiles), span):
                terms = [scores_ref[at, lanes] + rows_ref[:, lanes] for lanes in tiles[start : start + span]]
                if state is None:
                    highest = tree(terms, jnp.maximum)
                    state = highest, tree([jnp.exp2(term - highest) for term in terms], jnp.add)
                else:
                    state = running(*state, terms)
            top_ref[pl.ds(low, 8), :], sum_ref[pl.ds(low, 8), :] = state
        return carry

    lax.fori_loop(0, count // 32, scan, 0)


def rows_running(scores_ref, out_ref):
    count, total = scores_ref.shape
    beside, deep = 8, 16
    unset = (jnp.full((8, LANES), -jnp.inf, jnp.float32), jnp.zeros((8, LANES), jnp.float32))
    for start in range(0, total, beside * LANES):
        tiles = [pl.ds(start + j * LANES, LANES) for j in range(beside)]

        def step(i, carry, tiles=tiles):
            ats = [pl.ds(pl.multiple_of((i * deep + g) * 8, 8), 8) for g in range(deep)]
            return tuple(
                running(*state, [scores_ref[at, lanes] for at in ats])
                for state, lanes in zip(carry, tiles)
            )

        carry = lax.fori_loop(0, count // (8 * deep), step, (unset,) * beside)
        for lanes, state in zip(tiles, carry):
            out_ref[:, lanes] = down(*state)


def columns_exp(scores_ref, rows_ref, top_ref, sum_ref, base, count, keep_ref):
    tiles = lane_tiles(scores_ref)

    def highest(i, carry):
        places = [pl.ds(pl.multiple_of(i * 64 + g * 8, 8), 8) for g in range(8)]
        sources = [pl.ds(pl.multiple_of(base + i * 64 + g * 8, 8), 8) for g in range(8)]
        tops = [None] * 8
        for lanes in tiles:
            row = rows_ref[:, lanes]
            for g, source in enumerate(sources):
                term = scores_ref[source, lanes] + row
                tops[g] = term if tops[g] is None else jnp.maximum(tops[g], term)
        for place, top in zip(places, tops):
            top_ref[place, :] = top - LIFT
        return carry

    def total(i, carry):
        pairs = [halves(base + i * 64 + g * 16) for g in range(4)]
        places = [place for g in range(4) for place in halves(i * 64 + g * 16)[1]]
        tops = [top_ref[place, :] for place in places]
        sums = [jnp.zeros((8, LANES), jnp.float32)] * 8
        for lanes in tiles:
            row = rows_ref[:, lanes]
            for g, (at, sources) in enumerate(pairs):
                parts = []
                for h, source in enumerate(sources):
                    parts.append(jnp.exp2(scores_ref[source, lanes] + row - tops[2 * g + h]))
                    sums[2 * g + h] = sums[2 * g + h] + parts[h]
                if keep_ref is not None:
                    keep_ref[at, lanes] = jnp.concatenate(parts, axis=0).astype(keep_ref.dtype)
        for place, value in zip(places, sums):
            sum_ref[place, :] = value
        return carry

    lax.fori_loop(0, count // 64, highest, 0)
    if keep_ref is not None:
        tops = top_ref[pl.ds(0, count), :]
        top_ref[pl.ds(0, count), :] = jnp.broadcast_to(jnp.max(tops, axis=1, keepdims=True), tops.shape)
    lax.fori_loop(0, count // 64, total, 0)


def split_rows(line):
    row = lax.broadcasted_iota(jnp.int32, (16, line.shape[1]), 0)
    high, middle, low = (part.astype(jnp.float32) for part in pieces(line))
    spread = jnp.where(row == 0, high, jnp.where(row == 1, middle, jnp.where(row == 2, low, 0.0)))
    return spread.astype(jnp.bfloat16)


def split_rows(line):
    row = lax.broadcasted_iota(jnp.int32, (16, line.shape[1]), 0)
    high, middle, low = (part.astype(jnp.float32) for part in pieces(line))
    spread = jnp.where(row == 0, high, jnp.where(row == 1, middle, jnp.where(row == 2, low, 0.0)))
    return spread.astype(jnp.bfloat16)


def columns_product(keep_ref, kept_top_ref, factor, shift, log_tgt_line_ref, line_ref, base, count):
    factors = split_rows(factor)
    part = min(count, 512)
    for low in range(0, count, part):
        at = pl.ds(pl.multiple_of(base + low, part), part)
        sums = lax.dot_general(
            factors, keep_ref[at, :], (((1,), (1,)), ((), ())), preferred_element_type=jnp.float32
        )
        logs = kept_top_ref[:, at] + (shift - LIFT) + jnp.log2(jnp.sum(sums, axis=0, keepdims=True))
        line_ref[:, pl.ds(low, part)] = log_tgt_line_ref[:, at] - marg_power * logs


def columns_finish(top_ref, sum_ref, log_tgt_ref, cols_ref, base, count):
    part = min(count, 2048)
    for low in range(0, count, part):
        here = pl.ds(low, part)
        tops = top_ref[here, :]
        top = jnp.max(tops, axis=1, keepdims=True)
        total = jnp.sum(sum_ref[here, :] * jnp.exp2(tops - top), axis=1, keepdims=True)
        at = pl.ds(pl.multiple_of(base + low, part), part)
        cols_ref[here, :] = log_tgt_ref[at, :] - marg_power * (top + jnp.log2(total))


BESIDE, DEEP = 8, 4


def over_tiles(count, width, body, first, done):
    for start in range(0, width, BESIDE * LANES):
        tiles = [pl.ds(start + j * LANES, LANES) for j in range(BESIDE)]

        def step(i, carry, tiles=tiles):
            carry = list(carry)
            body([halves((i * DEEP + g) * 16) for g in range(DEEP)], tiles, carry)
            return tuple(carry)

        state = lax.fori_loop(0, count // (16 * DEEP), step, tuple(first for _ in tiles))
        for lanes, value in zip(tiles, state):
            done(lanes, value)


def rows_highest(scores_ref, cols_ref, top_ref):
    def body(pairs, tiles, carry):
        for _, places in pairs:
            for place in places:
                if cols_ref is not None:
                    potential = cols_ref[place, :]
                for j, lanes in enumerate(tiles):
                    term = scores_ref[place, lanes]
                    if cols_ref is not None:
                        term = term + potential
                    carry[j] = jnp.maximum(carry[j], term)

    def done(lanes, value):
        top_ref[:, lanes] = jnp.broadcast_to(jnp.max(value, axis=0, keepdims=True), value.shape) - LIFT

    over_tiles(*scores_ref.shape, body, jnp.full((8, LANES), -jnp.inf, jnp.float32), done)


def rows_exp(scores_ref, cols_ref, top_ref, out_ref, keep_ref):
    def body(pairs, tiles, carry):
        tops = [top_ref[:, lanes] for lanes in tiles]
        for at, places in pairs:
            if cols_ref is not None:
                potentials = [cols_ref[place, :] for place in places]
            for j, lanes in enumerate(tiles):
                terms = [scores_ref[place, lanes] for place in places]
                if cols_ref is not None:
                    terms = [term + potential for term, potential in zip(terms, potentials)]
                parts = [jnp.exp2(term - tops[j]) for term in terms]
                if keep_ref is not None:
                    keep_ref[at, lanes] = jnp.concatenate(parts, axis=0).astype(keep_ref.dtype)
                carry[j] = carry[j] + (parts[0] + parts[1])

    def done(lanes, value):
        out_ref[:, lanes] = down(top_ref[:, lanes], value)

    over_tiles(*scores_ref.shape, body, jnp.zeros((8, LANES), jnp.float32), done)


def rows_product(keep_ref, kept_top_ref, factor, shift, out_ref):
    factors = split_rows(factor)
    chunk = 512
    for start in range(0, keep_ref.shape[1], chunk):
        lanes = pl.ds(start, chunk)
        sums = jnp.dot(factors, keep_ref[:, lanes], preferred_element_type=jnp.float32)
        out_ref[:, lanes] = (
            kept_top_ref[0:1, lanes] + (shift - LIFT) + jnp.log2(jnp.sum(sums, axis=0, keepdims=True))
        )


def columns_either(rows, shared, kept, line_ref, scratch, base, count):
    scores_ref, log_tgt_ref, log_tgt_line_ref = shared
    keep_ref, kept_top_ref, kept_rows_ref = kept
    rows_ref, cols_ref, top_ref, sum_ref = scratch
    change = rows - kept_rows_ref[...]
    shift = jnp.max(change)
    near = shift - jnp.min(change) <= SPAN

    @pl.when(near)
    def _():
        factor = jnp.exp2(change - (shift - LIFT))
        columns_product(keep_ref, kept_top_ref, factor, shift, log_tgt_line_ref, line_ref, base, count)

    @pl.when(jnp.logical_not(near))
    def _():
        rows_ref[...] = jnp.broadcast_to(rows, rows_ref.shape)
        columns_running(scores_ref, rows_ref, top_ref, sum_ref, base, count)
        columns_finish(top_ref, sum_ref, log_tgt_ref, cols_ref, base, count)
        line_ref[...] = cols_ref[...].T[0:1, :]


def rows_either(scores_ref, line_ref, kept, cols_ref, row_top_ref, out_ref):
    keep_ref, kept_top_ref, kept_line_ref = kept
    change = line_ref[...] - kept_line_ref[...]
    shift = jnp.max(change)
    near = shift - jnp.min(change) <= SPAN

    @pl.when(near)
    def _():
        rows_product(keep_ref, kept_top_ref, jnp.exp2(change - (shift - LIFT)), shift, out_ref)

    @pl.when(jnp.logical_not(near))
    def _():
        cols_ref[...] = jnp.broadcast_to(line_ref[...], (LANES, line_ref.shape[1])).T
        rows_highest(scores_ref, cols_ref, row_top_ref)
        rows_exp(scores_ref, cols_ref, row_top_ref, out_ref, None)


def first_kernel(scores_ref, sums_ref, more_ref, log_src_ref, log_tgt_ref, log_tgt_line_ref, *refs):
    out_ref, keep_ref, row_top_ref, line_ref = refs[:4]
    rows_ref, cols_ref, top_ref, sum_ref = refs[4:]
    rows_ref[...] = jnp.broadcast_to(row_values(log_src_ref, sums_ref, more_ref), rows_ref.shape)
    count = scores_ref.shape[0]
    columns_running(scores_ref, rows_ref, top_ref, sum_ref, 0, count)
    columns_finish(top_ref, sum_ref, log_tgt_ref, cols_ref, 0, count)
    line_ref[...] = cols_ref[...].T[0:1, :]
    rows_highest(scores_ref, cols_ref, row_top_ref)
    rows_exp(scores_ref, cols_ref, row_top_ref, out_ref, keep_ref)


def second_kernel(scores_ref, sums_ref, more_ref, log_src_ref, log_tgt_ref, log_tgt_line_ref, *refs):
    kept, (out_ref, keep_ref, kept_top_ref, base_ref) = refs[:3], refs[3:7]
    rows_ref, cols_ref, top_ref, sum_ref, line_ref, row_top_ref = refs[7:]
    base_ref[...] = row_values(log_src_ref, sums_ref, more_ref)
    rows_ref[...] = jnp.broadcast_to(base_ref[...], rows_ref.shape)
    count = scores_ref.shape[0]
    columns_exp(scores_ref, rows_ref, top_ref, sum_ref, 0, count, keep_ref)
    columns_finish(top_ref, sum_ref, log_tgt_ref, cols_ref, 0, count)
    kept_top_ref[...] = top_ref[...].T[0:1, :]
    line_ref[...] = cols_ref[...].T[0:1, :]
    rows_either(scores_ref, line_ref, kept, cols_ref, row_top_ref, out_ref)


def later_kernel(scores_ref, sums_ref, more_ref, log_src_ref, log_tgt_ref, log_tgt_line_ref, *refs):
    kept, kept_columns, out_ref = refs[:3], refs[3:6], refs[6]
    scratch, line_ref, row_top_ref = refs[7:11], refs[11], refs[12]
    rows = row_values(log_src_ref, sums_ref, more_ref)
    shared = scores_ref, log_tgt_ref, log_tgt_line_ref
    columns_either(rows, shared, kept_columns, line_ref, scratch, 0, scores_ref.shape[0])
    rows_either(scores_ref, line_ref, kept, scratch[1], row_top_ref, out_ref)


def last_kernel(merged, scores_ref, sums_ref, more_ref, log_src_ref, log_tgt_ref, log_tgt_line_ref, *refs):
    kept_columns, (out_ref, row_ref, col_ref) = refs[:3], refs[3:6]
    scratch, line_ref, values_ref = refs[6:10], refs[10], refs[11]
    own_rows, own_cols = out_ref.shape
    rows = row_values(log_src_ref, sums_ref, more_ref)
    values_ref[...] = rows
    base = pl.multiple_of(lax.rem(lax.div(lax.axis_index("tgt"), 2), merged) * own_cols, own_cols)
    lanes = pl.ds(pl.multiple_of(lax.axis_index("src") * own_rows, own_rows), own_rows)
    shared = scores_ref, log_tgt_ref, log_tgt_line_ref
    columns_either(rows, shared, kept_columns, line_ref, scratch, base, own_cols)
    row_ref[...] = values_ref[:, lanes] * LN2
    col_ref[...] = line_ref[...] * LN2
    block = scores_ref[pl.ds(base, own_cols), lanes] + values_ref[:, lanes]
    out_ref[...] = (block.T + line_ref[...]) * LN2


def swap(value, axis, offset):
    return lax.ppermute(value, axis, [(i, i ^ offset) for i in range(lax.axis_size(axis))])


def staged_parts(value, axis, low, width):
    size = lax.axis_size(axis)
    terms = [value]
    while low < size:
        span = min(width, size // low)
        value = tree(terms, jnp.add)
        terms = [value] + [swap(value, axis, low * j) for j in range(1, span)]
        low *= span
    return terms


def shards(coupling, src_pcs, tgt_pcs, src_mass, tgt_mass):
    f32 = jnp.float32
    pcs = src_pcs.shape[0]
    rows, cols = coupling.shape
    src_size, tgt_size = lax.axis_size("src"), lax.axis_size("tgt")
    total_rows, total_cols = rows * src_size, cols * tgt_size
    merged = 1
    while 2 * merged * 2 <= tgt_size and 2 * merged * cols * total_rows * 4 <= SCORES_BYTES:
        merged *= 2
    wide = merged * cols
    packed_rows = -(-(pcs + 1) // 8) * 8

    arguments = (coupling, src_pcs, tgt_pcs, src_mass.reshape(1, -1), tgt_mass.reshape(1, -1))
    half, whole, moment = pl.pallas_call(
        front_kernel,
        out_shape=(
            pltpu.VMEM((packed_rows, rows // 2), f32),
            pltpu.VMEM((packed_rows, cols), f32),
            pltpu.VMEM((8, 4 * LANES), f32),
        ),
        in_specs=[pl.BlockSpec(memory_space=pltpu.HBM)] * 5,
        out_specs=(VMEM,) * 3,
        scratch_shapes=[pltpu.VMEM(a.shape, a.dtype) for a in arguments]
        + [pltpu.SemaphoreType.DMA((5,))],
        compiler_params=params(8),
    )(*[pltpu.with_memory_space_constraint(a, pltpu.HBM) for a in arguments])

    moment = moment + swap(moment, "tgt", 1)
    half, whole, moment = lax.optimization_barrier((half, whole, moment))
    parts, targets = [moment], [whole]
    if merged > 1:
        message = jnp.concatenate([whole, moment], axis=0)
        targets += [swap(message, "tgt", 2 * b) for b in range(1, merged)]
        parts += [target[packed_rows:] for target in targets[1:]]
    sources = [half] + [swap(half, "src", b) for b in range(1, src_size)]
    parts, sources, targets = lax.optimization_barrier((parts, sources, targets))
    if 2 * merged < tgt_size:
        parts = staged_parts(tree(parts, jnp.add), "tgt", 2 * merged, 4)
    moments = staged_parts(tree(parts, jnp.add), "src", 1, 4)
    near = jnp.concatenate(sources, axis=0)
    far = swap(near, "tgt", 1)

    src_all, turned, log_src, log_tgt, log_tgt_line = pl.pallas_call(
        functools.partial(prepare_kernel, pcs, src_size, merged),
        out_shape=(
            jax.ShapeDtypeStruct((4 * DEPTH, total_rows), jnp.bfloat16),
            jax.ShapeDtypeStruct((wide, LANES), jnp.bfloat16),
            jax.ShapeDtypeStruct((1, total_rows), f32),
            jax.ShapeDtypeStruct((wide, LANES), f32),
            jax.ShapeDtypeStruct((1, wide), f32),
        ),
        in_specs=[VMEM] * (2 + merged),
        out_specs=(VMEM,) * 5,
        compiler_params=params(10),
    )(near, far, *targets)
    scores, sums = pl.pallas_call(
        functools.partial(start_kernel, pcs, total_rows * total_cols),
        out_shape=(
            jax.ShapeDtypeStruct((wide, total_rows), f32),
            jax.ShapeDtypeStruct((1, total_rows), f32),
        ),
        in_specs=[VMEM] * (2 + len(moments)),
        out_specs=(VMEM,) * 2,
        scratch_shapes=[
            pltpu.VMEM((wide, 4 * DEPTH), jnp.bfloat16),
        ],
        compiler_params=params(14),
    )(src_all, turned, *moments)

    def both(value):
        offset = 2 * merged
        while offset < tgt_size:
            value = logsum(value, swap(value, "tgt", offset))
            offset *= 2
        return value, swap(value, "tgt", 1)

    bf16, block = jnp.bfloat16, (wide, total_rows)

    def call(kernel, sums, extra, outs, scratch):
        return pl.pallas_call(
            kernel,
            out_shape=tuple(jax.ShapeDtypeStruct(shape, bf16 if shape == block else f32) for shape in outs),
            in_specs=[VMEM] * (6 + len(extra)),
            out_specs=(VMEM,) * len(outs),
            scratch_shapes=[pltpu.VMEM(shape, f32) for shape in scratch],
            compiler_params=params(10),
        )(scores, *both(sums), log_src, log_tgt, log_tgt_line, *extra)

    line, lines, pads = (1, total_rows), (8, total_rows), (wide, LANES)
    side, columns = (1, wide), (lines, pads, pads, pads)
    sums, *kept_rows = call(first_kernel, sums, (), (line, block, lines, side), columns)
    sums, *kept_columns = call(
        second_kernel, sums, kept_rows, (line, block, side, line), (*columns, side, lines)
    )
    for iteration in range(ITERS - 3):
        (sums,) = call(
            later_kernel, sums, (*kept_rows, *kept_columns), (line,), (*columns, side, lines)
        )
    pads, side = (cols, LANES), (1, cols)
    log_coupling, row_potential, col_potential = call(
        functools.partial(last_kernel, merged), sums, kept_columns,
        ((rows, cols), (1, rows), side), (lines, pads, pads, pads, side, line),
    )
    return log_coupling, row_potential.reshape(-1), col_potential.reshape(-1)


def solution(mesh):
    in_specs = (P("src", "tgt"), P(None, "src"), P(None, "tgt"), P("src"), P("tgt"))
    out_specs = (P("src", "tgt"), P("src"), P("tgt"))
    return jax.shard_map(shards, mesh=mesh, in_specs=in_specs, out_specs=out_specs, check_vma=False)
```

profile of v0, /device:TPU:0, one launch (start us, length us, event | category | flops | bytes accessed | tf_op | source)
XLA Modules:
  0.0 71.5 jit_solution(5463954524769606651)
XLA Ops:
  0.6 1.6 %shard_map.76 = (f32[56,256]{1,0:T(8,128)S(1)}, f32[56,512]{1,0:T(8,128)S(1)}, f32[8,512]{1,0:T(8,128)S(1)}) custom-call(bf16[512,512]{1,0:T(8,128)(2,1)} %refs_0_.1, bf16[50,512]{1,0:T(8,128)(2,1)} %refs_1_.1, bf16[50,512]{1,0:T(8,128)(2,1)} %refs_2_.1, f32[1,512]{1,0:T(1,128)} %bitcast.4, f32[1,512]{1,0:T(1,128)} %bitcast.5), custom_call_target="tpu_custom_call" | custom-call | tf_op jit(solution)/shard_map/pallas_call | solution.py:490
  2.3 0.5 collective-permute-start
  2.8 0.8 %collective-permute-done = f32[8,512]{1,0:T(8,128)S(1)} collective-permute-done((f32[8,512]{1,0:T(8,128)S(1)}, f32[8,512]{1,0:T(8,128)S(1)}, u32[]{:S(2)}, u32[]{:S(2)}) %collective-permute-start) | collective-permute-done | bytes 16416 | tf_op jit(solution)/shard_map/ppermute | solution.py:463
  3.7 3.9 %collective-permute-start.3 = (f32[64,512]{1,0:T(8,128)S(1)}, f32[64,512]{1,0:T(8,128)S(1)}, u32[]{:S(2)}, u32[]{:S(2)}) collective-permute-start(f32[64,512]{1,0:T(8,128)S(1)} %constant_dynamic-update-slice_fusion), channel_id=1, source_target_pairs={{0,6},{1,7},{2,4},{3,5},{4,2},{5,3},{6,0},{7,1},{8,14},{9,15},{10,... | collective-permute-start | bytes 393224 | tf_op jit(solution)/shard_map/ppermute | solution.py:463
  7.5 0.5 collective-permute-start.2
  8.0 0.1 collective-permute-start.1
  8.2 4.0 %collective-permute-start.6 = (f32[56,256]{1,0:T(8,128)S(1)}, f32[56,256]{1,0:T(8,128)S(1)}, u32[]{:S(2)}, u32[]{:S(2)}) collective-permute-start(f32[56,256]{1,0:T(8,128)S(1)} %get-tuple-element.45), channel_id=1, source_target_pairs={{0,24},{8,16},{16,8},{24,0},{1,25},{9,17},{17,9},{25,1},{2,26},{10... | collective-permute-start | bytes 172040 | tf_op jit(solution)/shard_map/ppermute | solution.py:463
  12.2 1.2 %collective-permute-start.4 = (f32[56,256]{1,0:T(8,128)S(1)}, f32[56,256]{1,0:T(8,128)S(1)}, u32[]{:S(2)}, u32[]{:S(2)}) collective-permute-start(f32[56,256]{1,0:T(8,128)S(1)} %get-tuple-element.45), channel_id=1, source_target_pairs={{0,8},{8,0},{16,24},{24,16},{1,9},{9,1},{17,25},{25,17},{2,10},{10... | collective-permute-start | bytes 172040 | tf_op jit(solution)/shard_map/ppermute | solution.py:463
  13.4 0.7 %collective-permute-done.2.refs_2_ = f32[64,512]{1,0:T(8,128)S(1)} collective-permute-done((f32[64,512]{1,0:T(8,128)S(1)}, f32[64,512]{1,0:T(8,128)S(1)}, u32[]{:S(2)}, u32[]{:S(2)}) %collective-permute-start.2) | collective-permute-done | bytes 131104 | tf_op jit(solution)/shard_map/ppermute | solution.py:463
  14.2 0.3 collective-permute-done.1.refs_1_
  14.4 0.6 collective-permute-done.6
  15.0 2.2 %collective-permute-done.5 = f32[56,256]{1,0:T(8,128)S(1)} collective-permute-done((f32[56,256]{1,0:T(8,128)S(1)}, f32[56,256]{1,0:T(8,128)S(1)}, u32[]{:S(2)}, u32[]{:S(2)}) %collective-permute-start.5) | collective-permute-done | bytes 57376 | tf_op jit(solution)/shard_map/ppermute | solution.py:463
  17.2 0.0 collective-permute-done.4
  17.3 0.1 collective-permute-start.7
  17.4 2.7 %collective-permute-start.10 = (f32[8,512]{1,0:T(8,128)S(1)}, f32[8,512]{1,0:T(8,128)S(1)}, u32[]{:S(2)}, u32[]{:S(2)}) collective-permute-start(f32[8,512]{1,0:T(8,128)S(1)} %add_add_fusion.refs_0_), channel_id=1, source_target_pairs={{0,24},{8,16},{16,8},{24,0},{1,25},{9,17},{17,9},{25,1},{2,26},{10... | collective-permute-start | bytes 49160 | tf_op jit(solution)/shard_map/ppermute | solution.py:463
  20.1 1.7 %collective-permute-start.8 = (f32[8,512]{1,0:T(8,128)S(1)}, f32[8,512]{1,0:T(8,128)S(1)}, u32[]{:S(2)}, u32[]{:S(2)}) collective-permute-start(f32[8,512]{1,0:T(8,128)S(1)} %add_add_fusion.refs_0_), channel_id=1, source_target_pairs={{0,8},{8,0},{16,24},{24,16},{1,9},{9,1},{17,25},{25,17},{2,10},{10... | collective-permute-start | bytes 49160 | tf_op jit(solution)/shard_map/ppermute | solution.py:463
  21.9 0.7 %shard_map.77 = (bf16[256,2048]{1,0:T(8,128)(2,1)S(1)}, bf16[2048,128]{1,0:T(8,128)(2,1)S(1)}, f32[1,2048]{1,0:T(1,128)S(1)}, f32[2048,128]{1,0:T(8,128)S(1)}, f32[1,2048]{1,0:T(1,128)S(1)}) custom-call(f32[224,256]{1,0:T(8,128)S(1)} %constant_dynamic-update-slice_fusion.2.near_ref, f32[224,256]{1,0:T(8,128)S(1)} %collective-permute-done.7.far_ref, ...), custom_call_target="tpu_custom_call" | custom-call | tf_op jit(solution)/shard_map/pallas_call | solution.py:519
  22.6 0.4 collective-permute-done.10.refs_3_
  23.0 1.7 %collective-permute-done.9.refs_2_ = f32[8,512]{1,0:T(8,128)S(1)} collective-permute-done((f32[8,512]{1,0:T(8,128)S(1)}, f32[8,512]{1,0:T(8,128)S(1)}, u32[]{:S(2)}, u32[]{:S(2)}) %collective-permute-start.9) | collective-permute-done | bytes 16416 | tf_op jit(solution)/shard_map/ppermute | solution.py:463
  24.8 9.1 %shard_map.78 = (f32[2048,2048]{1,0:T(8,128)S(1)}, f32[1,2048]{1,0:T(1,128)S(1)}) custom-call(bf16[256,2048]{1,0:T(8,128)(2,1)S(1)} %get-tuple-element.53.src_all, bf16[2048,128]{1,0:T(8,128)(2,1)S(1)} %get-tuple-element.54.turned_ref, f32[8,512]{1,0:T(8,128)S(1)} %add_add_fusion.refs_0_, f32[8,512]{1,0:T(8,128)S(1)} %collective-permute-done.8.refs_1_, ...), custom_call_target="tpu_custom_call" | custom-call | tf_op jit(solution)/shard_map/pallas_call | solution.py:532
  33.8 0.1 collective-permute-start.11
  33.9 1.2 %collective-permute-done.11.more_ref = f32[1,2048]{1,0:T(1,128)S(1)} collective-permute-done((f32[1,2048]{1,0:T(1,128)S(1)}, f32[1,2048]{1,0:T(1,128)S(1)}, u32[]{:S(2)}, u32[]{:S(2)}) %collective-permute-start.11) | collective-permute-done | bytes 8224 | tf_op jit(solution)/shard_map/ppermute | solution.py:463
  35.1 10.5 %shard_map.79 = (f32[1,2048]{1,0:T(1,128)S(1)}, bf16[2048,2048]{1,0:T(8,128)(2,1)S(1)}, f32[8,2048]{1,0:T(8,128)S(1)}, f32[1,2048]{1,0:T(1,128)S(1)}) custom-call(f32[2048,2048]{1,0:T(8,128)S(1)} %get-tuple-element.59.scores_ref, f32[1,2048]{1,0:T(1,128)S(1)} %get-tuple-element.60.sums_ref, f32[1,2048]{1,0:T(1,128)S(1)} %collective-permute-done.11.more_ref, ...), custom_call_target="tpu_custom_call" | custom-call | tf_op jit(solution)/shard_map/pallas_call | solution.py:556
  45.6 0.2 collective-permute-start.12
  45.8 1.0 %collective-permute-done.12.more_ref = f32[1,2048]{1,0:T(1,128)S(1)} collective-permute-done((f32[1,2048]{1,0:T(1,128)S(1)}, f32[1,2048]{1,0:T(1,128)S(1)}, u32[]{:S(2)}, u32[]{:S(2)}) %collective-permute-start.12) | collective-permute-done | bytes 8224 | tf_op jit(solution)/shard_map/ppermute | solution.py:463
  46.8 11.8 %shard_map.80 = (f32[1,2048]{1,0:T(1,128)S(1)}, bf16[2048,2048]{1,0:T(8,128)(2,1)S(1)}, f32[1,2048]{1,0:T(1,128)S(1)}, f32[1,2048]{1,0:T(1,128)S(1)}) custom-call(f32[2048,2048]{1,0:T(8,128)S(1)} %get-tuple-element.59.scores_ref, f32[1,2048]{1,0:T(1,128)S(1)} %get-tuple-element.64.sums_ref, f32[1,2048]{1,0:T(1,128)S(1)} %collective-permute-done.12.more_ref, ...), custom_call_target="tpu_custom_call" | custom-call | tf_op jit(solution)/shard_map/pallas_call | solution.py:556
  58.6 0.2 collective-permute-start.13
  58.9 1.0 %collective-permute-done.13.more_ref = f32[1,2048]{1,0:T(1,128)S(1)} collective-permute-done((f32[1,2048]{1,0:T(1,128)S(1)}, f32[1,2048]{1,0:T(1,128)S(1)}, u32[]{:S(2)}, u32[]{:S(2)}) %collective-permute-start.13) | collective-permute-done | bytes 8224 | tf_op jit(solution)/shard_map/ppermute | solution.py:463
  59.9 7.5 %shard_map.81.sums_ref = f32[1,2048]{1,0:T(1,128)S(1)} custom-call(f32[2048,2048]{1,0:T(8,128)S(1)} %get-tuple-element.59.scores_ref, f32[1,2048]{1,0:T(1,128)S(1)} %get-tuple-element.68.sums_ref, f32[1,2048]{1,0:T(1,128)S(1)} %collective-permute-done.13.more_ref, f32[1,2048]{1,0:T(1,128)S(1)} %get-tuple-element.61.log_src_ref, ...), custom_call_target="tpu_custom_call" | custom-call | tf_op jit(solution)/shard_map/pallas_call | solution.py:556
  67.4 0.2 collective-permute-start.14
  67.6 1.0 %collective-permute-done.14.more_ref = f32[1,2048]{1,0:T(1,128)S(1)} collective-permute-done((f32[1,2048]{1,0:T(1,128)S(1)}, f32[1,2048]{1,0:T(1,128)S(1)}, u32[]{:S(2)}, u32[]{:S(2)}) %collective-permute-start.14) | collective-permute-done | bytes 8224 | tf_op jit(solution)/shard_map/ppermute | solution.py:463
  68.6 2.8 %shard_map.82 = (f32[512,512]{1,0:T(8,128)}, f32[1,512]{1,0:T(1,128)}, f32[1,512]{1,0:T(1,128)}) custom-call(f32[2048,2048]{1,0:T(8,128)S(1)} %get-tuple-element.59.scores_ref, f32[1,2048]{1,0:T(1,128)S(1)} %shard_map.81.sums_ref, f32[1,2048]{1,0:T(1,128)S(1)} %collective-permute-done.14.more_ref, f32[1,2048]{1,0:T(1,128)S(1)} %get-tuple-element.61.log_src_ref, ...), custom_call_target="tpu_custom_call" | custom-call | tf_op jit(solution)/shard_map/pallas_call | solution.py:556
  (16 shorter events, 0.1 us)
Async XLA Ops:
  2.3 1.4 %collective-permute-start = (f32[8,512]{1,0:T(8,128)S(1)}, f32[8,512]{1,0:T(8,128)S(1)}, u32[]{:S(2)}, u32[]{:S(2)}) collective-permute-start(f32[8,512]{1,0:T(8,128)S(1)} %get-tuple-element.41), channel_id=1, source_target_pairs={{0,1},{1,0},{2,3},{3,2},{4,5},{5,4},{6,7},{7,6},{8,9},{9,8},{10,11... | collective-permute-start | bytes 49160 | tf_op jit(solution)/shard_map/ppermute | solution.py:463
  3.7 8.5 %collective-permute-start.3 = (f32[64,512]{1,0:T(8,128)S(1)}, f32[64,512]{1,0:T(8,128)S(1)}, u32[]{:S(2)}, u32[]{:S(2)}) collective-permute-start(f32[64,512]{1,0:T(8,128)S(1)} %constant_dynamic-update-slice_fusion), channel_id=1, source_target_pairs={{0,6},{1,7},{2,4},{3,5},{4,2},{5,3},{6,0},{7,1},{8,14},{9,15},{10,... | collective-permute-start | bytes 393224 | tf_op jit(solution)/shard_map/ppermute | solution.py:463
  7.5 6.6 %collective-permute-start.2 = (f32[64,512]{1,0:T(8,128)S(1)}, f32[64,512]{1,0:T(8,128)S(1)}, u32[]{:S(2)}, u32[]{:S(2)}) collective-permute-start(f32[64,512]{1,0:T(8,128)S(1)} %constant_dynamic-update-slice_fusion), channel_id=1, source_target_pairs={{0,4},{1,5},{2,6},{3,7},{4,0},{5,1},{6,2},{7,3},{8,12},{9,13},{10,... | collective-permute-start | bytes 393224 | tf_op jit(solution)/shard_map/ppermute | solution.py:463
  8.0 6.4 %collective-permute-start.1 = (f32[64,512]{1,0:T(8,128)S(1)}, f32[64,512]{1,0:T(8,128)S(1)}, u32[]{:S(2)}, u32[]{:S(2)}) collective-permute-start(f32[64,512]{1,0:T(8,128)S(1)} %constant_dynamic-update-slice_fusion), channel_id=1, source_target_pairs={{0,2},{1,3},{2,0},{3,1},{4,6},{5,7},{6,4},{7,5},{8,10},{9,11},{10,... | collective-permute-start | bytes 393224 | tf_op jit(solution)/shard_map/ppermute | solution.py:463
  8.2 6.8 %collective-permute-start.6 = (f32[56,256]{1,0:T(8,128)S(1)}, f32[56,256]{1,0:T(8,128)S(1)}, u32[]{:S(2)}, u32[]{:S(2)}) collective-permute-start(f32[56,256]{1,0:T(8,128)S(1)} %get-tuple-element.45), channel_id=1, source_target_pairs={{0,24},{8,16},{16,8},{24,0},{1,25},{9,17},{17,9},{25,1},{2,26},{10... | collective-permute-start | bytes 172040 | tf_op jit(solution)/shard_map/ppermute | solution.py:463
  12.2 5.1 %collective-permute-start.5 = (f32[56,256]{1,0:T(8,128)S(1)}, f32[56,256]{1,0:T(8,128)S(1)}, u32[]{:S(2)}, u32[]{:S(2)}) collective-permute-start(f32[56,256]{1,0:T(8,128)S(1)} %get-tuple-element.45), channel_id=1, source_target_pairs={{0,16},{8,24},{16,0},{24,8},{1,17},{9,25},{17,1},{25,9},{2,18},{10... | collective-permute-start | bytes 172040 | tf_op jit(solution)/shard_map/ppermute | solution.py:463
  12.2 5.1 %collective-permute-start.4 = (f32[56,256]{1,0:T(8,128)S(1)}, f32[56,256]{1,0:T(8,128)S(1)}, u32[]{:S(2)}, u32[]{:S(2)}) collective-permute-start(f32[56,256]{1,0:T(8,128)S(1)} %get-tuple-element.45), channel_id=1, source_target_pairs={{0,8},{8,0},{16,24},{24,16},{1,9},{9,1},{17,25},{25,17},{2,10},{10... | collective-permute-start | bytes 172040 | tf_op jit(solution)/shard_map/ppermute | solution.py:463
  17.3 4.6 %collective-permute-start.7 = (f32[224,256]{1,0:T(8,128)S(1)}, f32[224,256]{1,0:T(8,128)S(1)}, u32[]{:S(2)}, u32[]{:S(2)}) collective-permute-start(f32[224,256]{1,0:T(8,128)S(1)} %constant_dynamic-update-slice_fusion.2.near_ref), channel_id=1, source_target_pairs={{0,1},{1,0},{2,3},{3,2},{4,5},{5,4},{6,7},{7,6},{8,9},{9,8},{10,11... | collective-permute-start | bytes 688136 | tf_op jit(solution)/shard_map/ppermute | solution.py:463
  17.4 5.6 %collective-permute-start.10 = (f32[8,512]{1,0:T(8,128)S(1)}, f32[8,512]{1,0:T(8,128)S(1)}, u32[]{:S(2)}, u32[]{:S(2)}) collective-permute-start(f32[8,512]{1,0:T(8,128)S(1)} %add_add_fusion.refs_0_), channel_id=1, source_target_pairs={{0,24},{8,16},{16,8},{24,0},{1,25},{9,17},{17,9},{25,1},{2,26},{10... | collective-permute-start | bytes 49160 | tf_op jit(solution)/shard_map/ppermute | solution.py:463
  20.1 4.6 %collective-permute-start.9 = (f32[8,512]{1,0:T(8,128)S(1)}, f32[8,512]{1,0:T(8,128)S(1)}, u32[]{:S(2)}, u32[]{:S(2)}) collective-permute-start(f32[8,512]{1,0:T(8,128)S(1)} %add_add_fusion.refs_0_), channel_id=1, source_target_pairs={{0,16},{8,24},{16,0},{24,8},{1,17},{9,25},{17,1},{25,9},{2,18},{10... | collective-permute-start | bytes 49160 | tf_op jit(solution)/shard_map/ppermute | solution.py:463
  20.1 4.6 %collective-permute-start.8 = (f32[8,512]{1,0:T(8,128)S(1)}, f32[8,512]{1,0:T(8,128)S(1)}, u32[]{:S(2)}, u32[]{:S(2)}) collective-permute-start(f32[8,512]{1,0:T(8,128)S(1)} %add_add_fusion.refs_0_), channel_id=1, source_target_pairs={{0,8},{8,0},{16,24},{24,16},{1,9},{9,1},{17,25},{25,17},{2,10},{10... | collective-permute-start | bytes 49160 | tf_op jit(solution)/shard_map/ppermute | solution.py:463
  33.8 1.2 %collective-permute-start.11 = (f32[1,2048]{1,0:T(1,128)S(1)}, f32[1,2048]{1,0:T(1,128)S(1)}, u32[]{:S(2)}, u32[]{:S(2)}) collective-permute-start(f32[1,2048]{1,0:T(1,128)S(1)} %get-tuple-element.60.sums_ref), channel_id=1, source_target_pairs={{0,1},{1,0},{2,3},{3,2},{4,5},{5,4},{6,7},{7,6},{8,9},{9,8},{10,11... | collective-permute-start | bytes 24584 | tf_op jit(solution)/shard_map/ppermute | solution.py:463
  45.6 1.2 %collective-permute-start.12 = (f32[1,2048]{1,0:T(1,128)S(1)}, f32[1,2048]{1,0:T(1,128)S(1)}, u32[]{:S(2)}, u32[]{:S(2)}) collective-permute-start(f32[1,2048]{1,0:T(1,128)S(1)} %get-tuple-element.64.sums_ref), channel_id=1, source_target_pairs={{0,1},{1,0},{2,3},{3,2},{4,5},{5,4},{6,7},{7,6},{8,9},{9,8},{10,11... | collective-permute-start | bytes 24584 | tf_op jit(solution)/shard_map/ppermute | solution.py:463
  58.6 1.2 %collective-permute-start.13 = (f32[1,2048]{1,0:T(1,128)S(1)}, f32[1,2048]{1,0:T(1,128)S(1)}, u32[]{:S(2)}, u32[]{:S(2)}) collective-permute-start(f32[1,2048]{1,0:T(1,128)S(1)} %get-tuple-element.68.sums_ref), channel_id=1, source_target_pairs={{0,1},{1,0},{2,3},{3,2},{4,5},{5,4},{6,7},{7,6},{8,9},{9,8},{10,11... | collective-permute-start | bytes 24584 | tf_op jit(solution)/shard_map/ppermute | solution.py:463
  67.4 1.2 %collective-permute-start.14 = (f32[1,2048]{1,0:T(1,128)S(1)}, f32[1,2048]{1,0:T(1,128)S(1)}, u32[]{:S(2)}, u32[]{:S(2)}) collective-permute-start(f32[1,2048]{1,0:T(1,128)S(1)} %shard_map.81.sums_ref), channel_id=1, source_target_pairs={{0,1},{1,0},{2,3},{3,2},{4,5},{5,4},{6,7},{7,6},{8,9},{9,8},{10,11... | collective-permute-start | bytes 24584 | tf_op jit(solution)/shard_map/ppermute | solution.py:463
where the time goes:
time: 71.6 us; the launch traced here: 71.5 us
  Pallas kernels  44.1 us (62%)
  starting transfers between devices  15.5 us (22%)
  waiting for transfers between devices  11 us (15%)
  between operations  0.75 us (1%)
    pallas_call x4, Pallas kernels, call(): pl.pallas_call(kernel, out_shape=tuple((jax.ShapeDtypeStruct(shape, bf16...  32.6 us
    ppermute x15, starting transfers between devices, swap(): lax.ppermute(value, axis, [(i, i ^ offset) for i in range(lax.axis_size(a...  15.5 us
    ppermute x15, waiting for transfers between devices, swap(): lax.ppermute(value, axis, [(i, i ^ offset) for i in range(lax.axis_size(a...  11 us
    pallas_call x1, Pallas kernels, shards(): pl.pallas_call(functools.partial(start_kernel, pcs, total_rows * total_co...  9.06 us
    pallas_call x1, Pallas kernels, shards(): pl.pallas_call(front_kernel, out_shape=(pltpu.VMEM((packed_rows, rows //...  1.65 us
  transfers between devices with their start and end apart: 15, of which 11 were waited for; matrix products, arithmetic and copies ran while one was open for 0% of the time, Pallas kernels for 1%

commit v1 on v0

--- a/solution.py
+++ b/solution.py
@@ -113,9 +113,8 @@
         turned_ref[pl.ds(base, width), :] = turned.astype(jnp.bfloat16)
 
 
-def start_kernel(pcs, entries, src_all, turned_ref, *refs):
-    moment_refs, (scores_ref, sums_ref, weights) = refs[:-3], refs[-3:]
-    total_rows = src_all.shape[1]
+def start_kernel(pcs, entries, turned_ref, *refs):
+    moment_refs, weights = refs[:-1], refs[-1]
     packed = tree([ref[...] for ref in moment_refs], jnp.add) * entries ** (-0.5)
     spread = jnp.sqrt(jnp.sum(packed * packed) * (1.0 / (pcs * pcs)) + tiny_eps)
     packed = packed / spread * (2.0 / (eps_reg * pcs) / LN2)
@@ -140,20 +139,6 @@
         high, middle, low = pieces(weighted)
         weights[at, :LANES] = jnp.where(first, high, middle)
         weights[at, LANES:] = jnp.where(first, low, jnp.zeros_like(low))
-
-    chunk, rows = 1024, min(256, scores_ref.shape[0])
-    across = total_rows // chunk
-
-    def step(i, carry):
-        lanes = pl.ds(pl.multiple_of(lax.rem(i, across) * chunk, chunk), chunk)
-        at = pl.ds(pl.multiple_of(lax.div(i, across) * rows, rows), rows)
-        scores_ref[at, lanes] = jnp.dot(
-            weights[at, :], src_all[:, lanes], preferred_element_type=jnp.float32
-        )
-        return carry
-
-    lax.fori_loop(0, across * (scores_ref.shape[0] // rows), step, 0)
-    rows_running(scores_ref, sums_ref)
 
 
 def down(highest, summed):
@@ -529,19 +514,21 @@
         out_specs=(VMEM,) * 5,
         compiler_params=params(10),
     )(near, far, *targets)
-    scores, sums = pl.pallas_call(
+    weights = pl.pallas_call(
         functools.partial(start_kernel, pcs, total_rows * total_cols),
-        out_shape=(
-            jax.ShapeDtypeStruct((wide, total_rows), f32),
-            jax.ShapeDtypeStruct((1, total_rows), f32),
-        ),
-        in_specs=[VMEM] * (2 + len(moments)),
-        out_specs=(VMEM,) * 2,
-        scratch_shapes=[
-            pltpu.VMEM((wide, 4 * DEPTH), jnp.bfloat16),
-        ],
-        compiler_params=params(14),
-    )(src_all, turned, *moments)
+        out_shape=jax.ShapeDtypeStruct((wide, 4 * DEPTH), jnp.bfloat16),
+        in_specs=[VMEM] * (1 + len(moments)),
+        out_specs=VMEM,
+        compiler_params=params(10),
+    )(turned, *moments)
+    scores = jnp.dot(weights, src_all, preferred_element_type=f32)
+    sums = pl.pallas_call(
+        rows_running,
+        out_shape=jax.ShapeDtypeStruct((1, total_rows), f32),
+        in_specs=[VMEM],
+        out_specs=VMEM,
+        compiler_params=params(10),
+    )(scores)
 
     def both(value):
         offset = 2 * merged

time: 71.6 us -> 69.3 us (0.968)
  Pallas kernels: 44.1 us -> 39.4 us
  matrix products: 0 us -> 2.34 us
    pallas_call x1, Pallas kernels: 9.06 us -> 0.76 us  [shards(): pl.pallas_call(functools.partial(start_kernel, pcs, total_rows * total_co...]
    pallas_call x0 -> x1, Pallas kernels: none -> 3.46 us  [shards(): pl.pallas_call(rows_running, out_shape=jax.ShapeDtypeStruct((1, total_row...]
    dot_general x0 -> x1, matrix products: none -> 2.34 us  [shards(): scores = jnp.dot(weights, src_all, preferred_element_type=f32)]
where the time goes in v1:
time: 69.3 us; the launch traced here: 69.2 us
  Pallas kernels  39.4 us (57%)
  starting transfers between devices  15.5 us (22%)
  waiting for transfers between devices  11 us (16%)
  matrix products  2.34 us (3%)
  between operations  0.77 us (1%)
    pallas_call x4, Pallas kernels, call(): pl.pallas_call(kernel, out_shape=tuple((jax.ShapeDtypeStruct(shape, bf16...  32.8 us
    ppermute x15, starting transfers between devices, swap(): lax.ppermute(value, axis, [(i, i ^ offset) for i in range(lax.axis_size(a...  15.5 us
    ppermute x15, waiting for transfers between devices, swap(): lax.ppermute(value, axis, [(i, i ^ offset) for i in range(lax.axis_size(a...  11 us
    pallas_call x1, Pallas kernels, shards(): pl.pallas_call(rows_running, out_shape=jax.ShapeDtypeStruct((1, total_row...  3.46 us
    dot_general x1, matrix products, shards(): scores = jnp.dot(weights, src_all, preferred_element_type=f32)  2.34 us
    pallas_call x1, Pallas kernels, shards(): pl.pallas_call(front_kernel, out_shape=(pltpu.VMEM((packed_rows, rows //...  1.65 us
  transfers between devices with their start and end apart: 15, of which 11 were waited for; matrix products, arithmetic and copies ran while one was open for 0% of the time, Pallas kernels for 1%

profile of v1, /device:TPU:0, one launch (start us, length us, event | category | flops | bytes accessed | tf_op | source)
XLA Modules:
  0.0 69.2 jit_solution(3764786591949132313)
XLA Ops:
  0.6 1.6 %shard_map.76 = (f32[56,256]{1,0:T(8,128)S(1)}, f32[56,512]{1,0:T(8,128)S(1)}, f32[8,512]{1,0:T(8,128)S(1)}) custom-call(bf16[512,512]{1,0:T(8,128)(2,1)} %refs_0_.1, bf16[50,512]{1,0:T(8,128)(2,1)} %refs_1_.1, bf16[50,512]{1,0:T(8,128)(2,1)} %refs_2_.1, f32[1,512]{1,0:T(1,128)} %bitcast.6, f32[1,512]{1,0:T(1,128)} %bitcast.7), custom_call_target="tpu_custom_call" | custom-call | tf_op jit(solution)/shard_map/pallas_call | solution.py:475
  2.3 0.5 collective-permute-start
  2.8 0.8 %collective-permute-done = f32[8,512]{1,0:T(8,128)S(1)} collective-permute-done((f32[8,512]{1,0:T(8,128)S(1)}, f32[8,512]{1,0:T(8,128)S(1)}, u32[]{:S(2)}, u32[]{:S(2)}) %collective-permute-start) | collective-permute-done | bytes 16416 | tf_op jit(solution)/shard_map/ppermute | solution.py:448
  3.7 3.9 %collective-permute-start.3 = (f32[64,512]{1,0:T(8,128)S(1)}, f32[64,512]{1,0:T(8,128)S(1)}, u32[]{:S(2)}, u32[]{:S(2)}) collective-permute-start(f32[64,512]{1,0:T(8,128)S(1)} %constant_dynamic-update-slice_fusion), channel_id=1, source_target_pairs={{0,6},{1,7},{2,4},{3,5},{4,2},{5,3},{6,0},{7,1},{8,14},{9,15},{10,... | collective-permute-start | bytes 393224 | tf_op jit(solution)/shard_map/ppermute | solution.py:448
  7.5 0.5 collective-permute-start.2
  8.0 0.1 collective-permute-start.1
  8.2 4.0 %collective-permute-start.6 = (f32[56,256]{1,0:T(8,128)S(1)}, f32[56,256]{1,0:T(8,128)S(1)}, u32[]{:S(2)}, u32[]{:S(2)}) collective-permute-start(f32[56,256]{1,0:T(8,128)S(1)} %get-tuple-element.43), channel_id=1, source_target_pairs={{0,24},{8,16},{16,8},{24,0},{1,25},{9,17},{17,9},{25,1},{2,26},{10... | collective-permute-start | bytes 172040 | tf_op jit(solution)/shard_map/ppermute | solution.py:448
  12.2 1.2 %collective-permute-start.4 = (f32[56,256]{1,0:T(8,128)S(1)}, f32[56,256]{1,0:T(8,128)S(1)}, u32[]{:S(2)}, u32[]{:S(2)}) collective-permute-start(f32[56,256]{1,0:T(8,128)S(1)} %get-tuple-element.43), channel_id=1, source_target_pairs={{0,8},{8,0},{16,24},{24,16},{1,9},{9,1},{17,25},{25,17},{2,10},{10... | collective-permute-start | bytes 172040 | tf_op jit(solution)/shard_map/ppermute | solution.py:448
  13.4 0.8 %collective-permute-done.2.refs_2_ = f32[64,512]{1,0:T(8,128)S(1)} collective-permute-done((f32[64,512]{1,0:T(8,128)S(1)}, f32[64,512]{1,0:T(8,128)S(1)}, u32[]{:S(2)}, u32[]{:S(2)}) %collective-permute-start.2) | collective-permute-done | bytes 131104 | tf_op jit(solution)/shard_map/ppermute | solution.py:448
  14.2 0.3 collective-permute-done.1.refs_1_
  14.4 0.6 collective-permute-done.6
  15.0 2.2 %collective-permute-done.5 = f32[56,256]{1,0:T(8,128)S(1)} collective-permute-done((f32[56,256]{1,0:T(8,128)S(1)}, f32[56,256]{1,0:T(8,128)S(1)}, u32[]{:S(2)}, u32[]{:S(2)}) %collective-permute-start.5) | collective-permute-done | bytes 57376 | tf_op jit(solution)/shard_map/ppermute | solution.py:448
  17.3 0.1 collective-permute-start.7
  17.4 2.7 %collective-permute-start.10 = (f32[8,512]{1,0:T(8,128)S(1)}, f32[8,512]{1,0:T(8,128)S(1)}, u32[]{:S(2)}, u32[]{:S(2)}) collective-permute-start(f32[8,512]{1,0:T(8,128)S(1)} %add_add_fusion.refs_0_), channel_id=1, source_target_pairs={{0,24},{8,16},{16,8},{24,0},{1,25},{9,17},{17,9},{25,1},{2,26},{10... | collective-permute-start | bytes 49160 | tf_op jit(solution)/shard_map/ppermute | solution.py:448
  20.1 1.7 %collective-permute-start.8 = (f32[8,512]{1,0:T(8,128)S(1)}, f32[8,512]{1,0:T(8,128)S(1)}, u32[]{:S(2)}, u32[]{:S(2)}) collective-permute-start(f32[8,512]{1,0:T(8,128)S(1)} %add_add_fusion.refs_0_), channel_id=1, source_target_pairs={{0,8},{8,0},{16,24},{24,16},{1,9},{9,1},{17,25},{25,17},{2,10},{10... | collective-permute-start | bytes 49160 | tf_op jit(solution)/shard_map/ppermute | solution.py:448
  21.9 0.7 %shard_map.77 = (bf16[256,2048]{1,0:T(8,128)(2,1)S(1)}, bf16[2048,128]{1,0:T(8,128)(2,1)S(1)}, f32[1,2048]{1,0:T(1,128)S(1)}, f32[2048,128]{1,0:T(8,128)S(1)}, f32[1,2048]{1,0:T(1,128)S(1)}) custom-call(f32[224,256]{1,0:T(8,128)S(1)} %constant_dynamic-update-slice_fusion.2.near_ref, f32[224,256]{1,0:T(8,128)S(1)} %collective-permute-done.7.far_ref, ...), custom_call_target="tpu_custom_call" | custom-call | tf_op jit(solution)/shard_map/pallas_call | solution.py:504
  22.6 0.4 collective-permute-done.10.refs_3_
  23.0 1.7 %collective-permute-done.9.refs_2_ = f32[8,512]{1,0:T(8,128)S(1)} collective-permute-done((f32[8,512]{1,0:T(8,128)S(1)}, f32[8,512]{1,0:T(8,128)S(1)}, u32[]{:S(2)}, u32[]{:S(2)}) %collective-permute-start.9) | collective-permute-done | bytes 16416 | tf_op jit(solution)/shard_map/ppermute | solution.py:448
  24.8 0.8 %shard_map.78 = bf16[2048,256]{1,0:T(8,128)(2,1)S(1)} custom-call(bf16[2048,128]{1,0:T(8,128)(2,1)S(1)} %get-tuple-element.51.turned_ref, f32[8,512]{1,0:T(8,128)S(1)} %add_add_fusion.refs_0_, f32[8,512]{1,0:T(8,128)S(1)} %collective-permute-done.8.refs_1_, f32[8,512]{1,0:T(8,128)S(1)} %collective-permute-done.9.refs_2_, ...), custom_call_target="tpu_custom_call" | custom-call | tf_op jit(solution)/shard_map/pallas_call | solution.py:517
  25.5 2.3 %fusion.scores_ref = f32[2048,2048]{1,0:T(8,128)S(1)} fusion(bf16[2048,256]{1,0:T(8,128)(2,1)S(1)} %shard_map.78, bf16[256,2048]{1,0:T(8,128)(2,1)S(1)} %get-tuple-element.56), kind=kOutput, calls=%fused_computation.7 | convolution fusion | flops 2147483648 | bytes 18874368 | tf_op jit(solution)/shard_map/dot_general | solution.py:524
  27.9 3.5 %shard_map.79.sums_ref = f32[1,2048]{1,0:T(1,128)S(1)} custom-call(f32[2048,2048]{1,0:T(8,128)S(1)} %fusion.scores_ref), custom_call_target="tpu_custom_call" | custom-call | tf_op jit(solution)/shard_map/pallas_call | solution.py:525
  31.4 1.2 %collective-permute-done.11.more_ref = f32[1,2048]{1,0:T(1,128)S(1)} collective-permute-done((f32[1,2048]{1,0:T(1,128)S(1)}, f32[1,2048]{1,0:T(1,128)S(1)}, u32[]{:S(2)}, u32[]{:S(2)}) %collective-permute-start.11) | collective-permute-done | bytes 8224 | tf_op jit(solution)/shard_map/ppermute | solution.py:448
  32.6 10.5 %shard_map.80 = (f32[1,2048]{1,0:T(1,128)S(1)}, bf16[2048,2048]{1,0:T(8,128)(2,1)S(1)}, f32[8,2048]{1,0:T(8,128)S(1)}, f32[1,2048]{1,0:T(1,128)S(1)}) custom-call(f32[2048,2048]{1,0:T(8,128)S(1)} %fusion.scores_ref, f32[1,2048]{1,0:T(1,128)S(1)} %shard_map.79.sums_ref, f32[1,2048]{1,0:T(1,128)S(1)} %collective-permute-done.11.more_ref, ...), custom_call_target="tpu_custom_call" | custom-call | tf_op jit(solution)/shard_map/pallas_call | solution.py:543
  43.1 0.2 collective-permute-start.12
  43.3 1.0 %collective-permute-done.12.more_ref = f32[1,2048]{1,0:T(1,128)S(1)} collective-permute-done((f32[1,2048]{1,0:T(1,128)S(1)}, f32[1,2048]{1,0:T(1,128)S(1)}, u32[]{:S(2)}, u32[]{:S(2)}) %collective-permute-start.12) | collective-permute-done | bytes 8224 | tf_op jit(solution)/shard_map/ppermute | solution.py:448
  44.3 11.8 %shard_map.81 = (f32[1,2048]{1,0:T(1,128)S(1)}, bf16[2048,2048]{1,0:T(8,128)(2,1)S(1)}, f32[1,2048]{1,0:T(1,128)S(1)}, f32[1,2048]{1,0:T(1,128)S(1)}) custom-call(f32[2048,2048]{1,0:T(8,128)S(1)} %fusion.scores_ref, f32[1,2048]{1,0:T(1,128)S(1)} %get-tuple-element.60.sums_ref, f32[1,2048]{1,0:T(1,128)S(1)} %collective-permute-done.12.more_ref, ...), custom_call_target="tpu_custom_call" | custom-call | tf_op jit(solution)/shard_map/pallas_call | solution.py:543
  56.1 0.2 collective-permute-start.13
  56.4 1.0 %collective-permute-done.13.more_ref = f32[1,2048]{1,0:T(1,128)S(1)} collective-permute-done((f32[1,2048]{1,0:T(1,128)S(1)}, f32[1,2048]{1,0:T(1,128)S(1)}, u32[]{:S(2)}, u32[]{:S(2)}) %collective-permute-start.13) | collective-permute-done | bytes 8224 | tf_op jit(solution)/shard_map/ppermute | solution.py:448
  57.4 7.7 %shard_map.82.sums_ref = f32[1,2048]{1,0:T(1,128)S(1)} custom-call(f32[2048,2048]{1,0:T(8,128)S(1)} %fusion.scores_ref, f32[1,2048]{1,0:T(1,128)S(1)} %get-tuple-element.64.sums_ref, f32[1,2048]{1,0:T(1,128)S(1)} %collective-permute-done.13.more_ref, f32[1,2048]{1,0:T(1,128)S(1)} %get-tuple-element.57.log_src_ref, ...), custom_call_target="tpu_custom_call" | custom-call | tf_op jit(solution)/shard_map/pallas_call | solution.py:543
  65.1 0.2 collective-permute-start.14
  65.3 1.0 %collective-permute-done.14.more_ref = f32[1,2048]{1,0:T(1,128)S(1)} collective-permute-done((f32[1,2048]{1,0:T(1,128)S(1)}, f32[1,2048]{1,0:T(1,128)S(1)}, u32[]{:S(2)}, u32[]{:S(2)}) %collective-permute-start.14) | collective-permute-done | bytes 8224 | tf_op jit(solution)/shard_map/ppermute | solution.py:448
  66.3 2.8 %shard_map.83 = (f32[512,512]{1,0:T(8,128)}, f32[1,512]{1,0:T(1,128)}, f32[1,512]{1,0:T(1,128)}) custom-call(f32[2048,2048]{1,0:T(8,128)S(1)} %fusion.scores_ref, f32[1,2048]{1,0:T(1,128)S(1)} %shard_map.82.sums_ref, f32[1,2048]{1,0:T(1,128)S(1)} %collective-permute-done.14.more_ref, f32[1,2048]{1,0:T(1,128)S(1)} %get-tuple-element.57.log_src_ref, ...), custom_call_target="tpu_custom_call" | custom-call | tf_op jit(solution)/shard_map/pallas_call | solution.py:543
  (18 shorter events, 0.1 us)
Async XLA Ops:
  2.3 1.4 %collective-permute-start = (f32[8,512]{1,0:T(8,128)S(1)}, f32[8,512]{1,0:T(8,128)S(1)}, u32[]{:S(2)}, u32[]{:S(2)}) collective-permute-start(f32[8,512]{1,0:T(8,128)S(1)} %get-tuple-element.39), channel_id=1, source_target_pairs={{0,1},{1,0},{2,3},{3,2},{4,5},{5,4},{6,7},{7,6},{8,9},{9,8},{10,11... | collective-permute-start | bytes 49160 | tf_op jit(solution)/shard_map/ppermute | solution.py:448
  3.7 8.5 %collective-permute-start.3 = (f32[64,512]{1,0:T(8,128)S(1)}, f32[64,512]{1,0:T(8,128)S(1)}, u32[]{:S(2)}, u32[]{:S(2)}) collective-permute-start(f32[64,512]{1,0:T(8,128)S(1)} %constant_dynamic-update-slice_fusion), channel_id=1, source_target_pairs={{0,6},{1,7},{2,4},{3,5},{4,2},{5,3},{6,0},{7,1},{8,14},{9,15},{10,... | collective-permute-start | bytes 393224 | tf_op jit(solution)/shard_map/ppermute | solution.py:448
  7.5 6.6 %collective-permute-start.2 = (f32[64,512]{1,0:T(8,128)S(1)}, f32[64,512]{1,0:T(8,128)S(1)}, u32[]{:S(2)}, u32[]{:S(2)}) collective-permute-start(f32[64,512]{1,0:T(8,128)S(1)} %constant_dynamic-update-slice_fusion), channel_id=1, source_target_pairs={{0,4},{1,5},{2,6},{3,7},{4,0},{5,1},{6,2},{7,3},{8,12},{9,13},{10,... | collective-permute-start | bytes 393224 | tf_op jit(solution)/shard_map/ppermute | solution.py:448
  8.0 6.4 %collective-permute-start.1 = (f32[64,512]{1,0:T(8,128)S(1)}, f32[64,512]{1,0:T(8,128)S(1)}, u32[]{:S(2)}, u32[]{:S(2)}) collective-permute-start(f32[64,512]{1,0:T(8,128)S(1)} %constant_dynamic-update-slice_fusion), channel_id=1, source_target_pairs={{0,2},{1,3},{2,0},{3,1},{4,6},{5,7},{6,4},{7,5},{8,10},{9,11},{10,... | collective-permute-start | bytes 393224 | tf_op jit(solution)/shard_map/ppermute | solution.py:448
  8.2 6.8 %collective-permute-start.6 = (f32[56,256]{1,0:T(8,128)S(1)}, f32[56,256]{1,0:T(8,128)S(1)}, u32[]{:S(2)}, u32[]{:S(2)}) collective-permute-start(f32[56,256]{1,0:T(8,128)S(1)} %get-tuple-element.43), channel_id=1, source_target_pairs={{0,24},{8,16},{16,8},{24,0},{1,25},{9,17},{17,9},{25,1},{2,26},{10... | collective-permute-start | bytes 172040 | tf_op jit(solution)/shard_map/ppermute | solution.py:448
  12.2 5.1 %collective-permute-start.5 = (f32[56,256]{1,0:T(8,128)S(1)}, f32[56,256]{1,0:T(8,128)S(1)}, u32[]{:S(2)}, u32[]{:S(2)}) collective-permute-start(f32[56,256]{1,0:T(8,128)S(1)} %get-tuple-element.43), channel_id=1, source_target_pairs={{0,16},{8,24},{16,0},{24,8},{1,17},{9,25},{17,1},{25,9},{2,18},{10... | collective-permute-start | bytes 172040 | tf_op jit(solution)/shard_map/ppermute | solution.py:448
  12.2 5.1 %collective-permute-start.4 = (f32[56,256]{1,0:T(8,128)S(1)}, f32[56,256]{1,0:T(8,128)S(1)}, u32[]{:S(2)}, u32[]{:S(2)}) collective-permute-start(f32[56,256]{1,0:T(8,128)S(1)} %get-tuple-element.43), channel_id=1, source_target_pairs={{0,8},{8,0},{16,24},{24,16},{1,9},{9,1},{17,25},{25,17},{2,10},{10... | collective-permute-start | bytes 172040 | tf_op jit(solution)/shard_map/ppermute | solution.py:448
  17.3 4.6 %collective-permute-start.7 = (f32[224,256]{1,0:T(8,128)S(1)}, f32[224,256]{1,0:T(8,128)S(1)}, u32[]{:S(2)}, u32[]{:S(2)}) collective-permute-start(f32[224,256]{1,0:T(8,128)S(1)} %constant_dynamic-update-slice_fusion.2.near_ref), channel_id=1, source_target_pairs={{0,1},{1,0},{2,3},{3,2},{4,5},{5,4},{6,7},{7,6},{8,9},{9,8},{10,11... | collective-permute-start | bytes 688136 | tf_op jit(solution)/shard_map/ppermute | solution.py:448
  17.4 5.6 %collective-permute-start.10 = (f32[8,512]{1,0:T(8,128)S(1)}, f32[8,512]{1,0:T(8,128)S(1)}, u32[]{:S(2)}, u32[]{:S(2)}) collective-permute-start(f32[8,512]{1,0:T(8,128)S(1)} %add_add_fusion.refs_0_), channel_id=1, source_target_pairs={{0,24},{8,16},{16,8},{24,0},{1,25},{9,17},{17,9},{25,1},{2,26},{10... | collective-permute-start | bytes 49160 | tf_op jit(solution)/shard_map/ppermute | solution.py:448
  20.1 4.6 %collective-permute-start.9 = (f32[8,512]{1,0:T(8,128)S(1)}, f32[8,512]{1,0:T(8,128)S(1)}, u32[]{:S(2)}, u32[]{:S(2)}) collective-permute-start(f32[8,512]{1,0:T(8,128)S(1)} %add_add_fusion.refs_0_), channel_id=1, source_target_pairs={{0,16},{8,24},{16,0},{24,8},{1,17},{9,25},{17,1},{25,9},{2,18},{10... | collective-permute-start | bytes 49160 | tf_op jit(solution)/shard_map/ppermute | solution.py:448
  20.1 4.6 %collective-permute-start.8 = (f32[8,512]{1,0:T(8,128)S(1)}, f32[8,512]{1,0:T(8,128)S(1)}, u32[]{:S(2)}, u32[]{:S(2)}) collective-permute-start(f32[8,512]{1,0:T(8,128)S(1)} %add_add_fusion.refs_0_), channel_id=1, source_target_pairs={{0,8},{8,0},{16,24},{24,16},{1,9},{9,1},{17,25},{25,17},{2,10},{10... | collective-permute-start | bytes 49160 | tf_op jit(solution)/shard_map/ppermute | solution.py:448
  31.3 1.2 %collective-permute-start.11 = (f32[1,2048]{1,0:T(1,128)S(1)}, f32[1,2048]{1,0:T(1,128)S(1)}, u32[]{:S(2)}, u32[]{:S(2)}) collective-permute-start(f32[1,2048]{1,0:T(1,128)S(1)} %shard_map.79.sums_ref), channel_id=1, source_target_pairs={{0,1},{1,0},{2,3},{3,2},{4,5},{5,4},{6,7},{7,6},{8,9},{9,8},{10,11... | collective-permute-start | bytes 24584 | tf_op jit(solution)/shard_map/ppermute | solution.py:448
  43.1 1.2 %collective-permute-start.12 = (f32[1,2048]{1,0:T(1,128)S(1)}, f32[1,2048]{1,0:T(1,128)S(1)}, u32[]{:S(2)}, u32[]{:S(2)}) collective-permute-start(f32[1,2048]{1,0:T(1,128)S(1)} %get-tuple-element.60.sums_ref), channel_id=1, source_target_pairs={{0,1},{1,0},{2,3},{3,2},{4,5},{5,4},{6,7},{7,6},{8,9},{9,8},{10,11... | collective-permute-start | bytes 24584 | tf_op jit(solution)/shard_map/ppermute | solution.py:448
  56.1 1.2 %collective-permute-start.13 = (f32[1,2048]{1,0:T(1,128)S(1)}, f32[1,2048]{1,0:T(1,128)S(1)}, u32[]{:S(2)}, u32[]{:S(2)}) collective-permute-start(f32[1,2048]{1,0:T(1,128)S(1)} %get-tuple-element.64.sums_ref), channel_id=1, source_target_pairs={{0,1},{1,0},{2,3},{3,2},{4,5},{5,4},{6,7},{7,6},{8,9},{9,8},{10,11... | collective-permute-start | bytes 24584 | tf_op jit(solution)/shard_map/ppermute | solution.py:448
  65.1 1.2 %collective-permute-start.14 = (f32[1,2048]{1,0:T(1,128)S(1)}, f32[1,2048]{1,0:T(1,128)S(1)}, u32[]{:S(2)}, u32[]{:S(2)}) collective-permute-start(f32[1,2048]{1,0:T(1,128)S(1)} %shard_map.82.sums_ref), channel_id=1, source_target_pairs={{0,1},{1,0},{2,3},{3,2},{4,5},{5,4},{6,7},{7,6},{8,9},{9,8},{10,11... | collective-permute-start | bytes 24584 | tf_op jit(solution)/shard_map/ppermute | solution.py:448

commit v2 on v1

--- a/solution.py
+++ b/solution.py
@@ -50,23 +50,21 @@
 
 
 def front_kernel(*refs):
-    sources, (half_ref, whole_ref, moment_ref), local, sems = refs[:5], refs[5:8], refs[8:13], refs[13]
+    sources, (src_pack_ref, tgt_pack_ref, moment_ref), local, sems = refs[:5], refs[5:8], refs[8:13], refs[13]
     copies = [pltpu.make_async_copy(a, b, sems.at[i]) for i, (a, b) in enumerate(zip(sources, local))]
     for copy in copies:
         copy.start()
     coupling_ref, src_ref, tgt_ref, src_mass_ref, tgt_mass_ref = local
     pcs = src_ref.shape[0]
-    half = half_ref.shape[1]
-    odd = lax.rem(lax.axis_index("tgt"), 2)
     for copy in copies[1:]:
         copy.wait()
     src = src_ref[...].astype(jnp.float32)
     tgt = tgt_ref[...].astype(jnp.float32)
-    below = jnp.zeros((half_ref.shape[0] - pcs - 1, 2 * half), jnp.float32)
+    below = jnp.zeros((src_pack_ref.shape[0] - pcs - 1, src.shape[1]), jnp.float32)
     joined = jnp.concatenate([src, jnp.log2(src_mass_ref[...]), below], axis=0)
-    half_ref[...] = jnp.where(odd == 0, joined[:, :half], joined[:, half:])
-    below = jnp.zeros((half_ref.shape[0] - pcs - 1, tgt.shape[1]), jnp.float32)
-    whole_ref[...] = jnp.concatenate([tgt, jnp.log2(tgt_mass_ref[...]), below], axis=0)
+    src_pack_ref[...] = joined
+    below = jnp.zeros((src_pack_ref.shape[0] - pcs - 1, tgt.shape[1]), jnp.float32)
+    tgt_pack_ref[...] = jnp.concatenate([tgt, jnp.log2(tgt_mass_ref[...]), below], axis=0)
     src = padded(src).astype(jnp.bfloat16)
     tgt = padded(tgt).astype(jnp.bfloat16)
     twice = jnp.concatenate([src, src], axis=0)
@@ -82,35 +80,25 @@
         moment_ref[:, i * LANES : (i + 1) * LANES] = moment[i * 8 : i * 8 + 8]
 
 
-def prepare_kernel(pcs, blocks, merged, near_ref, far_ref, *refs):
-    tgt_refs, (src_ref, turned_ref, log_src_ref, log_tgt_ref, line_ref) = refs[:merged], refs[merged:]
-    packed_rows = near_ref.shape[0] // blocks
-    half = near_ref.shape[1]
-    width = tgt_refs[0].shape[1]
-    z = lax.axis_index("src")
-    t = lax.axis_index("tgt")
-    odd = lax.rem(t, 2)
-    total_rows = 2 * half * blocks
-    total_cols = width * lax.axis_size("tgt")
+def prepare_kernel(pcs, total_cols, packs_ref, tgt_packs_ref, src_ref, turned_ref, log_src_ref, log_tgt_ref, line_ref):
+    blocks, _, height = packs_ref.shape
+    merged, _, width = tgt_packs_ref.shape
     for b in range(blocks):
-        place = jnp.bitwise_xor(z, b)
-        for ref, side in ((near_ref, odd), (far_ref, 1 - odd)):
-            block = ref[pl.ds(b * packed_rows, packed_rows), :]
-            lanes = pl.ds(pl.multiple_of((place * 2 + side) * half, half), half)
-            log_src_ref[:, lanes] = marg_power * (block[pcs : pcs + 1] + math.log2(total_cols))
-            block = padded(block).astype(jnp.bfloat16)
-            for copy in range(4):
-                src_ref[pl.ds(copy * DEPTH, DEPTH), lanes] = block
-    mine = lax.rem(lax.div(t, 2), merged)
+        block = packs_ref[b]
+        lanes = pl.ds(b * height, height)
+        log_src_ref[:, lanes] = marg_power * (block[pcs : pcs + 1] + math.log2(total_cols))
+        block = padded(block).astype(jnp.bfloat16)
+        for copy in range(4):
+            src_ref[pl.ds(copy * DEPTH, DEPTH), lanes] = block
     for b in range(merged):
-        base = pl.multiple_of(jnp.bitwise_xor(mine, b) * width, width)
-        block = padded(tgt_refs[b][:packed_rows, :])
-        line_ref[:, pl.ds(base, width)] = marg_power * (block[pcs : pcs + 1] + math.log2(total_rows))
+        block = padded(tgt_packs_ref[b])
+        at = pl.ds(b * width, width)
+        line_ref[:, at] = marg_power * (block[pcs : pcs + 1] + math.log2(blocks * height))
         turned = jnp.concatenate([block, block], axis=0).T
-        log_tgt_ref[pl.ds(base, width), :] = jnp.broadcast_to(
-            marg_power * (turned[:, pcs : pcs + 1] + math.log2(total_rows)), (width, LANES)
+        log_tgt_ref[at, :] = jnp.broadcast_to(
+            marg_power * (turned[:, pcs : pcs + 1] + math.log2(blocks * height)), (width, LANES)
         )
-        turned_ref[pl.ds(base, width), :] = turned.astype(jnp.bfloat16)
+        turned_ref[at, :] = turned.astype(jnp.bfloat16)
 
 
 def start_kernel(pcs, entries, turned_ref, *refs):
@@ -472,10 +460,10 @@
     packed_rows = -(-(pcs + 1) // 8) * 8
 
     arguments = (coupling, src_pcs, tgt_pcs, src_mass.reshape(1, -1), tgt_mass.reshape(1, -1))
-    half, whole, moment = pl.pallas_call(
+    src_pack, tgt_pack, moment = pl.pallas_call(
         front_kernel,
         out_shape=(
-            pltpu.VMEM((packed_rows, rows // 2), f32),
+            pltpu.VMEM((packed_rows, rows), f32),
             pltpu.VMEM((packed_rows, cols), f32),
             pltpu.VMEM((8, 4 * LANES), f32),
         ),
@@ -486,23 +474,16 @@
         compiler_params=params(8),
     )(*[pltpu.with_memory_space_constraint(a, pltpu.HBM) for a in arguments])
 
+    src_packs = lax.all_gather(src_pack, "src")
+    ring = range(0, 2 * merged, 2)
+    groups = [[i + j for j in ring] for k in range(0, tgt_size, 2 * merged) for i in (k, k + 1)]
+    tgt_packs = lax.all_gather(tgt_pack, "tgt", axis_index_groups=groups) if merged > 1 else tgt_pack[None]
     moment = moment + swap(moment, "tgt", 1)
-    half, whole, moment = lax.optimization_barrier((half, whole, moment))
-    parts, targets = [moment], [whole]
-    if merged > 1:
-        message = jnp.concatenate([whole, moment], axis=0)
-        targets += [swap(message, "tgt", 2 * b) for b in range(1, merged)]
-        parts += [target[packed_rows:] for target in targets[1:]]
-    sources = [half] + [swap(half, "src", b) for b in range(1, src_size)]
-    parts, sources, targets = lax.optimization_barrier((parts, sources, targets))
-    if 2 * merged < tgt_size:
-        parts = staged_parts(tree(parts, jnp.add), "tgt", 2 * merged, 4)
+    parts = staged_parts(moment, "tgt", 2, 4)
     moments = staged_parts(tree(parts, jnp.add), "src", 1, 4)
-    near = jnp.concatenate(sources, axis=0)
-    far = swap(near, "tgt", 1)
 
     src_all, turned, log_src, log_tgt, log_tgt_line = pl.pallas_call(
-        functools.partial(prepare_kernel, pcs, src_size, merged),
+        functools.partial(prepare_kernel, pcs, total_cols),
         out_shape=(
             jax.ShapeDtypeStruct((4 * DEPTH, total_rows), jnp.bfloat16),
             jax.ShapeDtypeStruct((wide, LANES), jnp.bfloat16),
@@ -510,10 +491,10 @@
             jax.ShapeDtypeStruct((wide, LANES), f32),
             jax.ShapeDtypeStruct((1, wide), f32),
         ),
-        in_specs=[VMEM] * (2 + merged),
+        in_specs=[VMEM] * 2,
         out_specs=(VMEM,) * 5,
         compiler_params=params(10),
-    )(near, far, *targets)
+    )(src_packs, tgt_packs)
     weights = pl.pallas_call(
         functools.partial(start_kernel, pcs, total_rows * total_cols),
         out_shape=jax.ShapeDtypeStruct((wide, 4 * DEPTH), jnp.bfloat16),

time: 69.3 us -> 83.3 us (1.20)
  blocking collectives: 0 us -> 25.2 us
  waiting for transfers between devices: 11 us -> 5.03 us
  starting transfers between devices: 15.5 us -> 10.5 us
    all_gather x0 -> x2, blocking collectives: none -> 25.2 us  [the longest x1 15.4 us: shards(): src_packs = lax.all_gather(src_pack, 'src')]
    ppermute x15 -> x11, waiting for transfers between devices: 11 us -> 5.03 us  [swap(): lax.ppermute(value, axis, [(i, i ^ offset) for i in range(lax.axis_size(a...]
    ppermute x15 -> x11, starting transfers between devices: 15.5 us -> 10.5 us  [swap(): lax.ppermute(value, axis, [(i, i ^ offset) for i in range(lax.axis_size(a...]
  transfers between devices with their start and end apart: 15 -> 11, of which waited for: 11 -> 5; matrix products, arithmetic and copies ran while one was open for 0% -> 0% of each run, Pallas kernels for 1% -> 1%
where the time goes in v2:
time: 83.3 us; the launch traced here: 83.2 us
  Pallas kernels  39.4 us (47%)
  blocking collectives  25.2 us (30%)
  starting transfers between devices  10.5 us (13%)
  waiting for transfers between devices  5.03 us (6%)
  matrix products  2.34 us (3%)
    pallas_call x4, Pallas kernels, call(): pl.pallas_call(kernel, out_shape=tuple((jax.ShapeDtypeStruct(shape, bf16...  32.8 us
    all_gather x1, blocking collectives, shards(): src_packs = lax.all_gather(src_pack, 'src')  15.4 us
    ppermute x11, starting transfers between devices, swap(): lax.ppermute(value, axis, [(i, i ^ offset) for i in range(lax.axis_size(a...  10.5 us
    all_gather x1, blocking collectives, shards(): lax.all_gather(tgt_pack, 'tgt', axis_index_groups=groups)  9.77 us
    ppermute x11, waiting for transfers between devices, swap(): lax.ppermute(value, axis, [(i, i ^ offset) for i in range(lax.axis_size(a...  5.03 us
    pallas_call x1, Pallas kernels, shards(): pl.pallas_call(rows_running, out_shape=jax.ShapeDtypeStruct((1, total_row...  3.46 us
    dot_general x1, matrix products, shards(): scores = jnp.dot(weights, src_all, preferred_element_type=f32)  2.34 us
  transfers between devices with their start and end apart: 11, of which 5 were waited for; matrix products, arithmetic and copies ran while one was open for 0% of the time, Pallas kernels for 1%

profile of v2, /device:TPU:0, one launch (start us, length us, event | category | flops | bytes accessed | tf_op | source)
XLA Modules:
  0.0 83.2 jit_solution(5730118214822417399)
XLA Ops:
  0.6 1.6 %shard_map.76 = (f32[56,512]{1,0:T(8,128)S(1)}, f32[56,512]{1,0:T(8,128)S(1)}, f32[8,512]{1,0:T(8,128)S(1)}) custom-call(bf16[512,512]{1,0:T(8,128)(2,1)} %refs_0_.1, bf16[50,512]{1,0:T(8,128)(2,1)} %refs_1_.1, bf16[50,512]{1,0:T(8,128)(2,1)} %refs_2_.1, f32[1,512]{1,0:T(1,128)} %bitcast.10, f32[1,512]{1,0:T(1,128)} %bitcast.11), custom_call_target="tpu_custom_call" | custom-call | tf_op jit(solution)/shard_map/pallas_call | solution.py:463
  2.3 0.5 collective-permute-start
  2.8 0.8 %collective-permute-done = f32[8,512]{1,0:T(8,128)S(1)} collective-permute-done((f32[8,512]{1,0:T(8,128)S(1)}, f32[8,512]{1,0:T(8,128)S(1)}, u32[]{:S(2)}, u32[]{:S(2)}) %collective-permute-start) | collective-permute-done | bytes 16416 | tf_op jit(solution)/shard_map/ppermute | solution.py:436
  3.7 3.8 %collective-permute-start.3 = (f32[8,512]{1,0:T(8,128)S(1)}, f32[8,512]{1,0:T(8,128)S(1)}, u32[]{:S(2)}, u32[]{:S(2)}) collective-permute-start(f32[8,512]{1,0:T(8,128)S(1)} %add.12), channel_id=1, source_target_pairs={{0,6},{1,7},{2,4},{3,5},{4,2},{5,3},{6,0},{7,1},{8,14},{9,15},{10,... | collective-permute-start | bytes 49160 | tf_op jit(solution)/shard_map/ppermute | solution.py:436
  7.4 0.5 collective-permute-start.2
  7.9 0.1 collective-permute-start.1
  8.1 15.4 %all-gather = f32[224,512]{1,0:T(8,128)S(1)} all-gather(f32[56,512]{1,0:T(8,128)S(1)} %get-tuple-element.22), channel_id=2, replica_groups=mesh['src'=4,'tgt'=8] {'src'}, dimensions={0}, use_global_device_ids=true | all-gather | bytes 573440 | tf_op jit(solution)/shard_map/all_gather | solution.py:477
  23.5 0.0 collective-permute-done.3
  23.5 0.0 collective-permute-done.2
  23.5 0.0 collective-permute-done.1
  23.5 4.2 %collective-permute-start.6 = (f32[8,512]{1,0:T(8,128)S(1)}, f32[8,512]{1,0:T(8,128)S(1)}, u32[]{:S(2)}, u32[]{:S(2)}) collective-permute-start(f32[8,512]{1,0:T(8,128)S(1)} %add_add_fusion.refs_0_), channel_id=1, source_target_pairs={{0,24},{8,16},{16,8},{24,0},{1,25},{9,17},{17,9},{25,1},{2,26},{10... | collective-permute-start | bytes 49160 | tf_op jit(solution)/shard_map/ppermute | solution.py:436
  27.7 0.0 collective-permute-start.5
  27.7 0.6 collective-permute-start.4
  28.3 9.8 %all-gather.1 = f32[224,512]{1,0:T(8,128)S(1)} all-gather(f32[56,512]{1,0:T(8,128)S(1)} %get-tuple-element.23), channel_id=3, replica_groups={{0,2,4,6},{1,3,5,7},{8,10,12,14},{9,11,13,15},{16,18,20,22},{17,19,21,2..., dimensions={0}, use_global_device_ids=true | all-gather | bytes 573440 | tf_op jit(solution)/shard_map/all_gather | solution.py:480
  38.1 0.7 shard_map.77
  38.7 0.0 collective-permute-done.6.refs_3_
  38.7 0.0 collective-permute-done.4.refs_1_
  38.8 0.8 shard_map.78
  39.5 2.3 %fusion.scores_ref = f32[2048,2048]{1,0:T(8,128)S(1)} fusion(bf16[2048,256]{1,0:T(8,128)(2,1)S(1)} %shard_map.78, bf16[256,2048]{1,0:T(8,128)(2,1)S(1)} %get-tuple-element.26), kind=kOutput, calls=%fused_computation.1 | convolution fusion | flops 2147483648 | bytes 18874368 | tf_op jit(solution)/shard_map/dot_general | solution.py:505
  41.9 3.5 %shard_map.79.sums_ref = f32[1,2048]{1,0:T(1,128)S(1)} custom-call(f32[2048,2048]{1,0:T(8,128)S(1)} %fusion.scores_ref), custom_call_target="tpu_custom_call" | custom-call | tf_op jit(solution)/shard_map/pallas_call | solution.py:506
  45.3 0.1 collective-permute-start.7
  45.4 1.2 %collective-permute-done.7.more_ref = f32[1,2048]{1,0:T(1,128)S(1)} collective-permute-done((f32[1,2048]{1,0:T(1,128)S(1)}, f32[1,2048]{1,0:T(1,128)S(1)}, u32[]{:S(2)}, u32[]{:S(2)}) %collective-permute-start.7) | collective-permute-done | bytes 8224 | tf_op jit(solution)/shard_map/ppermute | solution.py:436
  46.6 10.5 %shard_map.80 = (f32[1,2048]{1,0:T(1,128)S(1)}, bf16[2048,2048]{1,0:T(8,128)(2,1)S(1)}, f32[8,2048]{1,0:T(8,128)S(1)}, f32[1,2048]{1,0:T(1,128)S(1)}) custom-call(f32[2048,2048]{1,0:T(8,128)S(1)} %fusion.scores_ref, f32[1,2048]{1,0:T(1,128)S(1)} %shard_map.79.sums_ref, f32[1,2048]{1,0:T(1,128)S(1)} %collective-permute-done.7.more_ref, ...), custom_call_target="tpu_custom_call" | custom-call | tf_op jit(solution)/shard_map/pallas_call | solution.py:524
  57.1 0.2 collective-permute-start.8
  57.3 1.0 %collective-permute-done.8.more_ref = f32[1,2048]{1,0:T(1,128)S(1)} collective-permute-done((f32[1,2048]{1,0:T(1,128)S(1)}, f32[1,2048]{1,0:T(1,128)S(1)}, u32[]{:S(2)}, u32[]{:S(2)}) %collective-permute-start.8) | collective-permute-done | bytes 8224 | tf_op jit(solution)/shard_map/ppermute | solution.py:436
  58.3 11.8 %shard_map.81 = (f32[1,2048]{1,0:T(1,128)S(1)}, bf16[2048,2048]{1,0:T(8,128)(2,1)S(1)}, f32[1,2048]{1,0:T(1,128)S(1)}, f32[1,2048]{1,0:T(1,128)S(1)}) custom-call(f32[2048,2048]{1,0:T(8,128)S(1)} %fusion.scores_ref, f32[1,2048]{1,0:T(1,128)S(1)} %get-tuple-element.30.sums_ref, f32[1,2048]{1,0:T(1,128)S(1)} %collective-permute-done.8.more_ref, ...), custom_call_target="tpu_custom_call" | custom-call | tf_op jit(solution)/shard_map/pallas_call | solution.py:524
  70.1 0.2 collective-permute-start.9
  70.4 1.0 %collective-permute-done.9.more_ref = f32[1,2048]{1,0:T(1,128)S(1)} collective-permute-done((f32[1,2048]{1,0:T(1,128)S(1)}, f32[1,2048]{1,0:T(1,128)S(1)}, u32[]{:S(2)}, u32[]{:S(2)}) %collective-permute-start.9) | collective-permute-done | bytes 8224 | tf_op jit(solution)/shard_map/ppermute | solution.py:436
  71.4 7.7 %shard_map.82.sums_ref = f32[1,2048]{1,0:T(1,128)S(1)} custom-call(f32[2048,2048]{1,0:T(8,128)S(1)} %fusion.scores_ref, f32[1,2048]{1,0:T(1,128)S(1)} %get-tuple-element.34.sums_ref, f32[1,2048]{1,0:T(1,128)S(1)} %collective-permute-done.9.more_ref, f32[1,2048]{1,0:T(1,128)S(1)} %get-tuple-element.27.log_src_ref, ...), custom_call_target="tpu_custom_call" | custom-call | tf_op jit(solution)/shard_map/pallas_call | solution.py:524
  79.1 0.2 collective-permute-start.10
  79.3 1.0 %collective-permute-done.10.more_ref = f32[1,2048]{1,0:T(1,128)S(1)} collective-permute-done((f32[1,2048]{1,0:T(1,128)S(1)}, f32[1,2048]{1,0:T(1,128)S(1)}, u32[]{:S(2)}, u32[]{:S(2)}) %collective-permute-start.10) | collective-permute-done | bytes 8224 | tf_op jit(solution)/shard_map/ppermute | solution.py:436
  80.3 2.8 %shard_map.83 = (f32[512,512]{1,0:T(8,128)}, f32[1,512]{1,0:T(1,128)}, f32[1,512]{1,0:T(1,128)}) custom-call(f32[2048,2048]{1,0:T(8,128)S(1)} %fusion.scores_ref, f32[1,2048]{1,0:T(1,128)S(1)} %shard_map.82.sums_ref, f32[1,2048]{1,0:T(1,128)S(1)} %collective-permute-done.10.more_ref, f32[1,2048]{1,0:T(1,128)S(1)} %get-tuple-element.27.log_src_ref, ...), custom_call_target="tpu_custom_call" | custom-call | tf_op jit(solution)/shard_map/pallas_call | solution.py:524
  (3 shorter events, 0.0 us)
Async XLA Ops:
  2.3 1.4 %collective-permute-start = (f32[8,512]{1,0:T(8,128)S(1)}, f32[8,512]{1,0:T(8,128)S(1)}, u32[]{:S(2)}, u32[]{:S(2)}) collective-permute-start(f32[8,512]{1,0:T(8,128)S(1)} %get-tuple-element.25), channel_id=1, source_target_pairs={{0,1},{1,0},{2,3},{3,2},{4,5},{5,4},{6,7},{7,6},{8,9},{9,8},{10,11... | collective-permute-start | bytes 49160 | tf_op jit(solution)/shard_map/ppermute | solution.py:436
  3.7 19.8 %collective-permute-start.3 = (f32[8,512]{1,0:T(8,128)S(1)}, f32[8,512]{1,0:T(8,128)S(1)}, u32[]{:S(2)}, u32[]{:S(2)}) collective-permute-start(f32[8,512]{1,0:T(8,128)S(1)} %add.12), channel_id=1, source_target_pairs={{0,6},{1,7},{2,4},{3,5},{4,2},{5,3},{6,0},{7,1},{8,14},{9,15},{10,... | collective-permute-start | bytes 49160 | tf_op jit(solution)/shard_map/ppermute | solution.py:436
  7.4 16.0 %collective-permute-start.2 = (f32[8,512]{1,0:T(8,128)S(1)}, f32[8,512]{1,0:T(8,128)S(1)}, u32[]{:S(2)}, u32[]{:S(2)}) collective-permute-start(f32[8,512]{1,0:T(8,128)S(1)} %add.12), channel_id=1, source_target_pairs={{0,4},{1,5},{2,6},{3,7},{4,0},{5,1},{6,2},{7,3},{8,12},{9,13},{10,... | collective-permute-start | bytes 49160 | tf_op jit(solution)/shard_map/ppermute | solution.py:436
  7.9 15.5 %collective-permute-start.1 = (f32[8,512]{1,0:T(8,128)S(1)}, f32[8,512]{1,0:T(8,128)S(1)}, u32[]{:S(2)}, u32[]{:S(2)}) collective-permute-start(f32[8,512]{1,0:T(8,128)S(1)} %add.12), channel_id=1, source_target_pairs={{0,2},{1,3},{2,0},{3,1},{4,6},{5,7},{6,4},{7,5},{8,10},{9,11},{10,... | collective-permute-start | bytes 49160 | tf_op jit(solution)/shard_map/ppermute | solution.py:436
  23.5 15.2 %collective-permute-start.6 = (f32[8,512]{1,0:T(8,128)S(1)}, f32[8,512]{1,0:T(8,128)S(1)}, u32[]{:S(2)}, u32[]{:S(2)}) collective-permute-start(f32[8,512]{1,0:T(8,128)S(1)} %add_add_fusion.refs_0_), channel_id=1, source_target_pairs={{0,24},{8,16},{16,8},{24,0},{1,25},{9,17},{17,9},{25,1},{2,26},{10... | collective-permute-start | bytes 49160 | tf_op jit(solution)/shard_map/ppermute | solution.py:436
  27.7 11.1 %collective-permute-start.5 = (f32[8,512]{1,0:T(8,128)S(1)}, f32[8,512]{1,0:T(8,128)S(1)}, u32[]{:S(2)}, u32[]{:S(2)}) collective-permute-start(f32[8,512]{1,0:T(8,128)S(1)} %add_add_fusion.refs_0_), channel_id=1, source_target_pairs={{0,16},{8,24},{16,0},{24,8},{1,17},{9,25},{17,1},{25,9},{2,18},{10... | collective-permute-start | bytes 49160 | tf_op jit(solution)/shard_map/ppermute | solution.py:436
  27.7 11.1 %collective-permute-start.4 = (f32[8,512]{1,0:T(8,128)S(1)}, f32[8,512]{1,0:T(8,128)S(1)}, u32[]{:S(2)}, u32[]{:S(2)}) collective-permute-start(f32[8,512]{1,0:T(8,128)S(1)} %add_add_fusion.refs_0_), channel_id=1, source_target_pairs={{0,8},{8,0},{16,24},{24,16},{1,9},{9,1},{17,25},{25,17},{2,10},{10... | collective-permute-start | bytes 49160 | tf_op jit(solution)/shard_map/ppermute | solution.py:436
  45.3 1.2 %collective-permute-start.7 = (f32[1,2048]{1,0:T(1,128)S(1)}, f32[1,2048]{1,0:T(1,128)S(1)}, u32[]{:S(2)}, u32[]{:S(2)}) collective-permute-start(f32[1,2048]{1,0:T(1,128)S(1)} %shard_map.79.sums_ref), channel_id=1, source_target_pairs={{0,1},{1,0},{2,3},{3,2},{4,5},{5,4},{6,7},{7,6},{8,9},{9,8},{10,11... | collective-permute-start | bytes 24584 | tf_op jit(solution)/shard_map/ppermute | solution.py:436
  57.1 1.2 %collective-permute-start.8 = (f32[1,2048]{1,0:T(1,128)S(1)}, f32[1,2048]{1,0:T(1,128)S(1)}, u32[]{:S(2)}, u32[]{:S(2)}) collective-permute-start(f32[1,2048]{1,0:T(1,128)S(1)} %get-tuple-element.30.sums_ref), channel_id=1, source_target_pairs={{0,1},{1,0},{2,3},{3,2},{4,5},{5,4},{6,7},{7,6},{8,9},{9,8},{10,11... | collective-permute-start | bytes 24584 | tf_op jit(solution)/shard_map/ppermute | solution.py:436
  70.1 1.2 %collective-permute-start.9 = (f32[1,2048]{1,0:T(1,128)S(1)}, f32[1,2048]{1,0:T(1,128)S(1)}, u32[]{:S(2)}, u32[]{:S(2)}) collective-permute-start(f32[1,2048]{1,0:T(1,128)S(1)} %get-tuple-element.34.sums_ref), channel_id=1, source_target_pairs={{0,1},{1,0},{2,3},{3,2},{4,5},{5,4},{6,7},{7,6},{8,9},{9,8},{10,11... | collective-permute-start | bytes 24584 | tf_op jit(solution)/shard_map/ppermute | solution.py:436
  79.1 1.2 %collective-permute-start.10 = (f32[1,2048]{1,0:T(1,128)S(1)}, f32[1,2048]{1,0:T(1,128)S(1)}, u32[]{:S(2)}, u32[]{:S(2)}) collective-permute-start(f32[1,2048]{1,0:T(1,128)S(1)} %shard_map.82.sums_ref), channel_id=1, source_target_pairs={{0,1},{1,0},{2,3},{3,2},{4,5},{5,4},{6,7},{7,6},{8,9},{9,8},{10,11... | collective-permute-start | bytes 24584 | tf_op jit(solution)/shard_map/ppermute | solution.py:436

commit v3 on v1

--- a/solution.py
+++ b/solution.py
@@ -211,44 +211,48 @@
             out_ref[:, lanes] = down(*state)
 
 
-def columns_exp(scores_ref, rows_ref, top_ref, sum_ref, base, count, keep_ref):
+def columns_exp(scores_ref, rows_ref, top_ref, sum_ref, rounded_ref, count, keep_ref):
     tiles = lane_tiles(scores_ref)
 
     def highest(i, carry):
         places = [pl.ds(pl.multiple_of(i * 64 + g * 8, 8), 8) for g in range(8)]
-        sources = [pl.ds(pl.multiple_of(base + i * 64 + g * 8, 8), 8) for g in range(8)]
         tops = [None] * 8
         for lanes in tiles:
             row = rows_ref[:, lanes]
-            for g, source in enumerate(sources):
-                term = scores_ref[source, lanes] + row
+            for g, place in enumerate(places):
+                term = scores_ref[place, lanes] + row
                 tops[g] = term if tops[g] is None else jnp.maximum(tops[g], term)
         for place, top in zip(places, tops):
             top_ref[place, :] = top - LIFT
         return carry
 
     def total(i, carry):
-        pairs = [halves(base + i * 64 + g * 16) for g in range(4)]
-        places = [place for g in range(4) for place in halves(i * 64 + g * 16)[1]]
+        pairs = [halves(i * 64 + g * 16) for g in range(4)]
+        places = [place for _, pair in pairs for place in pair]
         tops = [top_ref[place, :] for place in places]
         sums = [jnp.zeros((8, LANES), jnp.float32)] * 8
+        rounded = [jnp.zeros((8, LANES), jnp.float32)] * 8
         for lanes in tiles:
             row = rows_ref[:, lanes]
             for g, (at, sources) in enumerate(pairs):
-                parts = []
-                for h, source in enumerate(sources):
-                    parts.append(jnp.exp2(scores_ref[source, lanes] + row - tops[2 * g + h]))
+                parts = [
+                    jnp.exp2(scores_ref[source, lanes] + row - tops[2 * g + h])
+                    for h, source in enumerate(sources)
+                ]
+                kept = jnp.concatenate(parts, axis=0).astype(keep_ref.dtype)
+                keep_ref[at, lanes] = kept
+                kept = kept.astype(jnp.float32)
+                for h in range(2):
                     sums[2 * g + h] = sums[2 * g + h] + parts[h]
-                if keep_ref is not None:
-                    keep_ref[at, lanes] = jnp.concatenate(parts, axis=0).astype(keep_ref.dtype)
-        for place, value in zip(places, sums):
+                    rounded[2 * g + h] = rounded[2 * g + h] + kept[8 * h : 8 * h + 8]
+        for place, value, other in zip(places, sums, rounded):
             sum_ref[place, :] = value
+            rounded_ref[place, :] = other
         return carry
 
     lax.fori_loop(0, count // 64, highest, 0)
-    if keep_ref is not None:
-        tops = top_ref[pl.ds(0, count), :]
-        top_ref[pl.ds(0, count), :] = jnp.broadcast_to(jnp.max(tops, axis=1, keepdims=True), tops.shape)
+    tops = top_ref[...]
+    top_ref[...] = jnp.broadcast_to(jnp.max(tops, axis=1, keepdims=True), tops.shape)
     lax.fori_loop(0, count // 64, total, 0)
 
 
@@ -324,25 +328,31 @@
     over_tiles(*scores_ref.shape, body, jnp.full((8, LANES), -jnp.inf, jnp.float32), done)
 
 
-def rows_exp(scores_ref, cols_ref, top_ref, out_ref, keep_ref):
+def rows_exp(scores_ref, cols_ref, top_ref, out_ref, keep_ref, level_ref):
     def body(pairs, tiles, carry):
         tops = [top_ref[:, lanes] for lanes in tiles]
         for at, places in pairs:
-            if cols_ref is not None:
-                potentials = [cols_ref[place, :] for place in places]
+            potentials = [cols_ref[place, :] for place in places]
             for j, lanes in enumerate(tiles):
-                terms = [scores_ref[place, lanes] for place in places]
-                if cols_ref is not None:
-                    terms = [term + potential for term, potential in zip(terms, potentials)]
+                terms = [scores_ref[place, lanes] + c for place, c in zip(places, potentials)]
                 parts = [jnp.exp2(term - tops[j]) for term in terms]
+                summed, rounded = carry[j]
                 if keep_ref is not None:
-                    keep_ref[at, lanes] = jnp.concatenate(parts, axis=0).astype(keep_ref.dtype)
-                carry[j] = carry[j] + (parts[0] + parts[1])
+                    kept = jnp.concatenate(parts, axis=0).astype(keep_ref.dtype)
+                    keep_ref[at, lanes] = kept
+                    kept = kept.astype(jnp.float32)
+                    rounded = rounded + (kept[:8] + kept[8:])
+                carry[j] = summed + (parts[0] + parts[1]), rounded
 
     def done(lanes, value):
-        out_ref[:, lanes] = down(top_ref[:, lanes], value)
-
-    over_tiles(*scores_ref.shape, body, jnp.zeros((8, LANES), jnp.float32), done)
+        exact = down(top_ref[:, lanes], value[0])
+        out_ref[:, lanes] = exact
+        if keep_ref is not None:
+            level = top_ref[:, lanes] + (exact - down(top_ref[:, lanes], value[1]))
+            level_ref[:, lanes] = level
+
+    zero = jnp.zeros((8, LANES), jnp.float32)
+    over_tiles(*scores_ref.shape, body, (zero, zero), done)
 
 
 def rows_product(keep_ref, kept_top_ref, factor, shift, out_ref):
@@ -391,7 +401,7 @@
     def _():
         cols_ref[...] = jnp.broadcast_to(line_ref[...], (LANES, line_ref.shape[1])).T
         rows_highest(scores_ref, cols_ref, row_top_ref)
-        rows_exp(scores_ref, cols_ref, row_top_ref, out_ref, None)
+        rows_exp(scores_ref, cols_ref, row_top_ref, out_ref, None, None)
 
 
 def first_kernel(scores_ref, sums_ref, more_ref, log_src_ref, log_tgt_ref, log_tgt_line_ref, *refs):
@@ -403,18 +413,20 @@
     columns_finish(top_ref, sum_ref, log_tgt_ref, cols_ref, 0, count)
     line_ref[...] = cols_ref[...].T[0:1, :]
     rows_highest(scores_ref, cols_ref, row_top_ref)
-    rows_exp(scores_ref, cols_ref, row_top_ref, out_ref, keep_ref)
+    rows_exp(scores_ref, cols_ref, row_top_ref, out_ref, keep_ref, row_top_ref)
 
 
 def second_kernel(scores_ref, sums_ref, more_ref, log_src_ref, log_tgt_ref, log_tgt_line_ref, *refs):
     kept, (out_ref, keep_ref, kept_top_ref, base_ref) = refs[:3], refs[3:7]
-    rows_ref, cols_ref, top_ref, sum_ref, line_ref, row_top_ref = refs[7:]
+    rows_ref, cols_ref, top_ref, sum_ref, line_ref, row_top_ref, rounded_ref = refs[7:]
     base_ref[...] = row_values(log_src_ref, sums_ref, more_ref)
     rows_ref[...] = jnp.broadcast_to(base_ref[...], rows_ref.shape)
     count = scores_ref.shape[0]
-    columns_exp(scores_ref, rows_ref, top_ref, sum_ref, 0, count, keep_ref)
-    columns_finish(top_ref, sum_ref, log_tgt_ref, cols_ref, 0, count)
-    kept_top_ref[...] = top_ref[...].T[0:1, :]
+    columns_exp(scores_ref, rows_ref, top_ref, sum_ref, rounded_ref, count, keep_ref)
+    totals = jnp.log2(jnp.sum(sum_ref[...], axis=1, keepdims=True))
+    level = top_ref[...] + (totals - jnp.log2(jnp.sum(rounded_ref[...], axis=1, keepdims=True)))
+    kept_top_ref[...] = level.T[0:1, :]
+    cols_ref[...] = log_tgt_ref[...] - marg_power * (top_ref[...] + totals)
     line_ref[...] = cols_ref[...].T[0:1, :]
     rows_either(scores_ref, line_ref, kept, cols_ref, row_top_ref, out_ref)
 
@@ -553,7 +565,7 @@
     side, columns = (1, wide), (lines, pads, pads, pads)
     sums, *kept_rows = call(first_kernel, sums, (), (line, block, lines, side), columns)
     sums, *kept_columns = call(
-        second_kernel, sums, kept_rows, (line, block, side, line), (*columns, side, lines)
+        second_kernel, sums, kept_rows, (line, block, side, line), (*columns, side, lines, pads)
     )
     for iteration in range(ITERS - 3):
         (sums,) = call(

time: 69.3 us -> 73.5 us (1.061); the launches traced: 69.2 us -> 74.7 us
  Pallas kernels: 39.4 us -> 45 us
    pallas_call x4, Pallas kernels: 32.8 us -> 38.4 us  [call(): pl.pallas_call(kernel, out_shape=tuple((jax.ShapeDtypeStruct(shape, bf16...]
where the time goes in v3:
time: 73.5 us; the launch traced here: 74.7 us
  Pallas kernels  45 us (61%)
  starting transfers between devices  15.5 us (21%)
  waiting for transfers between devices  11 us (15%)
  matrix products  2.34 us (3%)
  between operations  0.76 us (1%)
    pallas_call x4, Pallas kernels, call(): pl.pallas_call(kernel, out_shape=tuple((jax.ShapeDtypeStruct(shape, bf16...  38.4 us
    ppermute x15, starting transfers between devices, swap(): lax.ppermute(value, axis, [(i, i ^ offset) for i in range(lax.axis_size(a...  15.5 us
    ppermute x15, waiting for transfers between devices, swap(): lax.ppermute(value, axis, [(i, i ^ offset) for i in range(lax.axis_size(a...  11 us
    pallas_call x1, Pallas kernels, shards(): pl.pallas_call(rows_running, out_shape=jax.ShapeDtypeStruct((1, total_row...  3.46 us
    dot_general x1, matrix products, shards(): scores = jnp.dot(weights, src_all, preferred_element_type=f32)  2.34 us
    pallas_call x1, Pallas kernels, shards(): pl.pallas_call(front_kernel, out_shape=(pltpu.VMEM((packed_rows, rows //...  1.65 us
  transfers between devices with their start and end apart: 15, of which 11 were waited for; matrix products, arithmetic and copies ran while one was open for 0% of the time, Pallas kernels for 1%

profile of v3, /device:TPU:0, one launch (start us, length us, event | category | flops | bytes accessed | tf_op | source)
XLA Modules:
  0.0 74.7 jit_solution(14839829277805906239)
XLA Ops:
  0.6 1.6 %shard_map.76 = (f32[56,256]{1,0:T(8,128)S(1)}, f32[56,512]{1,0:T(8,128)S(1)}, f32[8,512]{1,0:T(8,128)S(1)}) custom-call(bf16[512,512]{1,0:T(8,128)(2,1)} %refs_0_.1, bf16[50,512]{1,0:T(8,128)(2,1)} %refs_1_.1, bf16[50,512]{1,0:T(8,128)(2,1)} %refs_2_.1, f32[1,512]{1,0:T(1,128)} %bitcast.6, f32[1,512]{1,0:T(1,128)} %bitcast.7), custom_call_target="tpu_custom_call" | custom-call | tf_op jit(solution)/shard_map/pallas_call | solution.py:487
  2.3 0.5 collective-permute-start
  2.8 0.8 %collective-permute-done = f32[8,512]{1,0:T(8,128)S(1)} collective-permute-done((f32[8,512]{1,0:T(8,128)S(1)}, f32[8,512]{1,0:T(8,128)S(1)}, u32[]{:S(2)}, u32[]{:S(2)}) %collective-permute-start) | collective-permute-done | bytes 16416 | tf_op jit(solution)/shard_map/ppermute | solution.py:460
  3.7 3.9 %collective-permute-start.3 = (f32[64,512]{1,0:T(8,128)S(1)}, f32[64,512]{1,0:T(8,128)S(1)}, u32[]{:S(2)}, u32[]{:S(2)}) collective-permute-start(f32[64,512]{1,0:T(8,128)S(1)} %constant_dynamic-update-slice_fusion), channel_id=1, source_target_pairs={{0,6},{1,7},{2,4},{3,5},{4,2},{5,3},{6,0},{7,1},{8,14},{9,15},{10,... | collective-permute-start | bytes 393224 | tf_op jit(solution)/shard_map/ppermute | solution.py:460
  7.5 0.5 collective-permute-start.2
  8.0 0.1 collective-permute-start.1
  8.2 4.0 %collective-permute-start.6 = (f32[56,256]{1,0:T(8,128)S(1)}, f32[56,256]{1,0:T(8,128)S(1)}, u32[]{:S(2)}, u32[]{:S(2)}) collective-permute-start(f32[56,256]{1,0:T(8,128)S(1)} %get-tuple-element.43), channel_id=1, source_target_pairs={{0,24},{8,16},{16,8},{24,0},{1,25},{9,17},{17,9},{25,1},{2,26},{10... | collective-permute-start | bytes 172040 | tf_op jit(solution)/shard_map/ppermute | solution.py:460
  12.2 1.2 %collective-permute-start.4 = (f32[56,256]{1,0:T(8,128)S(1)}, f32[56,256]{1,0:T(8,128)S(1)}, u32[]{:S(2)}, u32[]{:S(2)}) collective-permute-start(f32[56,256]{1,0:T(8,128)S(1)} %get-tuple-element.43), channel_id=1, source_target_pairs={{0,8},{8,0},{16,24},{24,16},{1,9},{9,1},{17,25},{25,17},{2,10},{10... | collective-permute-start | bytes 172040 | tf_op jit(solution)/shard_map/ppermute | solution.py:460
  13.4 0.8 %collective-permute-done.2.refs_2_ = f32[64,512]{1,0:T(8,128)S(1)} collective-permute-done((f32[64,512]{1,0:T(8,128)S(1)}, f32[64,512]{1,0:T(8,128)S(1)}, u32[]{:S(2)}, u32[]{:S(2)}) %collective-permute-start.2) | collective-permute-done | bytes 131104 | tf_op jit(solution)/shard_map/ppermute | solution.py:460
  14.2 0.3 collective-permute-done.1.refs_1_
  14.4 0.6 collective-permute-done.6
  15.0 2.2 %collective-permute-done.5 = f32[56,256]{1,0:T(8,128)S(1)} collective-permute-done((f32[56,256]{1,0:T(8,128)S(1)}, f32[56,256]{1,0:T(8,128)S(1)}, u32[]{:S(2)}, u32[]{:S(2)}) %collective-permute-start.5) | collective-permute-done | bytes 57376 | tf_op jit(solution)/shard_map/ppermute | solution.py:460
  17.3 0.1 collective-permute-start.7
  17.4 2.7 %collective-permute-start.10 = (f32[8,512]{1,0:T(8,128)S(1)}, f32[8,512]{1,0:T(8,128)S(1)}, u32[]{:S(2)}, u32[]{:S(2)}) collective-permute-start(f32[8,512]{1,0:T(8,128)S(1)} %add_add_fusion.refs_0_), channel_id=1, source_target_pairs={{0,24},{8,16},{16,8},{24,0},{1,25},{9,17},{17,9},{25,1},{2,26},{10... | collective-permute-start | bytes 49160 | tf_op jit(solution)/shard_map/ppermute | solution.py:460
  20.1 1.7 %collective-permute-start.8 = (f32[8,512]{1,0:T(8,128)S(1)}, f32[8,512]{1,0:T(8,128)S(1)}, u32[]{:S(2)}, u32[]{:S(2)}) collective-permute-start(f32[8,512]{1,0:T(8,128)S(1)} %add_add_fusion.refs_0_), channel_id=1, source_target_pairs={{0,8},{8,0},{16,24},{24,16},{1,9},{9,1},{17,25},{25,17},{2,10},{10... | collective-permute-start | bytes 49160 | tf_op jit(solution)/shard_map/ppermute | solution.py:460
  21.9 0.7 shard_map.77
  22.6 0.4 collective-permute-done.10.refs_3_
  23.0 1.7 %collective-permute-done.9.refs_2_ = f32[8,512]{1,0:T(8,128)S(1)} collective-permute-done((f32[8,512]{1,0:T(8,128)S(1)}, f32[8,512]{1,0:T(8,128)S(1)}, u32[]{:S(2)}, u32[]{:S(2)}) %collective-permute-start.9) | collective-permute-done | bytes 16416 | tf_op jit(solution)/shard_map/ppermute | solution.py:460
  24.8 0.8 %shard_map.78 = bf16[2048,256]{1,0:T(8,128)(2,1)S(1)} custom-call(bf16[2048,128]{1,0:T(8,128)(2,1)S(1)} %get-tuple-element.51.turned_ref, f32[8,512]{1,0:T(8,128)S(1)} %add_add_fusion.refs_0_, f32[8,512]{1,0:T(8,128)S(1)} %collective-permute-done.8.refs_1_, f32[8,512]{1,0:T(8,128)S(1)} %collective-permute-done.9.refs_2_, ...), custom_call_target="tpu_custom_call" | custom-call | tf_op jit(solution)/shard_map/pallas_call | solution.py:529
  25.5 2.3 %fusion.scores_ref = f32[2048,2048]{1,0:T(8,128)S(1)} fusion(bf16[2048,256]{1,0:T(8,128)(2,1)S(1)} %shard_map.78, bf16[256,2048]{1,0:T(8,128)(2,1)S(1)} %get-tuple-element.56), kind=kOutput, calls=%fused_computation.7 | convolution fusion | flops 2147483648 | bytes 18874368 | tf_op jit(solution)/shard_map/dot_general | solution.py:536
  27.9 3.5 %shard_map.79.sums_ref = f32[1,2048]{1,0:T(1,128)S(1)} custom-call(f32[2048,2048]{1,0:T(8,128)S(1)} %fusion.scores_ref), custom_call_target="tpu_custom_call" | custom-call | tf_op jit(solution)/shard_map/pallas_call | solution.py:537
  31.4 1.2 %collective-permute-done.11.more_ref = f32[1,2048]{1,0:T(1,128)S(1)} collective-permute-done((f32[1,2048]{1,0:T(1,128)S(1)}, f32[1,2048]{1,0:T(1,128)S(1)}, u32[]{:S(2)}, u32[]{:S(2)}) %collective-permute-start.11) | collective-permute-done | bytes 8224 | tf_op jit(solution)/shard_map/ppermute | solution.py:460
  32.6 11.9 %shard_map.80 = (f32[1,2048]{1,0:T(1,128)S(1)}, bf16[2048,2048]{1,0:T(8,128)(2,1)S(1)}, f32[8,2048]{1,0:T(8,128)S(1)}, f32[1,2048]{1,0:T(1,128)S(1)}) custom-call(f32[2048,2048]{1,0:T(8,128)S(1)} %fusion.scores_ref, f32[1,2048]{1,0:T(1,128)S(1)} %shard_map.79.sums_ref, f32[1,2048]{1,0:T(1,128)S(1)} %collective-permute-done.11.more_ref, ...), custom_call_target="tpu_custom_call" | custom-call | tf_op jit(solution)/shard_map/pallas_call | solution.py:555
  44.5 0.2 collective-permute-start.12
  44.7 1.0 %collective-permute-done.12.more_ref = f32[1,2048]{1,0:T(1,128)S(1)} collective-permute-done((f32[1,2048]{1,0:T(1,128)S(1)}, f32[1,2048]{1,0:T(1,128)S(1)}, u32[]{:S(2)}, u32[]{:S(2)}) %collective-permute-start.12) | collective-permute-done | bytes 8224 | tf_op jit(solution)/shard_map/ppermute | solution.py:460
  45.7 13.2 %shard_map.81 = (f32[1,2048]{1,0:T(1,128)S(1)}, bf16[2048,2048]{1,0:T(8,128)(2,1)S(1)}, f32[1,2048]{1,0:T(1,128)S(1)}, f32[1,2048]{1,0:T(1,128)S(1)}) custom-call(f32[2048,2048]{1,0:T(8,128)S(1)} %fusion.scores_ref, f32[1,2048]{1,0:T(1,128)S(1)} %get-tuple-element.60.sums_ref, f32[1,2048]{1,0:T(1,128)S(1)} %collective-permute-done.12.more_ref, ...), custom_call_target="tpu_custom_call" | custom-call | tf_op jit(solution)/shard_map/pallas_call | solution.py:555
  58.9 0.2 collective-permute-start.13
  59.1 1.0 %collective-permute-done.13.more_ref = f32[1,2048]{1,0:T(1,128)S(1)} collective-permute-done((f32[1,2048]{1,0:T(1,128)S(1)}, f32[1,2048]{1,0:T(1,128)S(1)}, u32[]{:S(2)}, u32[]{:S(2)}) %collective-permute-start.13) | collective-permute-done | bytes 8224 | tf_op jit(solution)/shard_map/ppermute | solution.py:460
  60.2 10.5 %shard_map.82.sums_ref = f32[1,2048]{1,0:T(1,128)S(1)} custom-call(f32[2048,2048]{1,0:T(8,128)S(1)} %fusion.scores_ref, f32[1,2048]{1,0:T(1,128)S(1)} %get-tuple-element.64.sums_ref, f32[1,2048]{1,0:T(1,128)S(1)} %collective-permute-done.13.more_ref, f32[1,2048]{1,0:T(1,128)S(1)} %get-tuple-element.57.log_src_ref, ...), custom_call_target="tpu_custom_call" | custom-call | tf_op jit(solution)/shard_map/pallas_call | solution.py:555
  70.7 0.2 collective-permute-start.14
  70.9 1.0 %collective-permute-done.14.more_ref = f32[1,2048]{1,0:T(1,128)S(1)} collective-permute-done((f32[1,2048]{1,0:T(1,128)S(1)}, f32[1,2048]{1,0:T(1,128)S(1)}, u32[]{:S(2)}, u32[]{:S(2)}) %collective-permute-start.14) | collective-permute-done | bytes 8224 | tf_op jit(solution)/shard_map/ppermute | solution.py:460
  71.9 2.8 %shard_map.83 = (f32[512,512]{1,0:T(8,128)}, f32[1,512]{1,0:T(1,128)}, f32[1,512]{1,0:T(1,128)}) custom-call(f32[2048,2048]{1,0:T(8,128)S(1)} %fusion.scores_ref, f32[1,2048]{1,0:T(1,128)S(1)} %shard_map.82.sums_ref, f32[1,2048]{1,0:T(1,128)S(1)} %collective-permute-done.14.more_ref, f32[1,2048]{1,0:T(1,128)S(1)} %get-tuple-element.57.log_src_ref, ...), custom_call_target="tpu_custom_call" | custom-call | tf_op jit(solution)/shard_map/pallas_call | solution.py:555
  (18 shorter events, 0.1 us)
Async XLA Ops:
  2.3 1.4 %collective-permute-start = (f32[8,512]{1,0:T(8,128)S(1)}, f32[8,512]{1,0:T(8,128)S(1)}, u32[]{:S(2)}, u32[]{:S(2)}) collective-permute-start(f32[8,512]{1,0:T(8,128)S(1)} %get-tuple-element.39), channel_id=1, source_target_pairs={{0,1},{1,0},{2,3},{3,2},{4,5},{5,4},{6,7},{7,6},{8,9},{9,8},{10,11... | collective-permute-start | bytes 49160 | tf_op jit(solution)/shard_map/ppermute | solution.py:460
  3.7 8.5 %collective-permute-start.3 = (f32[64,512]{1,0:T(8,128)S(1)}, f32[64,512]{1,0:T(8,128)S(1)}, u32[]{:S(2)}, u32[]{:S(2)}) collective-permute-start(f32[64,512]{1,0:T(8,128)S(1)} %constant_dynamic-update-slice_fusion), channel_id=1, source_target_pairs={{0,6},{1,7},{2,4},{3,5},{4,2},{5,3},{6,0},{7,1},{8,14},{9,15},{10,... | collective-permute-start | bytes 393224 | tf_op jit(solution)/shard_map/ppermute | solution.py:460
  7.5 6.6 %collective-permute-start.2 = (f32[64,512]{1,0:T(8,128)S(1)}, f32[64,512]{1,0:T(8,128)S(1)}, u32[]{:S(2)}, u32[]{:S(2)}) collective-permute-start(f32[64,512]{1,0:T(8,128)S(1)} %constant_dynamic-update-slice_fusion), channel_id=1, source_target_pairs={{0,4},{1,5},{2,6},{3,7},{4,0},{5,1},{6,2},{7,3},{8,12},{9,13},{10,... | collective-permute-start | bytes 393224 | tf_op jit(solution)/shard_map/ppermute | solution.py:460
  8.0 6.4 %collective-permute-start.1 = (f32[64,512]{1,0:T(8,128)S(1)}, f32[64,512]{1,0:T(8,128)S(1)}, u32[]{:S(2)}, u32[]{:S(2)}) collective-permute-start(f32[64,512]{1,0:T(8,128)S(1)} %constant_dynamic-update-slice_fusion), channel_id=1, source_target_pairs={{0,2},{1,3},{2,0},{3,1},{4,6},{5,7},{6,4},{7,5},{8,10},{9,11},{10,... | collective-permute-start | bytes 393224 | tf_op jit(solution)/shard_map/ppermute | solution.py:460
  8.2 6.8 %collective-permute-start.6 = (f32[56,256]{1,0:T(8,128)S(1)}, f32[56,256]{1,0:T(8,128)S(1)}, u32[]{:S(2)}, u32[]{:S(2)}) collective-permute-start(f32[56,256]{1,0:T(8,128)S(1)} %get-tuple-element.43), channel_id=1, source_target_pairs={{0,24},{8,16},{16,8},{24,0},{1,25},{9,17},{17,9},{25,1},{2,26},{10... | collective-permute-start | bytes 172040 | tf_op jit(solution)/shard_map/ppermute | solution.py:460
  12.2 5.1 %collective-permute-start.5 = (f32[56,256]{1,0:T(8,128)S(1)}, f32[56,256]{1,0:T(8,128)S(1)}, u32[]{:S(2)}, u32[]{:S(2)}) collective-permute-start(f32[56,256]{1,0:T(8,128)S(1)} %get-tuple-element.43), channel_id=1, source_target_pairs={{0,16},{8,24},{16,0},{24,8},{1,17},{9,25},{17,1},{25,9},{2,18},{10... | collective-permute-start | bytes 172040 | tf_op jit(solution)/shard_map/ppermute | solution.py:460
  12.2 5.1 %collective-permute-start.4 = (f32[56,256]{1,0:T(8,128)S(1)}, f32[56,256]{1,0:T(8,128)S(1)}, u32[]{:S(2)}, u32[]{:S(2)}) collective-permute-start(f32[56,256]{1,0:T(8,128)S(1)} %get-tuple-element.43), channel_id=1, source_target_pairs={{0,8},{8,0},{16,24},{24,16},{1,9},{9,1},{17,25},{25,17},{2,10},{10... | collective-permute-start | bytes 172040 | tf_op jit(solution)/shard_map/ppermute | solution.py:460
  17.3 4.6 %collective-permute-start.7 = (f32[224,256]{1,0:T(8,128)S(1)}, f32[224,256]{1,0:T(8,128)S(1)}, u32[]{:S(2)}, u32[]{:S(2)}) collective-permute-start(f32[224,256]{1,0:T(8,128)S(1)} %constant_dynamic-update-slice_fusion.2.near_ref), channel_id=1, source_target_pairs={{0,1},{1,0},{2,3},{3,2},{4,5},{5,4},{6,7},{7,6},{8,9},{9,8},{10,11... | collective-permute-start | bytes 688136 | tf_op jit(solution)/shard_map/ppermute | solution.py:460
  17.4 5.6 %collective-permute-start.10 = (f32[8,512]{1,0:T(8,128)S(1)}, f32[8,512]{1,0:T(8,128)S(1)}, u32[]{:S(2)}, u32[]{:S(2)}) collective-permute-start(f32[8,512]{1,0:T(8,128)S(1)} %add_add_fusion.refs_0_), channel_id=1, source_target_pairs={{0,24},{8,16},{16,8},{24,0},{1,25},{9,17},{17,9},{25,1},{2,26},{10... | collective-permute-start | bytes 49160 | tf_op jit(solution)/shard_map/ppermute | solution.py:460
  20.1 4.6 %collective-permute-start.9 = (f32[8,512]{1,0:T(8,128)S(1)}, f32[8,512]{1,0:T(8,128)S(1)}, u32[]{:S(2)}, u32[]{:S(2)}) collective-permute-start(f32[8,512]{1,0:T(8,128)S(1)} %add_add_fusion.refs_0_), channel_id=1, source_target_pairs={{0,16},{8,24},{16,0},{24,8},{1,17},{9,25},{17,1},{25,9},{2,18},{10... | collective-permute-start | bytes 49160 | tf_op jit(solution)/shard_map/ppermute | solution.py:460
  20.1 4.6 %collective-permute-start.8 = (f32[8,512]{1,0:T(8,128)S(1)}, f32[8,512]{1,0:T(8,128)S(1)}, u32[]{:S(2)}, u32[]{:S(2)}) collective-permute-start(f32[8,512]{1,0:T(8,128)S(1)} %add_add_fusion.refs_0_), channel_id=1, source_target_pairs={{0,8},{8,0},{16,24},{24,16},{1,9},{9,1},{17,25},{25,17},{2,10},{10... | collective-permute-start | bytes 49160 | tf_op jit(solution)/shard_map/ppermute | solution.py:460
  31.3 1.2 %collective-permute-start.11 = (f32[1,2048]{1,0:T(1,128)S(1)}, f32[1,2048]{1,0:T(1,128)S(1)}, u32[]{:S(2)}, u32[]{:S(2)}) collective-permute-start(f32[1,2048]{1,0:T(1,128)S(1)} %shard_map.79.sums_ref), channel_id=1, source_target_pairs={{0,1},{1,0},{2,3},{3,2},{4,5},{5,4},{6,7},{7,6},{8,9},{9,8},{10,11... | collective-permute-start | bytes 24584 | tf_op jit(solution)/shard_map/ppermute | solution.py:460
  44.5 1.2 %collective-permute-start.12 = (f32[1,2048]{1,0:T(1,128)S(1)}, f32[1,2048]{1,0:T(1,128)S(1)}, u32[]{:S(2)}, u32[]{:S(2)}) collective-permute-start(f32[1,2048]{1,0:T(1,128)S(1)} %get-tuple-element.60.sums_ref), channel_id=1, source_target_pairs={{0,1},{1,0},{2,3},{3,2},{4,5},{5,4},{6,7},{7,6},{8,9},{9,8},{10,11... | collective-permute-start | bytes 24584 | tf_op jit(solution)/shard_map/ppermute | solution.py:460
  58.9 1.2 %collective-permute-start.13 = (f32[1,2048]{1,0:T(1,128)S(1)}, f32[1,2048]{1,0:T(1,128)S(1)}, u32[]{:S(2)}, u32[]{:S(2)}) collective-permute-start(f32[1,2048]{1,0:T(1,128)S(1)} %get-tuple-element.64.sums_ref), channel_id=1, source_target_pairs={{0,1},{1,0},{2,3},{3,2},{4,5},{5,4},{6,7},{7,6},{8,9},{9,8},{10,11... | collective-permute-start | bytes 24584 | tf_op jit(solution)/shard_map/ppermute | solution.py:460
  70.7 1.2 %collective-permute-start.14 = (f32[1,2048]{1,0:T(1,128)S(1)}, f32[1,2048]{1,0:T(1,128)S(1)}, u32[]{:S(2)}, u32[]{:S(2)}) collective-permute-start(f32[1,2048]{1,0:T(1,128)S(1)} %shard_map.82.sums_ref), channel_id=1, source_target_pairs={{0,1},{1,0},{2,3},{3,2},{4,5},{5,4},{6,7},{7,6},{8,9},{9,8},{10,11... | collective-permute-start | bytes 24584 | tf_op jit(solution)/shard_map/ppermute | solution.py:460

commit v4 on v3

--- a/solution.py
+++ b/solution.py
@@ -19,6 +19,8 @@
 LN2 = math.log(2.0)
 SCORES_BYTES = 1 << 24
 LIFT = 54.0
+FAINT = 2.0**-60
+SAMPLE = 4
 SPAN = 145.0
 VMEM = pl.BlockSpec(memory_space=pltpu.VMEM)
 
@@ -211,7 +213,7 @@
             out_ref[:, lanes] = down(*state)
 
 
-def columns_exp(scores_ref, rows_ref, top_ref, sum_ref, rounded_ref, count, keep_ref):
+def columns_exp(scores_ref, rows_ref, top_ref, sum_ref, exact_ref, rounded_ref, count, keep_ref):
     tiles = lane_tiles(scores_ref)
 
     def highest(i, carry):
@@ -231,8 +233,9 @@
         places = [place for _, pair in pairs for place in pair]
         tops = [top_ref[place, :] for place in places]
         sums = [jnp.zeros((8, LANES), jnp.float32)] * 8
+        exact = [jnp.zeros((8, LANES), jnp.float32)] * 8
         rounded = [jnp.zeros((8, LANES), jnp.float32)] * 8
-        for lanes in tiles:
+        for j, lanes in enumerate(tiles):
             row = rows_ref[:, lanes]
             for g, (at, sources) in enumerate(pairs):
                 parts = [
@@ -241,13 +244,17 @@
                 ]
                 kept = jnp.concatenate(parts, axis=0).astype(keep_ref.dtype)
                 keep_ref[at, lanes] = kept
-                kept = kept.astype(jnp.float32)
                 for h in range(2):
                     sums[2 * g + h] = sums[2 * g + h] + parts[h]
-                    rounded[2 * g + h] = rounded[2 * g + h] + kept[8 * h : 8 * h + 8]
-        for place, value, other in zip(places, sums, rounded):
+                if j % SAMPLE == 0:
+                    kept = kept.astype(jnp.float32)
+                    for h in range(2):
+                        exact[2 * g + h] = exact[2 * g + h] + parts[h]
+                        rounded[2 * g + h] = rounded[2 * g + h] + kept[8 * h : 8 * h + 8]
+        for place, value, before, after in zip(places, sums, exact, rounded):
             sum_ref[place, :] = value
-            rounded_ref[place, :] = other
+            exact_ref[place, :] = before
+            rounded_ref[place, :] = after
         return carry
 
     lax.fori_loop(0, count // 64, highest, 0)
@@ -331,28 +338,29 @@
 def rows_exp(scores_ref, cols_ref, top_ref, out_ref, keep_ref, level_ref):
     def body(pairs, tiles, carry):
         tops = [top_ref[:, lanes] for lanes in tiles]
-        for at, places in pairs:
+        for g, (at, places) in enumerate(pairs):
             potentials = [cols_ref[place, :] for place in places]
             for j, lanes in enumerate(tiles):
                 terms = [scores_ref[place, lanes] + c for place, c in zip(places, potentials)]
                 parts = [jnp.exp2(term - tops[j]) for term in terms]
-                summed, rounded = carry[j]
+                summed, exact, rounded = carry[j]
+                both = parts[0] + parts[1]
                 if keep_ref is not None:
                     kept = jnp.concatenate(parts, axis=0).astype(keep_ref.dtype)
                     keep_ref[at, lanes] = kept
-                    kept = kept.astype(jnp.float32)
-                    rounded = rounded + (kept[:8] + kept[8:])
-                carry[j] = summed + (parts[0] + parts[1]), rounded
+                    if g % SAMPLE == 0:
+                        kept = kept.astype(jnp.float32)
+                        exact, rounded = exact + both, rounded + (kept[:8] + kept[8:])
+                carry[j] = summed + both, exact, rounded
 
     def done(lanes, value):
-        exact = down(top_ref[:, lanes], value[0])
-        out_ref[:, lanes] = exact
+        out_ref[:, lanes] = down(top_ref[:, lanes], value[0])
         if keep_ref is not None:
-            level = top_ref[:, lanes] + (exact - down(top_ref[:, lanes], value[1]))
-            level_ref[:, lanes] = level
+            exact, rounded = (jnp.sum(part, axis=0, keepdims=True) + FAINT for part in value[1:])
+            level_ref[:, lanes] = top_ref[:, lanes] + jnp.log2(exact / rounded)
 
     zero = jnp.zeros((8, LANES), jnp.float32)
-    over_tiles(*scores_ref.shape, body, (zero, zero), done)
+    over_tiles(*scores_ref.shape, body, (zero, zero, zero), done)
 
 
 def rows_product(keep_ref, kept_top_ref, factor, shift, out_ref):
@@ -418,15 +426,16 @@
 
 def second_kernel(scores_ref, sums_ref, more_ref, log_src_ref, log_tgt_ref, log_tgt_line_ref, *refs):
     kept, (out_ref, keep_ref, kept_top_ref, base_ref) = refs[:3], refs[3:7]
-    rows_ref, cols_ref, top_ref, sum_ref, line_ref, row_top_ref, rounded_ref = refs[7:]
+    rows_ref, cols_ref, top_ref, sum_ref, line_ref, row_top_ref, rounded_ref, exact_ref = refs[7:]
     base_ref[...] = row_values(log_src_ref, sums_ref, more_ref)
     rows_ref[...] = jnp.broadcast_to(base_ref[...], rows_ref.shape)
     count = scores_ref.shape[0]
-    columns_exp(scores_ref, rows_ref, top_ref, sum_ref, rounded_ref, count, keep_ref)
-    totals = jnp.log2(jnp.sum(sum_ref[...], axis=1, keepdims=True))
-    level = top_ref[...] + (totals - jnp.log2(jnp.sum(rounded_ref[...], axis=1, keepdims=True)))
+    columns_exp(scores_ref, rows_ref, top_ref, sum_ref, exact_ref, rounded_ref, count, keep_ref)
+    columns_finish(top_ref, sum_ref, log_tgt_ref, cols_ref, 0, count)
+    exact = jnp.sum(exact_ref[...], axis=1, keepdims=True)
+    rounded = jnp.sum(rounded_ref[...], axis=1, keepdims=True)
+    level = top_ref[...] + jnp.log2((exact + FAINT) / (rounded + FAINT))
     kept_top_ref[...] = level.T[0:1, :]
-    cols_ref[...] = log_tgt_ref[...] - marg_power * (top_ref[...] + totals)
     line_ref[...] = cols_ref[...].T[0:1, :]
     rows_either(scores_ref, line_ref, kept, cols_ref, row_top_ref, out_ref)
 
@@ -565,7 +574,7 @@
     side, columns = (1, wide), (lines, pads, pads, pads)
     sums, *kept_rows = call(first_kernel, sums, (), (line, block, lines, side), columns)
     sums, *kept_columns = call(
-        second_kernel, sums, kept_rows, (line, block, side, line), (*columns, side, lines, pads)
+        second_kernel, sums, kept_rows, (line, block, side, line), (*columns, side, lines, pads, pads)
     )
     for iteration in range(ITERS - 3):
         (sums,) = call(

time: 73.5 us -> 72.4 us (0.985)
  Pallas kernels: 45 us -> 44 us
    pallas_call x4, Pallas kernels: 38.4 us -> 37.4 us  [call(): pl.pallas_call(kernel, out_shape=tuple((jax.ShapeDtypeStruct(shape, bf16...]
where the time goes in v4:
time: 72.4 us; the launch traced here: 73.7 us
  Pallas kernels  44 us (61%)
  starting transfers between devices  15.5 us (21%)
  waiting for transfers between devices  11 us (15%)
  matrix products  2.34 us (3%)
  between operations  0.76 us (1%)
    pallas_call x4, Pallas kernels, call(): pl.pallas_call(kernel, out_shape=tuple((jax.ShapeDtypeStruct(shape, bf16...  37.4 us
    ppermute x15, starting transfers between devices, swap(): lax.ppermute(value, axis, [(i, i ^ offset) for i in range(lax.axis_size(a...  15.5 us
    ppermute x15, waiting for transfers between devices, swap(): lax.ppermute(value, axis, [(i, i ^ offset) for i in range(lax.axis_size(a...  11 us
    pallas_call x1, Pallas kernels, shards(): pl.pallas_call(rows_running, out_shape=jax.ShapeDtypeStruct((1, total_row...  3.46 us
    dot_general x1, matrix products, shards(): scores = jnp.dot(weights, src_all, preferred_element_type=f32)  2.34 us
    pallas_call x1, Pallas kernels, shards(): pl.pallas_call(front_kernel, out_shape=(pltpu.VMEM((packed_rows, rows //...  1.65 us
  transfers between devices with their start and end apart: 15, of which 11 were waited for; matrix products, arithmetic and copies ran while one was open for 0% of the time, Pallas kernels for 1%

profile of v4, /device:TPU:0, one launch (start us, length us, event | category | flops | bytes accessed | tf_op | source)
XLA Modules:
  0.0 73.7 jit_solution(9071570765691034154)
XLA Ops:
  0.6 1.6 %shard_map.76 = (f32[56,256]{1,0:T(8,128)S(1)}, f32[56,512]{1,0:T(8,128)S(1)}, f32[8,512]{1,0:T(8,128)S(1)}) custom-call(bf16[512,512]{1,0:T(8,128)(2,1)} %refs_0_.1, bf16[50,512]{1,0:T(8,128)(2,1)} %refs_1_.1, bf16[50,512]{1,0:T(8,128)(2,1)} %refs_2_.1, f32[1,512]{1,0:T(1,128)} %bitcast.6, f32[1,512]{1,0:T(1,128)} %bitcast.7), custom_call_target="tpu_custom_call" | custom-call | tf_op jit(solution)/shard_map/pallas_call | solution.py:496
  2.3 0.5 collective-permute-start
  2.8 0.8 %collective-permute-done = f32[8,512]{1,0:T(8,128)S(1)} collective-permute-done((f32[8,512]{1,0:T(8,128)S(1)}, f32[8,512]{1,0:T(8,128)S(1)}, u32[]{:S(2)}, u32[]{:S(2)}) %collective-permute-start) | collective-permute-done | bytes 16416 | tf_op jit(solution)/shard_map/ppermute | solution.py:469
  3.7 3.9 %collective-permute-start.3 = (f32[64,512]{1,0:T(8,128)S(1)}, f32[64,512]{1,0:T(8,128)S(1)}, u32[]{:S(2)}, u32[]{:S(2)}) collective-permute-start(f32[64,512]{1,0:T(8,128)S(1)} %constant_dynamic-update-slice_fusion), channel_id=1, source_target_pairs={{0,6},{1,7},{2,4},{3,5},{4,2},{5,3},{6,0},{7,1},{8,14},{9,15},{10,... | collective-permute-start | bytes 393224 | tf_op jit(solution)/shard_map/ppermute | solution.py:469
  7.5 0.5 collective-permute-start.2
  8.0 0.1 collective-permute-start.1
  8.2 4.0 %collective-permute-start.6 = (f32[56,256]{1,0:T(8,128)S(1)}, f32[56,256]{1,0:T(8,128)S(1)}, u32[]{:S(2)}, u32[]{:S(2)}) collective-permute-start(f32[56,256]{1,0:T(8,128)S(1)} %get-tuple-element.43), channel_id=1, source_target_pairs={{0,24},{8,16},{16,8},{24,0},{1,25},{9,17},{17,9},{25,1},{2,26},{10... | collective-permute-start | bytes 172040 | tf_op jit(solution)/shard_map/ppermute | solution.py:469
  12.2 1.2 %collective-permute-start.4 = (f32[56,256]{1,0:T(8,128)S(1)}, f32[56,256]{1,0:T(8,128)S(1)}, u32[]{:S(2)}, u32[]{:S(2)}) collective-permute-start(f32[56,256]{1,0:T(8,128)S(1)} %get-tuple-element.43), channel_id=1, source_target_pairs={{0,8},{8,0},{16,24},{24,16},{1,9},{9,1},{17,25},{25,17},{2,10},{10... | collective-permute-start | bytes 172040 | tf_op jit(solution)/shard_map/ppermute | solution.py:469
  13.4 0.8 %collective-permute-done.2.refs_2_ = f32[64,512]{1,0:T(8,128)S(1)} collective-permute-done((f32[64,512]{1,0:T(8,128)S(1)}, f32[64,512]{1,0:T(8,128)S(1)}, u32[]{:S(2)}, u32[]{:S(2)}) %collective-permute-start.2) | collective-permute-done | bytes 131104 | tf_op jit(solution)/shard_map/ppermute | solution.py:469
  14.2 0.3 collective-permute-done.1.refs_1_
  14.4 0.6 collective-permute-done.6
  15.0 2.2 %collective-permute-done.5 = f32[56,256]{1,0:T(8,128)S(1)} collective-permute-done((f32[56,256]{1,0:T(8,128)S(1)}, f32[56,256]{1,0:T(8,128)S(1)}, u32[]{:S(2)}, u32[]{:S(2)}) %collective-permute-start.5) | collective-permute-done | bytes 57376 | tf_op jit(solution)/shard_map/ppermute | solution.py:469
  17.3 0.1 collective-permute-start.7
  17.4 2.7 %collective-permute-start.10 = (f32[8,512]{1,0:T(8,128)S(1)}, f32[8,512]{1,0:T(8,128)S(1)}, u32[]{:S(2)}, u32[]{:S(2)}) collective-permute-start(f32[8,512]{1,0:T(8,128)S(1)} %add_add_fusion.refs_0_), channel_id=1, source_target_pairs={{0,24},{8,16},{16,8},{24,0},{1,25},{9,17},{17,9},{25,1},{2,26},{10... | collective-permute-start | bytes 49160 | tf_op jit(solution)/shard_map/ppermute | solution.py:469
  20.1 1.7 %collective-permute-start.8 = (f32[8,512]{1,0:T(8,128)S(1)}, f32[8,512]{1,0:T(8,128)S(1)}, u32[]{:S(2)}, u32[]{:S(2)}) collective-permute-start(f32[8,512]{1,0:T(8,128)S(1)} %add_add_fusion.refs_0_), channel_id=1, source_target_pairs={{0,8},{8,0},{16,24},{24,16},{1,9},{9,1},{17,25},{25,17},{2,10},{10... | collective-permute-start | bytes 49160 | tf_op jit(solution)/shard_map/ppermute | solution.py:469
  21.9 0.7 shard_map.77
  22.6 0.4 collective-permute-done.10.refs_3_
  23.0 1.7 %collective-permute-done.9.refs_2_ = f32[8,512]{1,0:T(8,128)S(1)} collective-permute-done((f32[8,512]{1,0:T(8,128)S(1)}, f32[8,512]{1,0:T(8,128)S(1)}, u32[]{:S(2)}, u32[]{:S(2)}) %collective-permute-start.9) | collective-permute-done | bytes 16416 | tf_op jit(solution)/shard_map/ppermute | solution.py:469
  24.8 0.8 %shard_map.78 = bf16[2048,256]{1,0:T(8,128)(2,1)S(1)} custom-call(bf16[2048,128]{1,0:T(8,128)(2,1)S(1)} %get-tuple-element.51.turned_ref, f32[8,512]{1,0:T(8,128)S(1)} %add_add_fusion.refs_0_, f32[8,512]{1,0:T(8,128)S(1)} %collective-permute-done.8.refs_1_, f32[8,512]{1,0:T(8,128)S(1)} %collective-permute-done.9.refs_2_, ...), custom_call_target="tpu_custom_call" | custom-call | tf_op jit(solution)/shard_map/pallas_call | solution.py:538
  25.5 2.3 %fusion.scores_ref = f32[2048,2048]{1,0:T(8,128)S(1)} fusion(bf16[2048,256]{1,0:T(8,128)(2,1)S(1)} %shard_map.78, bf16[256,2048]{1,0:T(8,128)(2,1)S(1)} %get-tuple-element.56), kind=kOutput, calls=%fused_computation.7 | convolution fusion | flops 2147483648 | bytes 18874368 | tf_op jit(solution)/shard_map/dot_general | solution.py:545
  27.9 3.5 %shard_map.79.sums_ref = f32[1,2048]{1,0:T(1,128)S(1)} custom-call(f32[2048,2048]{1,0:T(8,128)S(1)} %fusion.scores_ref), custom_call_target="tpu_custom_call" | custom-call | tf_op jit(solution)/shard_map/pallas_call | solution.py:546
  31.4 1.2 %collective-permute-done.11.more_ref = f32[1,2048]{1,0:T(1,128)S(1)} collective-permute-done((f32[1,2048]{1,0:T(1,128)S(1)}, f32[1,2048]{1,0:T(1,128)S(1)}, u32[]{:S(2)}, u32[]{:S(2)}) %collective-permute-start.11) | collective-permute-done | bytes 8224 | tf_op jit(solution)/shard_map/ppermute | solution.py:469
  32.6 11.4 %shard_map.80 = (f32[1,2048]{1,0:T(1,128)S(1)}, bf16[2048,2048]{1,0:T(8,128)(2,1)S(1)}, f32[8,2048]{1,0:T(8,128)S(1)}, f32[1,2048]{1,0:T(1,128)S(1)}) custom-call(f32[2048,2048]{1,0:T(8,128)S(1)} %fusion.scores_ref, f32[1,2048]{1,0:T(1,128)S(1)} %shard_map.79.sums_ref, f32[1,2048]{1,0:T(1,128)S(1)} %collective-permute-done.11.more_ref, ...), custom_call_target="tpu_custom_call" | custom-call | tf_op jit(solution)/shard_map/pallas_call | solution.py:564
  44.0 0.2 collective-permute-start.12
  44.2 1.0 %collective-permute-done.12.more_ref = f32[1,2048]{1,0:T(1,128)S(1)} collective-permute-done((f32[1,2048]{1,0:T(1,128)S(1)}, f32[1,2048]{1,0:T(1,128)S(1)}, u32[]{:S(2)}, u32[]{:S(2)}) %collective-permute-start.12) | collective-permute-done | bytes 8224 | tf_op jit(solution)/shard_map/ppermute | solution.py:469
  45.2 12.7 %shard_map.81 = (f32[1,2048]{1,0:T(1,128)S(1)}, bf16[2048,2048]{1,0:T(8,128)(2,1)S(1)}, f32[1,2048]{1,0:T(1,128)S(1)}, f32[1,2048]{1,0:T(1,128)S(1)}) custom-call(f32[2048,2048]{1,0:T(8,128)S(1)} %fusion.scores_ref, f32[1,2048]{1,0:T(1,128)S(1)} %get-tuple-element.60.sums_ref, f32[1,2048]{1,0:T(1,128)S(1)} %collective-permute-done.12.more_ref, ...), custom_call_target="tpu_custom_call" | custom-call | tf_op jit(solution)/shard_map/pallas_call | solution.py:564
  57.9 0.2 collective-permute-start.13
  58.1 1.0 %collective-permute-done.13.more_ref = f32[1,2048]{1,0:T(1,128)S(1)} collective-permute-done((f32[1,2048]{1,0:T(1,128)S(1)}, f32[1,2048]{1,0:T(1,128)S(1)}, u32[]{:S(2)}, u32[]{:S(2)}) %collective-permute-start.13) | collective-permute-done | bytes 8224 | tf_op jit(solution)/shard_map/ppermute | solution.py:469
  59.1 10.5 %shard_map.82.sums_ref = f32[1,2048]{1,0:T(1,128)S(1)} custom-call(f32[2048,2048]{1,0:T(8,128)S(1)} %fusion.scores_ref, f32[1,2048]{1,0:T(1,128)S(1)} %get-tuple-element.64.sums_ref, f32[1,2048]{1,0:T(1,128)S(1)} %collective-permute-done.13.more_ref, f32[1,2048]{1,0:T(1,128)S(1)} %get-tuple-element.57.log_src_ref, ...), custom_call_target="tpu_custom_call" | custom-call | tf_op jit(solution)/shard_map/pallas_call | solution.py:564
  69.6 0.2 collective-permute-start.14
  69.9 1.0 %collective-permute-done.14.more_ref = f32[1,2048]{1,0:T(1,128)S(1)} collective-permute-done((f32[1,2048]{1,0:T(1,128)S(1)}, f32[1,2048]{1,0:T(1,128)S(1)}, u32[]{:S(2)}, u32[]{:S(2)}) %collective-permute-start.14) | collective-permute-done | bytes 8224 | tf_op jit(solution)/shard_map/ppermute | solution.py:469
  70.9 2.8 %shard_map.83 = (f32[512,512]{1,0:T(8,128)}, f32[1,512]{1,0:T(1,128)}, f32[1,512]{1,0:T(1,128)}) custom-call(f32[2048,2048]{1,0:T(8,128)S(1)} %fusion.scores_ref, f32[1,2048]{1,0:T(1,128)S(1)} %shard_map.82.sums_ref, f32[1,2048]{1,0:T(1,128)S(1)} %collective-permute-done.14.more_ref, f32[1,2048]{1,0:T(1,128)S(1)} %get-tuple-element.57.log_src_ref, ...), custom_call_target="tpu_custom_call" | custom-call | tf_op jit(solution)/shard_map/pallas_call | solution.py:564
  (18 shorter events, 0.1 us)
Async XLA Ops:
  2.3 1.4 %collective-permute-start = (f32[8,512]{1,0:T(8,128)S(1)}, f32[8,512]{1,0:T(8,128)S(1)}, u32[]{:S(2)}, u32[]{:S(2)}) collective-permute-start(f32[8,512]{1,0:T(8,128)S(1)} %get-tuple-element.39), channel_id=1, source_target_pairs={{0,1},{1,0},{2,3},{3,2},{4,5},{5,4},{6,7},{7,6},{8,9},{9,8},{10,11... | collective-permute-start | bytes 49160 | tf_op jit(solution)/shard_map/ppermute | solution.py:469
  3.7 8.5 %collective-permute-start.3 = (f32[64,512]{1,0:T(8,128)S(1)}, f32[64,512]{1,0:T(8,128)S(1)}, u32[]{:S(2)}, u32[]{:S(2)}) collective-permute-start(f32[64,512]{1,0:T(8,128)S(1)} %constant_dynamic-update-slice_fusion), channel_id=1, source_target_pairs={{0,6},{1,7},{2,4},{3,5},{4,2},{5,3},{6,0},{7,1},{8,14},{9,15},{10,... | collective-permute-start | bytes 393224 | tf_op jit(solution)/shard_map/ppermute | solution.py:469
  7.5 6.6 %collective-permute-start.2 = (f32[64,512]{1,0:T(8,128)S(1)}, f32[64,512]{1,0:T(8,128)S(1)}, u32[]{:S(2)}, u32[]{:S(2)}) collective-permute-start(f32[64,512]{1,0:T(8,128)S(1)} %constant_dynamic-update-slice_fusion), channel_id=1, source_target_pairs={{0,4},{1,5},{2,6},{3,7},{4,0},{5,1},{6,2},{7,3},{8,12},{9,13},{10,... | collective-permute-start | bytes 393224 | tf_op jit(solution)/shard_map/ppermute | solution.py:469
  8.0 6.4 %collective-permute-start.1 = (f32[64,512]{1,0:T(8,128)S(1)}, f32[64,512]{1,0:T(8,128)S(1)}, u32[]{:S(2)}, u32[]{:S(2)}) collective-permute-start(f32[64,512]{1,0:T(8,128)S(1)} %constant_dynamic-update-slice_fusion), channel_id=1, source_target_pairs={{0,2},{1,3},{2,0},{3,1},{4,6},{5,7},{6,4},{7,5},{8,10},{9,11},{10,... | collective-permute-start | bytes 393224 | tf_op jit(solution)/shard_map/ppermute | solution.py:469
  8.2 6.8 %collective-permute-start.6 = (f32[56,256]{1,0:T(8,128)S(1)}, f32[56,256]{1,0:T(8,128)S(1)}, u32[]{:S(2)}, u32[]{:S(2)}) collective-permute-start(f32[56,256]{1,0:T(8,128)S(1)} %get-tuple-element.43), channel_id=1, source_target_pairs={{0,24},{8,16},{16,8},{24,0},{1,25},{9,17},{17,9},{25,1},{2,26},{10... | collective-permute-start | bytes 172040 | tf_op jit(solution)/shard_map/ppermute | solution.py:469
  12.2 5.1 %collective-permute-start.5 = (f32[56,256]{1,0:T(8,128)S(1)}, f32[56,256]{1,0:T(8,128)S(1)}, u32[]{:S(2)}, u32[]{:S(2)}) collective-permute-start(f32[56,256]{1,0:T(8,128)S(1)} %get-tuple-element.43), channel_id=1, source_target_pairs={{0,16},{8,24},{16,0},{24,8},{1,17},{9,25},{17,1},{25,9},{2,18},{10... | collective-permute-start | bytes 172040 | tf_op jit(solution)/shard_map/ppermute | solution.py:469
  12.2 5.1 %collective-permute-start.4 = (f32[56,256]{1,0:T(8,128)S(1)}, f32[56,256]{1,0:T(8,128)S(1)}, u32[]{:S(2)}, u32[]{:S(2)}) collective-permute-start(f32[56,256]{1,0:T(8,128)S(1)} %get-tuple-element.43), channel_id=1, source_target_pairs={{0,8},{8,0},{16,24},{24,16},{1,9},{9,1},{17,25},{25,17},{2,10},{10... | collective-permute-start | bytes 172040 | tf_op jit(solution)/shard_map/ppermute | solution.py:469
  17.3 4.6 %collective-permute-start.7 = (f32[224,256]{1,0:T(8,128)S(1)}, f32[224,256]{1,0:T(8,128)S(1)}, u32[]{:S(2)}, u32[]{:S(2)}) collective-permute-start(f32[224,256]{1,0:T(8,128)S(1)} %constant_dynamic-update-slice_fusion.2.near_ref), channel_id=1, source_target_pairs={{0,1},{1,0},{2,3},{3,2},{4,5},{5,4},{6,7},{7,6},{8,9},{9,8},{10,11... | collective-permute-start | bytes 688136 | tf_op jit(solution)/shard_map/ppermute | solution.py:469
  17.4 5.6 %collective-permute-start.10 = (f32[8,512]{1,0:T(8,128)S(1)}, f32[8,512]{1,0:T(8,128)S(1)}, u32[]{:S(2)}, u32[]{:S(2)}) collective-permute-start(f32[8,512]{1,0:T(8,128)S(1)} %add_add_fusion.refs_0_), channel_id=1, source_target_pairs={{0,24},{8,16},{16,8},{24,0},{1,25},{9,17},{17,9},{25,1},{2,26},{10... | collective-permute-start | bytes 49160 | tf_op jit(solution)/shard_map/ppermute | solution.py:469
  20.1 4.6 %collective-permute-start.9 = (f32[8,512]{1,0:T(8,128)S(1)}, f32[8,512]{1,0:T(8,128)S(1)}, u32[]{:S(2)}, u32[]{:S(2)}) collective-permute-start(f32[8,512]{1,0:T(8,128)S(1)} %add_add_fusion.refs_0_), channel_id=1, source_target_pairs={{0,16},{8,24},{16,0},{24,8},{1,17},{9,25},{17,1},{25,9},{2,18},{10... | collective-permute-start | bytes 49160 | tf_op jit(solution)/shard_map/ppermute | solution.py:469
  20.1 4.6 %collective-permute-start.8 = (f32[8,512]{1,0:T(8,128)S(1)}, f32[8,512]{1,0:T(8,128)S(1)}, u32[]{:S(2)}, u32[]{:S(2)}) collective-permute-start(f32[8,512]{1,0:T(8,128)S(1)} %add_add_fusion.refs_0_), channel_id=1, source_target_pairs={{0,8},{8,0},{16,24},{24,16},{1,9},{9,1},{17,25},{25,17},{2,10},{10... | collective-permute-start | bytes 49160 | tf_op jit(solution)/shard_map/ppermute | solution.py:469
  31.3 1.2 %collective-permute-start.11 = (f32[1,2048]{1,0:T(1,128)S(1)}, f32[1,2048]{1,0:T(1,128)S(1)}, u32[]{:S(2)}, u32[]{:S(2)}) collective-permute-start(f32[1,2048]{1,0:T(1,128)S(1)} %shard_map.79.sums_ref), channel_id=1, source_target_pairs={{0,1},{1,0},{2,3},{3,2},{4,5},{5,4},{6,7},{7,6},{8,9},{9,8},{10,11... | collective-permute-start | bytes 24584 | tf_op jit(solution)/shard_map/ppermute | solution.py:469
  44.0 1.2 %collective-permute-start.12 = (f32[1,2048]{1,0:T(1,128)S(1)}, f32[1,2048]{1,0:T(1,128)S(1)}, u32[]{:S(2)}, u32[]{:S(2)}) collective-permute-start(f32[1,2048]{1,0:T(1,128)S(1)} %get-tuple-element.60.sums_ref), channel_id=1, source_target_pairs={{0,1},{1,0},{2,3},{3,2},{4,5},{5,4},{6,7},{7,6},{8,9},{9,8},{10,11... | collective-permute-start | bytes 24584 | tf_op jit(solution)/shard_map/ppermute | solution.py:469
  57.9 1.2 %collective-permute-start.13 = (f32[1,2048]{1,0:T(1,128)S(1)}, f32[1,2048]{1,0:T(1,128)S(1)}, u32[]{:S(2)}, u32[]{:S(2)}) collective-permute-start(f32[1,2048]{1,0:T(1,128)S(1)} %get-tuple-element.64.sums_ref), channel_id=1, source_target_pairs={{0,1},{1,0},{2,3},{3,2},{4,5},{5,4},{6,7},{7,6},{8,9},{9,8},{10,11... | collective-permute-start | bytes 24584 | tf_op jit(solution)/shard_map/ppermute | solution.py:469
  69.6 1.2 %collective-permute-start.14 = (f32[1,2048]{1,0:T(1,128)S(1)}, f32[1,2048]{1,0:T(1,128)S(1)}, u32[]{:S(2)}, u32[]{:S(2)}) collective-permute-start(f32[1,2048]{1,0:T(1,128)S(1)} %shard_map.82.sums_ref), channel_id=1, source_target_pairs={{0,1},{1,0},{2,3},{3,2},{4,5},{5,4},{6,7},{7,6},{8,9},{9,8},{10,11... | collective-permute-start | bytes 24584 | tf_op jit(solution)/shard_map/ppermute | solution.py:469

commit v5 on v1

--- a/solution.py
+++ b/solution.py
@@ -289,7 +289,7 @@
         cols_ref[here, :] = log_tgt_ref[at, :] - marg_power * (top + jnp.log2(total))
 
 
-BESIDE, DEEP = 8, 4
+BESIDE, DEEP = 4, 8
 
 
 def over_tiles(count, width, body, first, done):

time: 69.3 us -> 69.4 us (level)
  no operation moved by 1% of the time
where the time goes in v5:
time: 69.4 us; the launch traced here: 68.9 us
  Pallas kernels  39.2 us (56%)
  starting transfers between devices  15.5 us (22%)
  waiting for transfers between devices  11 us (16%)
  matrix products  2.34 us (3%)
  between operations  0.76 us (1%)
    pallas_call x4, Pallas kernels, call(): pl.pallas_call(kernel, out_shape=tuple((jax.ShapeDtypeStruct(shape, bf16...  32.6 us
    ppermute x15, starting transfers between devices, swap(): lax.ppermute(value, axis, [(i, i ^ offset) for i in range(lax.axis_size(a...  15.5 us
    ppermute x15, waiting for transfers between devices, swap(): lax.ppermute(value, axis, [(i, i ^ offset) for i in range(lax.axis_size(a...  11 us
    pallas_call x1, Pallas kernels, shards(): pl.pallas_call(rows_running, out_shape=jax.ShapeDtypeStruct((1, total_row...  3.46 us
    dot_general x1, matrix products, shards(): scores = jnp.dot(weights, src_all, preferred_element_type=f32)  2.34 us
    pallas_call x1, Pallas kernels, shards(): pl.pallas_call(front_kernel, out_shape=(pltpu.VMEM((packed_rows, rows //...  1.65 us
  transfers between devices with their start and end apart: 15, of which 11 were waited for; matrix products, arithmetic and copies ran while one was open for 0% of the time, Pallas kernels for 1%

profile of v5, /device:TPU:0, one launch (start us, length us, event | category | flops | bytes accessed | tf_op | source)
XLA Modules:
  0.0 68.9 jit_solution(15573918142221988779)
XLA Ops:
  0.6 1.6 %shard_map.76 = (f32[56,256]{1,0:T(8,128)S(1)}, f32[56,512]{1,0:T(8,128)S(1)}, f32[8,512]{1,0:T(8,128)S(1)}) custom-call(bf16[512,512]{1,0:T(8,128)(2,1)} %refs_0_.1, bf16[50,512]{1,0:T(8,128)(2,1)} %refs_1_.1, bf16[50,512]{1,0:T(8,128)(2,1)} %refs_2_.1, f32[1,512]{1,0:T(1,128)} %bitcast.6, f32[1,512]{1,0:T(1,128)} %bitcast.7), custom_call_target="tpu_custom_call" | custom-call | tf_op jit(solution)/shard_map/pallas_call | solution.py:475
  2.3 0.5 collective-permute-start
  2.8 0.8 %collective-permute-done = f32[8,512]{1,0:T(8,128)S(1)} collective-permute-done((f32[8,512]{1,0:T(8,128)S(1)}, f32[8,512]{1,0:T(8,128)S(1)}, u32[]{:S(2)}, u32[]{:S(2)}) %collective-permute-start) | collective-permute-done | bytes 16416 | tf_op jit(solution)/shard_map/ppermute | solution.py:448
  3.7 3.9 %collective-permute-start.3 = (f32[64,512]{1,0:T(8,128)S(1)}, f32[64,512]{1,0:T(8,128)S(1)}, u32[]{:S(2)}, u32[]{:S(2)}) collective-permute-start(f32[64,512]{1,0:T(8,128)S(1)} %constant_dynamic-update-slice_fusion), channel_id=1, source_target_pairs={{0,6},{1,7},{2,4},{3,5},{4,2},{5,3},{6,0},{7,1},{8,14},{9,15},{10,... | collective-permute-start | bytes 393224 | tf_op jit(solution)/shard_map/ppermute | solution.py:448
  7.5 0.5 collective-permute-start.2
  8.0 0.1 collective-permute-start.1
  8.2 4.0 %collective-permute-start.6 = (f32[56,256]{1,0:T(8,128)S(1)}, f32[56,256]{1,0:T(8,128)S(1)}, u32[]{:S(2)}, u32[]{:S(2)}) collective-permute-start(f32[56,256]{1,0:T(8,128)S(1)} %get-tuple-element.43), channel_id=1, source_target_pairs={{0,24},{8,16},{16,8},{24,0},{1,25},{9,17},{17,9},{25,1},{2,26},{10... | collective-permute-start | bytes 172040 | tf_op jit(solution)/shard_map/ppermute | solution.py:448
  12.2 1.2 %collective-permute-start.4 = (f32[56,256]{1,0:T(8,128)S(1)}, f32[56,256]{1,0:T(8,128)S(1)}, u32[]{:S(2)}, u32[]{:S(2)}) collective-permute-start(f32[56,256]{1,0:T(8,128)S(1)} %get-tuple-element.43), channel_id=1, source_target_pairs={{0,8},{8,0},{16,24},{24,16},{1,9},{9,1},{17,25},{25,17},{2,10},{10... | collective-permute-start | bytes 172040 | tf_op jit(solution)/shard_map/ppermute | solution.py:448
  13.4 0.8 %collective-permute-done.2.refs_2_ = f32[64,512]{1,0:T(8,128)S(1)} collective-permute-done((f32[64,512]{1,0:T(8,128)S(1)}, f32[64,512]{1,0:T(8,128)S(1)}, u32[]{:S(2)}, u32[]{:S(2)}) %collective-permute-start.2) | collective-permute-done | bytes 131104 | tf_op jit(solution)/shard_map/ppermute | solution.py:448
  14.2 0.3 collective-permute-done.1.refs_1_
  14.4 0.6 collective-permute-done.6
  15.0 2.2 %collective-permute-done.5 = f32[56,256]{1,0:T(8,128)S(1)} collective-permute-done((f32[56,256]{1,0:T(8,128)S(1)}, f32[56,256]{1,0:T(8,128)S(1)}, u32[]{:S(2)}, u32[]{:S(2)}) %collective-permute-start.5) | collective-permute-done | bytes 57376 | tf_op jit(solution)/shard_map/ppermute | solution.py:448
  17.3 0.1 collective-permute-start.7
  17.4 2.7 %collective-permute-start.10 = (f32[8,512]{1,0:T(8,128)S(1)}, f32[8,512]{1,0:T(8,128)S(1)}, u32[]{:S(2)}, u32[]{:S(2)}) collective-permute-start(f32[8,512]{1,0:T(8,128)S(1)} %add_add_fusion.refs_0_), channel_id=1, source_target_pairs={{0,24},{8,16},{16,8},{24,0},{1,25},{9,17},{17,9},{25,1},{2,26},{10... | collective-permute-start | bytes 49160 | tf_op jit(solution)/shard_map/ppermute | solution.py:448
  20.1 1.7 %collective-permute-start.8 = (f32[8,512]{1,0:T(8,128)S(1)}, f32[8,512]{1,0:T(8,128)S(1)}, u32[]{:S(2)}, u32[]{:S(2)}) collective-permute-start(f32[8,512]{1,0:T(8,128)S(1)} %add_add_fusion.refs_0_), channel_id=1, source_target_pairs={{0,8},{8,0},{16,24},{24,16},{1,9},{9,1},{17,25},{25,17},{2,10},{10... | collective-permute-start | bytes 49160 | tf_op jit(solution)/shard_map/ppermute | solution.py:448
  21.9 0.7 %shard_map.77 = (bf16[256,2048]{1,0:T(8,128)(2,1)S(1)}, bf16[2048,128]{1,0:T(8,128)(2,1)S(1)}, f32[1,2048]{1,0:T(1,128)S(1)}, f32[2048,128]{1,0:T(8,128)S(1)}, f32[1,2048]{1,0:T(1,128)S(1)}) custom-call(f32[224,256]{1,0:T(8,128)S(1)} %constant_dynamic-update-slice_fusion.2.near_ref, f32[224,256]{1,0:T(8,128)S(1)} %collective-permute-done.7.far_ref, ...), custom_call_target="tpu_custom_call" | custom-call | tf_op jit(solution)/shard_map/pallas_call | solution.py:504
  22.6 0.4 collective-permute-done.10.refs_3_
  23.0 1.7 %collective-permute-done.9.refs_2_ = f32[8,512]{1,0:T(8,128)S(1)} collective-permute-done((f32[8,512]{1,0:T(8,128)S(1)}, f32[8,512]{1,0:T(8,128)S(1)}, u32[]{:S(2)}, u32[]{:S(2)}) %collective-permute-start.9) | collective-permute-done | bytes 16416 | tf_op jit(solution)/shard_map/ppermute | solution.py:448
  24.8 0.8 %shard_map.78 = bf16[2048,256]{1,0:T(8,128)(2,1)S(1)} custom-call(bf16[2048,128]{1,0:T(8,128)(2,1)S(1)} %get-tuple-element.51.turned_ref, f32[8,512]{1,0:T(8,128)S(1)} %add_add_fusion.refs_0_, f32[8,512]{1,0:T(8,128)S(1)} %collective-permute-done.8.refs_1_, f32[8,512]{1,0:T(8,128)S(1)} %collective-permute-done.9.refs_2_, ...), custom_call_target="tpu_custom_call" | custom-call | tf_op jit(solution)/shard_map/pallas_call | solution.py:517
  25.5 2.3 %fusion.scores_ref = f32[2048,2048]{1,0:T(8,128)S(1)} fusion(bf16[2048,256]{1,0:T(8,128)(2,1)S(1)} %shard_map.78, bf16[256,2048]{1,0:T(8,128)(2,1)S(1)} %get-tuple-element.56), kind=kOutput, calls=%fused_computation.7 | convolution fusion | flops 2147483648 | bytes 18874368 | tf_op jit(solution)/shard_map/dot_general | solution.py:524
  27.9 3.5 %shard_map.79.sums_ref = f32[1,2048]{1,0:T(1,128)S(1)} custom-call(f32[2048,2048]{1,0:T(8,128)S(1)} %fusion.scores_ref), custom_call_target="tpu_custom_call" | custom-call | tf_op jit(solution)/shard_map/pallas_call | solution.py:525
  31.4 1.2 %collective-permute-done.11.more_ref = f32[1,2048]{1,0:T(1,128)S(1)} collective-permute-done((f32[1,2048]{1,0:T(1,128)S(1)}, f32[1,2048]{1,0:T(1,128)S(1)}, u32[]{:S(2)}, u32[]{:S(2)}) %collective-permute-start.11) | collective-permute-done | bytes 8224 | tf_op jit(solution)/shard_map/ppermute | solution.py:448
  32.6 10.4 %shard_map.80 = (f32[1,2048]{1,0:T(1,128)S(1)}, bf16[2048,2048]{1,0:T(8,128)(2,1)S(1)}, f32[8,2048]{1,0:T(8,128)S(1)}, f32[1,2048]{1,0:T(1,128)S(1)}) custom-call(f32[2048,2048]{1,0:T(8,128)S(1)} %fusion.scores_ref, f32[1,2048]{1,0:T(1,128)S(1)} %shard_map.79.sums_ref, f32[1,2048]{1,0:T(1,128)S(1)} %collective-permute-done.11.more_ref, ...), custom_call_target="tpu_custom_call" | custom-call | tf_op jit(solution)/shard_map/pallas_call | solution.py:543
  43.0 0.2 collective-permute-start.12
  43.2 1.0 %collective-permute-done.12.more_ref = f32[1,2048]{1,0:T(1,128)S(1)} collective-permute-done((f32[1,2048]{1,0:T(1,128)S(1)}, f32[1,2048]{1,0:T(1,128)S(1)}, u32[]{:S(2)}, u32[]{:S(2)}) %collective-permute-start.12) | collective-permute-done | bytes 8224 | tf_op jit(solution)/shard_map/ppermute | solution.py:448
  44.3 12.1 %shard_map.81 = (f32[1,2048]{1,0:T(1,128)S(1)}, bf16[2048,2048]{1,0:T(8,128)(2,1)S(1)}, f32[1,2048]{1,0:T(1,128)S(1)}, f32[1,2048]{1,0:T(1,128)S(1)}) custom-call(f32[2048,2048]{1,0:T(8,128)S(1)} %fusion.scores_ref, f32[1,2048]{1,0:T(1,128)S(1)} %get-tuple-element.60.sums_ref, f32[1,2048]{1,0:T(1,128)S(1)} %collective-permute-done.12.more_ref, ...), custom_call_target="tpu_custom_call" | custom-call | tf_op jit(solution)/shard_map/pallas_call | solution.py:543
  56.3 0.2 collective-permute-start.13
  56.6 1.0 %collective-permute-done.13.more_ref = f32[1,2048]{1,0:T(1,128)S(1)} collective-permute-done((f32[1,2048]{1,0:T(1,128)S(1)}, f32[1,2048]{1,0:T(1,128)S(1)}, u32[]{:S(2)}, u32[]{:S(2)}) %collective-permute-start.13) | collective-permute-done | bytes 8224 | tf_op jit(solution)/shard_map/ppermute | solution.py:448
  57.6 7.9 %shard_map.82.sums_ref = f32[1,2048]{1,0:T(1,128)S(1)} custom-call(f32[2048,2048]{1,0:T(8,128)S(1)} %fusion.scores_ref, f32[1,2048]{1,0:T(1,128)S(1)} %get-tuple-element.64.sums_ref, f32[1,2048]{1,0:T(1,128)S(1)} %collective-permute-done.13.more_ref, f32[1,2048]{1,0:T(1,128)S(1)} %get-tuple-element.57.log_src_ref, ...), custom_call_target="tpu_custom_call" | custom-call | tf_op jit(solution)/shard_map/pallas_call | solution.py:543
  65.5 0.2 collective-permute-start.14
  65.8 1.0 %collective-permute-done.14.more_ref = f32[1,2048]{1,0:T(1,128)S(1)} collective-permute-done((f32[1,2048]{1,0:T(1,128)S(1)}, f32[1,2048]{1,0:T(1,128)S(1)}, u32[]{:S(2)}, u32[]{:S(2)}) %collective-permute-start.14) | collective-permute-done | bytes 8224 | tf_op jit(solution)/shard_map/ppermute | solution.py:448
  66.8 2.1 %shard_map.83 = (f32[512,512]{1,0:T(8,128)}, f32[1,512]{1,0:T(1,128)}, f32[1,512]{1,0:T(1,128)}) custom-call(f32[2048,2048]{1,0:T(8,128)S(1)} %fusion.scores_ref, f32[1,2048]{1,0:T(1,128)S(1)} %shard_map.82.sums_ref, f32[1,2048]{1,0:T(1,128)S(1)} %collective-permute-done.14.more_ref, f32[1,2048]{1,0:T(1,128)S(1)} %get-tuple-element.57.log_src_ref, ...), custom_call_target="tpu_custom_call" | custom-call | tf_op jit(solution)/shard_map/pallas_call | solution.py:543
  (18 shorter events, 0.1 us)
Async XLA Ops:
  2.3 1.4 %collective-permute-start = (f32[8,512]{1,0:T(8,128)S(1)}, f32[8,512]{1,0:T(8,128)S(1)}, u32[]{:S(2)}, u32[]{:S(2)}) collective-permute-start(f32[8,512]{1,0:T(8,128)S(1)} %get-tuple-element.39), channel_id=1, source_target_pairs={{0,1},{1,0},{2,3},{3,2},{4,5},{5,4},{6,7},{7,6},{8,9},{9,8},{10,11... | collective-permute-start | bytes 49160 | tf_op jit(solution)/shard_map/ppermute | solution.py:448
  3.7 8.5 %collective-permute-start.3 = (f32[64,512]{1,0:T(8,128)S(1)}, f32[64,512]{1,0:T(8,128)S(1)}, u32[]{:S(2)}, u32[]{:S(2)}) collective-permute-start(f32[64,512]{1,0:T(8,128)S(1)} %constant_dynamic-update-slice_fusion), channel_id=1, source_target_pairs={{0,6},{1,7},{2,4},{3,5},{4,2},{5,3},{6,0},{7,1},{8,14},{9,15},{10,... | collective-permute-start | bytes 393224 | tf_op jit(solution)/shard_map/ppermute | solution.py:448
  7.5 6.6 %collective-permute-start.2 = (f32[64,512]{1,0:T(8,128)S(1)}, f32[64,512]{1,0:T(8,128)S(1)}, u32[]{:S(2)}, u32[]{:S(2)}) collective-permute-start(f32[64,512]{1,0:T(8,128)S(1)} %constant_dynamic-update-slice_fusion), channel_id=1, source_target_pairs={{0,4},{1,5},{2,6},{3,7},{4,0},{5,1},{6,2},{7,3},{8,12},{9,13},{10,... | collective-permute-start | bytes 393224 | tf_op jit(solution)/shard_map/ppermute | solution.py:448
  8.0 6.4 %collective-permute-start.1 = (f32[64,512]{1,0:T(8,128)S(1)}, f32[64,512]{1,0:T(8,128)S(1)}, u32[]{:S(2)}, u32[]{:S(2)}) collective-permute-start(f32[64,512]{1,0:T(8,128)S(1)} %constant_dynamic-update-slice_fusion), channel_id=1, source_target_pairs={{0,2},{1,3},{2,0},{3,1},{4,6},{5,7},{6,4},{7,5},{8,10},{9,11},{10,... | collective-permute-start | bytes 393224 | tf_op jit(solution)/shard_map/ppermute | solution.py:448
  8.2 6.8 %collective-permute-start.6 = (f32[56,256]{1,0:T(8,128)S(1)}, f32[56,256]{1,0:T(8,128)S(1)}, u32[]{:S(2)}, u32[]{:S(2)}) collective-permute-start(f32[56,256]{1,0:T(8,128)S(1)} %get-tuple-element.43), channel_id=1, source_target_pairs={{0,24},{8,16},{16,8},{24,0},{1,25},{9,17},{17,9},{25,1},{2,26},{10... | collective-permute-start | bytes 172040 | tf_op jit(solution)/shard_map/ppermute | solution.py:448
  12.2 5.1 %collective-permute-start.5 = (f32[56,256]{1,0:T(8,128)S(1)}, f32[56,256]{1,0:T(8,128)S(1)}, u32[]{:S(2)}, u32[]{:S(2)}) collective-permute-start(f32[56,256]{1,0:T(8,128)S(1)} %get-tuple-element.43), channel_id=1, source_target_pairs={{0,16},{8,24},{16,0},{24,8},{1,17},{9,25},{17,1},{25,9},{2,18},{10... | collective-permute-start | bytes 172040 | tf_op jit(solution)/shard_map/ppermute | solution.py:448
  12.2 5.1 %collective-permute-start.4 = (f32[56,256]{1,0:T(8,128)S(1)}, f32[56,256]{1,0:T(8,128)S(1)}, u32[]{:S(2)}, u32[]{:S(2)}) collective-permute-start(f32[56,256]{1,0:T(8,128)S(1)} %get-tuple-element.43), channel_id=1, source_target_pairs={{0,8},{8,0},{16,24},{24,16},{1,9},{9,1},{17,25},{25,17},{2,10},{10... | collective-permute-start | bytes 172040 | tf_op jit(solution)/shard_map/ppermute | solution.py:448
  17.3 4.6 %collective-permute-start.7 = (f32[224,256]{1,0:T(8,128)S(1)}, f32[224,256]{1,0:T(8,128)S(1)}, u32[]{:S(2)}, u32[]{:S(2)}) collective-permute-start(f32[224,256]{1,0:T(8,128)S(1)} %constant_dynamic-update-slice_fusion.2.near_ref), channel_id=1, source_target_pairs={{0,1},{1,0},{2,3},{3,2},{4,5},{5,4},{6,7},{7,6},{8,9},{9,8},{10,11... | collective-permute-start | bytes 688136 | tf_op jit(solution)/shard_map/ppermute | solution.py:448
  17.4 5.6 %collective-permute-start.10 = (f32[8,512]{1,0:T(8,128)S(1)}, f32[8,512]{1,0:T(8,128)S(1)}, u32[]{:S(2)}, u32[]{:S(2)}) collective-permute-start(f32[8,512]{1,0:T(8,128)S(1)} %add_add_fusion.refs_0_), channel_id=1, source_target_pairs={{0,24},{8,16},{16,8},{24,0},{1,25},{9,17},{17,9},{25,1},{2,26},{10... | collective-permute-start | bytes 49160 | tf_op jit(solution)/shard_map/ppermute | solution.py:448
  20.1 4.6 %collective-permute-start.9 = (f32[8,512]{1,0:T(8,128)S(1)}, f32[8,512]{1,0:T(8,128)S(1)}, u32[]{:S(2)}, u32[]{:S(2)}) collective-permute-start(f32[8,512]{1,0:T(8,128)S(1)} %add_add_fusion.refs_0_), channel_id=1, source_target_pairs={{0,16},{8,24},{16,0},{24,8},{1,17},{9,25},{17,1},{25,9},{2,18},{10... | collective-permute-start | bytes 49160 | tf_op jit(solution)/shard_map/ppermute | solution.py:448
  20.1 4.6 %collective-permute-start.8 = (f32[8,512]{1,0:T(8,128)S(1)}, f32[8,512]{1,0:T(8,128)S(1)}, u32[]{:S(2)}, u32[]{:S(2)}) collective-permute-start(f32[8,512]{1,0:T(8,128)S(1)} %add_add_fusion.refs_0_), channel_id=1, source_target_pairs={{0,8},{8,0},{16,24},{24,16},{1,9},{9,1},{17,25},{25,17},{2,10},{10... | collective-permute-start | bytes 49160 | tf_op jit(solution)/shard_map/ppermute | solution.py:448
  31.3 1.2 %collective-permute-start.11 = (f32[1,2048]{1,0:T(1,128)S(1)}, f32[1,2048]{1,0:T(1,128)S(1)}, u32[]{:S(2)}, u32[]{:S(2)}) collective-permute-start(f32[1,2048]{1,0:T(1,128)S(1)} %shard_map.79.sums_ref), channel_id=1, source_target_pairs={{0,1},{1,0},{2,3},{3,2},{4,5},{5,4},{6,7},{7,6},{8,9},{9,8},{10,11... | collective-permute-start | bytes 24584 | tf_op jit(solution)/shard_map/ppermute | solution.py:448
  43.0 1.2 %collective-permute-start.12 = (f32[1,2048]{1,0:T(1,128)S(1)}, f32[1,2048]{1,0:T(1,128)S(1)}, u32[]{:S(2)}, u32[]{:S(2)}) collective-permute-start(f32[1,2048]{1,0:T(1,128)S(1)} %get-tuple-element.60.sums_ref), channel_id=1, source_target_pairs={{0,1},{1,0},{2,3},{3,2},{4,5},{5,4},{6,7},{7,6},{8,9},{9,8},{10,11... | collective-permute-start | bytes 24584 | tf_op jit(solution)/shard_map/ppermute | solution.py:448
  56.3 1.2 %collective-permute-start.13 = (f32[1,2048]{1,0:T(1,128)S(1)}, f32[1,2048]{1,0:T(1,128)S(1)}, u32[]{:S(2)}, u32[]{:S(2)}) collective-permute-start(f32[1,2048]{1,0:T(1,128)S(1)} %get-tuple-element.64.sums_ref), channel_id=1, source_target_pairs={{0,1},{1,0},{2,3},{3,2},{4,5},{5,4},{6,7},{7,6},{8,9},{9,8},{10,11... | collective-permute-start | bytes 24584 | tf_op jit(solution)/shard_map/ppermute | solution.py:448
  65.5 1.2 %collective-permute-start.14 = (f32[1,2048]{1,0:T(1,128)S(1)}, f32[1,2048]{1,0:T(1,128)S(1)}, u32[]{:S(2)}, u32[]{:S(2)}) collective-permute-start(f32[1,2048]{1,0:T(1,128)S(1)} %shard_map.82.sums_ref), channel_id=1, source_target_pairs={{0,1},{1,0},{2,3},{3,2},{4,5},{5,4},{6,7},{7,6},{8,9},{9,8},{10,11... | collective-permute-start | bytes 24584 | tf_op jit(solution)/shard_map/ppermute | solution.py:448

commit v6 on v1

--- a/solution.py
+++ b/solution.py
@@ -172,7 +172,7 @@
 
 def columns_running(scores_ref, rows_ref, top_ref, sum_ref, base, count):
     tiles = lane_tiles(scores_ref)
-    span = min(16, len(tiles))
+    span = min(8, len(tiles))
 
     def scan(i, carry):
         for u in range(4):
@@ -194,7 +194,7 @@
 
 def rows_running(scores_ref, out_ref):
     count, total = scores_ref.shape
-    beside, deep = 8, 16
+    beside, deep = 8, 8
     unset = (jnp.full((8, LANES), -jnp.inf, jnp.float32), jnp.zeros((8, LANES), jnp.float32))
     for start in range(0, total, beside * LANES):
         tiles = [pl.ds(start + j * LANES, LANES) for j in range(beside)]

time: 69.3 us -> 69.3 us (level)
  no operation moved by 1% of the time
where the time goes in v6:
time: 69.3 us; the launch traced here: 69.1 us
  Pallas kernels  39.4 us (57%)
  starting transfers between devices  15.5 us (22%)
  waiting for transfers between devices  11 us (16%)
  matrix products  2.34 us (3%)
  between operations  0.77 us (1%)
    pallas_call x4, Pallas kernels, call(): pl.pallas_call(kernel, out_shape=tuple((jax.ShapeDtypeStruct(shape, bf16...  32.2 us
    ppermute x15, starting transfers between devices, swap(): lax.ppermute(value, axis, [(i, i ^ offset) for i in range(lax.axis_size(a...  15.5 us
    ppermute x15, waiting for transfers between devices, swap(): lax.ppermute(value, axis, [(i, i ^ offset) for i in range(lax.axis_size(a...  11 us
    pallas_call x1, Pallas kernels, shards(): pl.pallas_call(rows_running, out_shape=jax.ShapeDtypeStruct((1, total_row...  4.02 us
    dot_general x1, matrix products, shards(): scores = jnp.dot(weights, src_all, preferred_element_type=f32)  2.34 us
    pallas_call x1, Pallas kernels, shards(): pl.pallas_call(front_kernel, out_shape=(pltpu.VMEM((packed_rows, rows //...  1.65 us
  transfers between devices with their start and end apart: 15, of which 11 were waited for; matrix products, arithmetic and copies ran while one was open for 0% of the time, Pallas kernels for 1%

profile of v6, /device:TPU:0, one launch (start us, length us, event | category | flops | bytes accessed | tf_op | source)
XLA Modules:
  0.0 69.1 jit_solution(5709356015570742850)
XLA Ops:
  0.6 1.6 %shard_map.76 = (f32[56,256]{1,0:T(8,128)S(1)}, f32[56,512]{1,0:T(8,128)S(1)}, f32[8,512]{1,0:T(8,128)S(1)}) custom-call(bf16[512,512]{1,0:T(8,128)(2,1)} %refs_0_.1, bf16[50,512]{1,0:T(8,128)(2,1)} %refs_1_.1, bf16[50,512]{1,0:T(8,128)(2,1)} %refs_2_.1, f32[1,512]{1,0:T(1,128)} %bitcast.6, f32[1,512]{1,0:T(1,128)} %bitcast.7), custom_call_target="tpu_custom_call" | custom-call | tf_op jit(solution)/shard_map/pallas_call | solution.py:475
  2.3 0.5 collective-permute-start
  2.8 0.8 %collective-permute-done = f32[8,512]{1,0:T(8,128)S(1)} collective-permute-done((f32[8,512]{1,0:T(8,128)S(1)}, f32[8,512]{1,0:T(8,128)S(1)}, u32[]{:S(2)}, u32[]{:S(2)}) %collective-permute-start) | collective-permute-done | bytes 16416 | tf_op jit(solution)/shard_map/ppermute | solution.py:448
  3.7 3.9 %collective-permute-start.3 = (f32[64,512]{1,0:T(8,128)S(1)}, f32[64,512]{1,0:T(8,128)S(1)}, u32[]{:S(2)}, u32[]{:S(2)}) collective-permute-start(f32[64,512]{1,0:T(8,128)S(1)} %constant_dynamic-update-slice_fusion), channel_id=1, source_target_pairs={{0,6},{1,7},{2,4},{3,5},{4,2},{5,3},{6,0},{7,1},{8,14},{9,15},{10,... | collective-permute-start | bytes 393224 | tf_op jit(solution)/shard_map/ppermute | solution.py:448
  7.5 0.5 collective-permute-start.2
  8.0 0.1 collective-permute-start.1
  8.2 4.0 %collective-permute-start.6 = (f32[56,256]{1,0:T(8,128)S(1)}, f32[56,256]{1,0:T(8,128)S(1)}, u32[]{:S(2)}, u32[]{:S(2)}) collective-permute-start(f32[56,256]{1,0:T(8,128)S(1)} %get-tuple-element.43), channel_id=1, source_target_pairs={{0,24},{8,16},{16,8},{24,0},{1,25},{9,17},{17,9},{25,1},{2,26},{10... | collective-permute-start | bytes 172040 | tf_op jit(solution)/shard_map/ppermute | solution.py:448
  12.2 1.2 %collective-permute-start.4 = (f32[56,256]{1,0:T(8,128)S(1)}, f32[56,256]{1,0:T(8,128)S(1)}, u32[]{:S(2)}, u32[]{:S(2)}) collective-permute-start(f32[56,256]{1,0:T(8,128)S(1)} %get-tuple-element.43), channel_id=1, source_target_pairs={{0,8},{8,0},{16,24},{24,16},{1,9},{9,1},{17,25},{25,17},{2,10},{10... | collective-permute-start | bytes 172040 | tf_op jit(solution)/shard_map/ppermute | solution.py:448
  13.4 0.8 %collective-permute-done.2.refs_2_ = f32[64,512]{1,0:T(8,128)S(1)} collective-permute-done((f32[64,512]{1,0:T(8,128)S(1)}, f32[64,512]{1,0:T(8,128)S(1)}, u32[]{:S(2)}, u32[]{:S(2)}) %collective-permute-start.2) | collective-permute-done | bytes 131104 | tf_op jit(solution)/shard_map/ppermute | solution.py:448
  14.2 0.3 collective-permute-done.1.refs_1_
  14.4 0.6 collective-permute-done.6
  15.0 2.2 %collective-permute-done.5 = f32[56,256]{1,0:T(8,128)S(1)} collective-permute-done((f32[56,256]{1,0:T(8,128)S(1)}, f32[56,256]{1,0:T(8,128)S(1)}, u32[]{:S(2)}, u32[]{:S(2)}) %collective-permute-start.5) | collective-permute-done | bytes 57376 | tf_op jit(solution)/shard_map/ppermute | solution.py:448
  17.3 0.1 collective-permute-start.7
  17.4 2.7 %collective-permute-start.10 = (f32[8,512]{1,0:T(8,128)S(1)}, f32[8,512]{1,0:T(8,128)S(1)}, u32[]{:S(2)}, u32[]{:S(2)}) collective-permute-start(f32[8,512]{1,0:T(8,128)S(1)} %add_add_fusion.refs_0_), channel_id=1, source_target_pairs={{0,24},{8,16},{16,8},{24,0},{1,25},{9,17},{17,9},{25,1},{2,26},{10... | collective-permute-start | bytes 49160 | tf_op jit(solution)/shard_map/ppermute | solution.py:448
  20.1 1.7 %collective-permute-start.8 = (f32[8,512]{1,0:T(8,128)S(1)}, f32[8,512]{1,0:T(8,128)S(1)}, u32[]{:S(2)}, u32[]{:S(2)}) collective-permute-start(f32[8,512]{1,0:T(8,128)S(1)} %add_add_fusion.refs_0_), channel_id=1, source_target_pairs={{0,8},{8,0},{16,24},{24,16},{1,9},{9,1},{17,25},{25,17},{2,10},{10... | collective-permute-start | bytes 49160 | tf_op jit(solution)/shard_map/ppermute | solution.py:448
  21.9 0.7 %shard_map.77 = (bf16[256,2048]{1,0:T(8,128)(2,1)S(1)}, bf16[2048,128]{1,0:T(8,128)(2,1)S(1)}, f32[1,2048]{1,0:T(1,128)S(1)}, f32[2048,128]{1,0:T(8,128)S(1)}, f32[1,2048]{1,0:T(1,128)S(1)}) custom-call(f32[224,256]{1,0:T(8,128)S(1)} %constant_dynamic-update-slice_fusion.2.near_ref, f32[224,256]{1,0:T(8,128)S(1)} %collective-permute-done.7.far_ref, ...), custom_call_target="tpu_custom_call" | custom-call | tf_op jit(solution)/shard_map/pallas_call | solution.py:504
  22.6 0.4 collective-permute-done.10.refs_3_
  23.0 1.7 %collective-permute-done.9.refs_2_ = f32[8,512]{1,0:T(8,128)S(1)} collective-permute-done((f32[8,512]{1,0:T(8,128)S(1)}, f32[8,512]{1,0:T(8,128)S(1)}, u32[]{:S(2)}, u32[]{:S(2)}) %collective-permute-start.9) | collective-permute-done | bytes 16416 | tf_op jit(solution)/shard_map/ppermute | solution.py:448
  24.8 0.8 %shard_map.78 = bf16[2048,256]{1,0:T(8,128)(2,1)S(1)} custom-call(bf16[2048,128]{1,0:T(8,128)(2,1)S(1)} %get-tuple-element.51.turned_ref, f32[8,512]{1,0:T(8,128)S(1)} %add_add_fusion.refs_0_, f32[8,512]{1,0:T(8,128)S(1)} %collective-permute-done.8.refs_1_, f32[8,512]{1,0:T(8,128)S(1)} %collective-permute-done.9.refs_2_, ...), custom_call_target="tpu_custom_call" | custom-call | tf_op jit(solution)/shard_map/pallas_call | solution.py:517
  25.5 2.3 %fusion.scores_ref = f32[2048,2048]{1,0:T(8,128)S(1)} fusion(bf16[2048,256]{1,0:T(8,128)(2,1)S(1)} %shard_map.78, bf16[256,2048]{1,0:T(8,128)(2,1)S(1)} %get-tuple-element.56), kind=kOutput, calls=%fused_computation.7 | convolution fusion | flops 2147483648 | bytes 18874368 | tf_op jit(solution)/shard_map/dot_general | solution.py:524
  27.9 4.0 %shard_map.79.sums_ref = f32[1,2048]{1,0:T(1,128)S(1)} custom-call(f32[2048,2048]{1,0:T(8,128)S(1)} %fusion.scores_ref), custom_call_target="tpu_custom_call" | custom-call | tf_op jit(solution)/shard_map/pallas_call | solution.py:525
  32.0 1.2 %collective-permute-done.11.more_ref = f32[1,2048]{1,0:T(1,128)S(1)} collective-permute-done((f32[1,2048]{1,0:T(1,128)S(1)}, f32[1,2048]{1,0:T(1,128)S(1)}, u32[]{:S(2)}, u32[]{:S(2)}) %collective-permute-start.11) | collective-permute-done | bytes 8224 | tf_op jit(solution)/shard_map/ppermute | solution.py:448
  33.1 10.0 %shard_map.80 = (f32[1,2048]{1,0:T(1,128)S(1)}, bf16[2048,2048]{1,0:T(8,128)(2,1)S(1)}, f32[8,2048]{1,0:T(8,128)S(1)}, f32[1,2048]{1,0:T(1,128)S(1)}) custom-call(f32[2048,2048]{1,0:T(8,128)S(1)} %fusion.scores_ref, f32[1,2048]{1,0:T(1,128)S(1)} %shard_map.79.sums_ref, f32[1,2048]{1,0:T(1,128)S(1)} %collective-permute-done.11.more_ref, ...), custom_call_target="tpu_custom_call" | custom-call | tf_op jit(solution)/shard_map/pallas_call | solution.py:543
  43.1 0.2 collective-permute-start.12
  43.4 1.0 %collective-permute-done.12.more_ref = f32[1,2048]{1,0:T(1,128)S(1)} collective-permute-done((f32[1,2048]{1,0:T(1,128)S(1)}, f32[1,2048]{1,0:T(1,128)S(1)}, u32[]{:S(2)}, u32[]{:S(2)}) %collective-permute-start.12) | collective-permute-done | bytes 8224 | tf_op jit(solution)/shard_map/ppermute | solution.py:448
  44.4 11.8 %shard_map.81 = (f32[1,2048]{1,0:T(1,128)S(1)}, bf16[2048,2048]{1,0:T(8,128)(2,1)S(1)}, f32[1,2048]{1,0:T(1,128)S(1)}, f32[1,2048]{1,0:T(1,128)S(1)}) custom-call(f32[2048,2048]{1,0:T(8,128)S(1)} %fusion.scores_ref, f32[1,2048]{1,0:T(1,128)S(1)} %get-tuple-element.60.sums_ref, f32[1,2048]{1,0:T(1,128)S(1)} %collective-permute-done.12.more_ref, ...), custom_call_target="tpu_custom_call" | custom-call | tf_op jit(solution)/shard_map/pallas_call | solution.py:543
  56.2 0.2 collective-permute-start.13
  56.4 1.0 %collective-permute-done.13.more_ref = f32[1,2048]{1,0:T(1,128)S(1)} collective-permute-done((f32[1,2048]{1,0:T(1,128)S(1)}, f32[1,2048]{1,0:T(1,128)S(1)}, u32[]{:S(2)}, u32[]{:S(2)}) %collective-permute-start.13) | collective-permute-done | bytes 8224 | tf_op jit(solution)/shard_map/ppermute | solution.py:448
  57.5 7.7 %shard_map.82.sums_ref = f32[1,2048]{1,0:T(1,128)S(1)} custom-call(f32[2048,2048]{1,0:T(8,128)S(1)} %fusion.scores_ref, f32[1,2048]{1,0:T(1,128)S(1)} %get-tuple-element.64.sums_ref, f32[1,2048]{1,0:T(1,128)S(1)} %collective-permute-done.13.more_ref, f32[1,2048]{1,0:T(1,128)S(1)} %get-tuple-element.57.log_src_ref, ...), custom_call_target="tpu_custom_call" | custom-call | tf_op jit(solution)/shard_map/pallas_call | solution.py:543
  65.2 0.2 collective-permute-start.14
  65.4 1.0 %collective-permute-done.14.more_ref = f32[1,2048]{1,0:T(1,128)S(1)} collective-permute-done((f32[1,2048]{1,0:T(1,128)S(1)}, f32[1,2048]{1,0:T(1,128)S(1)}, u32[]{:S(2)}, u32[]{:S(2)}) %collective-permute-start.14) | collective-permute-done | bytes 8224 | tf_op jit(solution)/shard_map/ppermute | solution.py:448
  66.4 2.7 %shard_map.83 = (f32[512,512]{1,0:T(8,128)}, f32[1,512]{1,0:T(1,128)}, f32[1,512]{1,0:T(1,128)}) custom-call(f32[2048,2048]{1,0:T(8,128)S(1)} %fusion.scores_ref, f32[1,2048]{1,0:T(1,128)S(1)} %shard_map.82.sums_ref, f32[1,2048]{1,0:T(1,128)S(1)} %collective-permute-done.14.more_ref, f32[1,2048]{1,0:T(1,128)S(1)} %get-tuple-element.57.log_src_ref, ...), custom_call_target="tpu_custom_call" | custom-call | tf_op jit(solution)/shard_map/pallas_call | solution.py:543
  (18 shorter events, 0.1 us)
Async XLA Ops:
  2.3 1.4 %collective-permute-start = (f32[8,512]{1,0:T(8,128)S(1)}, f32[8,512]{1,0:T(8,128)S(1)}, u32[]{:S(2)}, u32[]{:S(2)}) collective-permute-start(f32[8,512]{1,0:T(8,128)S(1)} %get-tuple-element.39), channel_id=1, source_target_pairs={{0,1},{1,0},{2,3},{3,2},{4,5},{5,4},{6,7},{7,6},{8,9},{9,8},{10,11... | collective-permute-start | bytes 49160 | tf_op jit(solution)/shard_map/ppermute | solution.py:448
  3.7 8.5 %collective-permute-start.3 = (f32[64,512]{1,0:T(8,128)S(1)}, f32[64,512]{1,0:T(8,128)S(1)}, u32[]{:S(2)}, u32[]{:S(2)}) collective-permute-start(f32[64,512]{1,0:T(8,128)S(1)} %constant_dynamic-update-slice_fusion), channel_id=1, source_target_pairs={{0,6},{1,7},{2,4},{3,5},{4,2},{5,3},{6,0},{7,1},{8,14},{9,15},{10,... | collective-permute-start | bytes 393224 | tf_op jit(solution)/shard_map/ppermute | solution.py:448
  7.5 6.6 %collective-permute-start.2 = (f32[64,512]{1,0:T(8,128)S(1)}, f32[64,512]{1,0:T(8,128)S(1)}, u32[]{:S(2)}, u32[]{:S(2)}) collective-permute-start(f32[64,512]{1,0:T(8,128)S(1)} %constant_dynamic-update-slice_fusion), channel_id=1, source_target_pairs={{0,4},{1,5},{2,6},{3,7},{4,0},{5,1},{6,2},{7,3},{8,12},{9,13},{10,... | collective-permute-start | bytes 393224 | tf_op jit(solution)/shard_map/ppermute | solution.py:448
  8.0 6.4 %collective-permute-start.1 = (f32[64,512]{1,0:T(8,128)S(1)}, f32[64,512]{1,0:T(8,128)S(1)}, u32[]{:S(2)}, u32[]{:S(2)}) collective-permute-start(f32[64,512]{1,0:T(8,128)S(1)} %constant_dynamic-update-slice_fusion), channel_id=1, source_target_pairs={{0,2},{1,3},{2,0},{3,1},{4,6},{5,7},{6,4},{7,5},{8,10},{9,11},{10,... | collective-permute-start | bytes 393224 | tf_op jit(solution)/shard_map/ppermute | solution.py:448
  8.2 6.8 %collective-permute-start.6 = (f32[56,256]{1,0:T(8,128)S(1)}, f32[56,256]{1,0:T(8,128)S(1)}, u32[]{:S(2)}, u32[]{:S(2)}) collective-permute-start(f32[56,256]{1,0:T(8,128)S(1)} %get-tuple-element.43), channel_id=1, source_target_pairs={{0,24},{8,16},{16,8},{24,0},{1,25},{9,17},{17,9},{25,1},{2,26},{10... | collective-permute-start | bytes 172040 | tf_op jit(solution)/shard_map/ppermute | solution.py:448
  12.2 5.1 %collective-permute-start.5 = (f32[56,256]{1,0:T(8,128)S(1)}, f32[56,256]{1,0:T(8,128)S(1)}, u32[]{:S(2)}, u32[]{:S(2)}) collective-permute-start(f32[56,256]{1,0:T(8,128)S(1)} %get-tuple-element.43), channel_id=1, source_target_pairs={{0,16},{8,24},{16,0},{24,8},{1,17},{9,25},{17,1},{25,9},{2,18},{10... | collective-permute-start | bytes 172040 | tf_op jit(solution)/shard_map/ppermute | solution.py:448
  12.2 5.1 %collective-permute-start.4 = (f32[56,256]{1,0:T(8,128)S(1)}, f32[56,256]{1,0:T(8,128)S(1)}, u32[]{:S(2)}, u32[]{:S(2)}) collective-permute-start(f32[56,256]{1,0:T(8,128)S(1)} %get-tuple-element.43), channel_id=1, source_target_pairs={{0,8},{8,0},{16,24},{24,16},{1,9},{9,1},{17,25},{25,17},{2,10},{10... | collective-permute-start | bytes 172040 | tf_op jit(solution)/shard_map/ppermute | solution.py:448
  17.3 4.6 %collective-permute-start.7 = (f32[224,256]{1,0:T(8,128)S(1)}, f32[224,256]{1,0:T(8,128)S(1)}, u32[]{:S(2)}, u32[]{:S(2)}) collective-permute-start(f32[224,256]{1,0:T(8,128)S(1)} %constant_dynamic-update-slice_fusion.2.near_ref), channel_id=1, source_target_pairs={{0,1},{1,0},{2,3},{3,2},{4,5},{5,4},{6,7},{7,6},{8,9},{9,8},{10,11... | collective-permute-start | bytes 688136 | tf_op jit(solution)/shard_map/ppermute | solution.py:448
  17.4 5.6 %collective-permute-start.10 = (f32[8,512]{1,0:T(8,128)S(1)}, f32[8,512]{1,0:T(8,128)S(1)}, u32[]{:S(2)}, u32[]{:S(2)}) collective-permute-start(f32[8,512]{1,0:T(8,128)S(1)} %add_add_fusion.refs_0_), channel_id=1, source_target_pairs={{0,24},{8,16},{16,8},{24,0},{1,25},{9,17},{17,9},{25,1},{2,26},{10... | collective-permute-start | bytes 49160 | tf_op jit(solution)/shard_map/ppermute | solution.py:448
  20.1 4.6 %collective-permute-start.9 = (f32[8,512]{1,0:T(8,128)S(1)}, f32[8,512]{1,0:T(8,128)S(1)}, u32[]{:S(2)}, u32[]{:S(2)}) collective-permute-start(f32[8,512]{1,0:T(8,128)S(1)} %add_add_fusion.refs_0_), channel_id=1, source_target_pairs={{0,16},{8,24},{16,0},{24,8},{1,17},{9,25},{17,1},{25,9},{2,18},{10... | collective-permute-start | bytes 49160 | tf_op jit(solution)/shard_map/ppermute | solution.py:448
  20.1 4.6 %collective-permute-start.8 = (f32[8,512]{1,0:T(8,128)S(1)}, f32[8,512]{1,0:T(8,128)S(1)}, u32[]{:S(2)}, u32[]{:S(2)}) collective-permute-start(f32[8,512]{1,0:T(8,128)S(1)} %add_add_fusion.refs_0_), channel_id=1, source_target_pairs={{0,8},{8,0},{16,24},{24,16},{1,9},{9,1},{17,25},{25,17},{2,10},{10... | collective-permute-start | bytes 49160 | tf_op jit(solution)/shard_map/ppermute | solution.py:448
  31.9 1.2 %collective-permute-start.11 = (f32[1,2048]{1,0:T(1,128)S(1)}, f32[1,2048]{1,0:T(1,128)S(1)}, u32[]{:S(2)}, u32[]{:S(2)}) collective-permute-start(f32[1,2048]{1,0:T(1,128)S(1)} %shard_map.79.sums_ref), channel_id=1, source_target_pairs={{0,1},{1,0},{2,3},{3,2},{4,5},{5,4},{6,7},{7,6},{8,9},{9,8},{10,11... | collective-permute-start | bytes 24584 | tf_op jit(solution)/shard_map/ppermute | solution.py:448
  43.1 1.2 %collective-permute-start.12 = (f32[1,2048]{1,0:T(1,128)S(1)}, f32[1,2048]{1,0:T(1,128)S(1)}, u32[]{:S(2)}, u32[]{:S(2)}) collective-permute-start(f32[1,2048]{1,0:T(1,128)S(1)} %get-tuple-element.60.sums_ref), channel_id=1, source_target_pairs={{0,1},{1,0},{2,3},{3,2},{4,5},{5,4},{6,7},{7,6},{8,9},{9,8},{10,11... | collective-permute-start | bytes 24584 | tf_op jit(solution)/shard_map/ppermute | solution.py:448
  56.2 1.2 %collective-permute-start.13 = (f32[1,2048]{1,0:T(1,128)S(1)}, f32[1,2048]{1,0:T(1,128)S(1)}, u32[]{:S(2)}, u32[]{:S(2)}) collective-permute-start(f32[1,2048]{1,0:T(1,128)S(1)} %get-tuple-element.64.sums_ref), channel_id=1, source_target_pairs={{0,1},{1,0},{2,3},{3,2},{4,5},{5,4},{6,7},{7,6},{8,9},{9,8},{10,11... | collective-permute-start | bytes 24584 | tf_op jit(solution)/shard_map/ppermute | solution.py:448
  65.2 1.2 %collective-permute-start.14 = (f32[1,2048]{1,0:T(1,128)S(1)}, f32[1,2048]{1,0:T(1,128)S(1)}, u32[]{:S(2)}, u32[]{:S(2)}) collective-permute-start(f32[1,2048]{1,0:T(1,128)S(1)} %shard_map.82.sums_ref), channel_id=1, source_target_pairs={{0,1},{1,0},{2,3},{3,2},{4,5},{5,4},{6,7},{7,6},{8,9},{9,8},{10,11... | collective-permute-start | bytes 24584 | tf_op jit(solution)/shard_map/ppermute | solution.py:448
